TPU v7x, 32 devices: a whole 2x2x4 slice. The times are simulated.
32 devices in a mesh: pipe: 2 (over x), expert: 8 (over z, y), tensor: 2 (over core).
Axes of the slice: x: 2, y: 2, z: 4, core: 2. Of those that a mesh axis runs over, the one named last changes fastest.
Arguments:
- tokens: bfloat16 [2048, 6144], P(('pipe', 'expert'), 'tensor'), parts along dimension 0, may hold values from -6 to 6
- grad_out: bfloat16 [2048, 6144], P(('pipe', 'expert'), 'tensor'), parts along dimension 0, may hold values from -6 to 6
- expert_ids: int32 [2048, 2], P(('pipe', 'expert')), parts along dimension 0, may hold values from 0 to 7, all different within a row; in each aligned block of 128 rows (0 to 127, 128 to 255, ...) at most 36 rows name the same one
- gate_probs: float32 [2048, 2], P(('pipe', 'expert')), parts along dimension 0, may hold values from 0.05 to 1
- w_gate: bfloat16 [6144, 2048], P('tensor', 'expert'), may hold values from -0.078125 to 0.078125
- w_up: bfloat16 [6144, 2048], P('tensor', 'expert'), may hold values from -0.078125 to 0.078125
- w_down: bfloat16 [2048, 6144], P('expert', 'tensor'), may hold values from -0.078125 to 0.078125
Outputs:
- grad_in: bfloat16 [2048, 6144], P(('pipe', 'expert'), 'tensor'), parts along dimension 0
- grad_gate: bfloat16 [12288, 2048], P(('pipe', 'tensor'), 'expert'), parts along dimension 0
- grad_up: bfloat16 [12288, 2048], P(('pipe', 'tensor'), 'expert'), parts along dimension 0
- grad_down: bfloat16 [4096, 6144], P(('pipe', 'expert'), 'tensor'), parts along dimension 0
There are 2 independent parts, one for each index of `pipe`. A program takes and returns all parts, laid end to end along the dimension named above; an argument that names none is the same for every part. Nothing has to cross between parts.
Inputs may be any that keep to these rules, and one draw needn't show every extreme that they name: `expert_ids`: each token names two different experts. In the rows of one device no expert is named by more than 36 tokens, a bound that some block reaches of them.
All inputs are finite; a program needn't handle non-finite values.
Results may differ from a plain program's by a relative error of at most 0.02.
Values may be sent and summed in bfloat16 or wider, within the bound.
No kernel may reach another device: no remote copies, remote signals or barrier semaphores. Data moves between devices by JAX's collectives and lax.ppermute only.
A program may use at most 128 MiB of HBM per device.

v0:
```python
import jax
import jax.numpy as jnp
from jax import lax
from jax.sharding import PartitionSpec as P

CAP = 36


window_expert = 0


def swiglu_grads(sums, width):
    z_gate = sums[:, :width]
    z_up = sums[:, width : 2 * width]
    d_hidden = sums[:, 2 * width :]
    sig = jax.nn.sigmoid(z_gate)
    act = z_gate * sig
    hidden = (act * z_up).astype(jnp.bfloat16)
    d_gate = (d_hidden * z_up * sig * (1.0 + z_gate * (1.0 - sig))).astype(jnp.bfloat16)
    d_up = (d_hidden * act).astype(jnp.bfloat16)
    return (hidden, jnp.concatenate([d_gate, d_up], axis=1))


def per_device(tokens, grad_out, expert_ids, gate_probs, w_gate, w_up, w_down):
    width = w_gate.shape[1]
    chosen = expert_ids == window_expert
    weight = jnp.sum(jnp.where(chosen, gate_probs, jnp.zeros_like(gate_probs)), axis=1)
    scaled = (weight[:, None] * grad_out.astype(jnp.float32)).astype(jnp.bfloat16)
    routed = jnp.any(chosen, axis=1)
    slot_of = jnp.cumsum(routed.astype(jnp.int32)) - 1
    slot_ids = jnp.arange(CAP, dtype=jnp.int32)
    placing = ((slot_of[None, :] == slot_ids[:, None]) & routed[None, :]).astype(jnp.bfloat16)
    send_x = jnp.dot(placing, tokens, preferred_element_type=jnp.float32).astype(jnp.bfloat16)
    send_dy = jnp.dot(placing, scaled, preferred_element_type=jnp.float32).astype(jnp.bfloat16)
    rows_x, rows_dy = (
        lax.all_gather(send_x, "expert", axis=0, tiled=True),
        lax.all_gather(send_dy, "expert", axis=0, tiled=True),
    )
    w_in = jnp.concatenate([w_gate, w_up], axis=1)
    front = jnp.dot(rows_x, w_in, preferred_element_type=jnp.float32)
    back = lax.dot_general(
        rows_dy, w_down, (((1,), (1,)), ((), ())), preferred_element_type=jnp.float32
    )
    partial_value = jnp.concatenate([front, back], axis=1)
    share = lax.psum_scatter(
        partial_value.astype(jnp.bfloat16), "tensor", scatter_dimension=0, tiled=True
    ).astype(jnp.float32)
    hidden_part, grads_part = swiglu_grads(share, width)
    hidden, d_pre = (
        lax.all_gather(hidden_part, "tensor", axis=0, tiled=True),
        lax.all_gather(grads_part, "tensor", axis=0, tiled=True),
    )
    summed = lax.psum_scatter(
        lax.dot_general(
            d_pre, w_in, (((1,), (1,)), ((), ())), preferred_element_type=jnp.float32
        ).astype(jnp.bfloat16),
        "expert",
        scatter_dimension=0,
        tiled=True,
    )
    grad_in = lax.dot_general(
        placing, summed, (((0,), (0,)), ((), ())), preferred_element_type=jnp.float32
    ).astype(jnp.bfloat16)
    grad_w_in = lax.dot_general(
        rows_x, d_pre, (((0,), (0,)), ((), ())), preferred_element_type=jnp.float32
    ).astype(jnp.bfloat16)
    grad_down = lax.dot_general(
        hidden, rows_dy, (((0,), (0,)), ((), ())), preferred_element_type=jnp.float32
    ).astype(jnp.bfloat16)
    return (grad_in, grad_w_in[:, :width], grad_w_in[:, width:], grad_down)


def solution(mesh):
    in_specs = (
        P(("pipe", "expert"), "tensor"),
        P(("pipe", "expert"), "tensor"),
        P(("pipe", "expert"), None),
        P(("pipe", "expert"), None),
        P("tensor", "expert"),
        P("tensor", "expert"),
        P("expert", "tensor"),
    )
    out_specs = (
        P(("pipe", "expert"), "tensor"),
        P(("pipe", "tensor"), "expert"),
        P(("pipe", "tensor"), "expert"),
        P(("pipe", "expert"), "tensor"),
    )
    return jax.shard_map(
        per_device, mesh=mesh, in_specs=in_specs, out_specs=out_specs, check_vma=False
    )
```

profile of v0, /device:TPU:0, one launch (start us, length us, event | category | flops | bytes accessed | tf_op | source)
XLA Modules:
  0.0 202.8 jit_solution(2408956200780389792)
XLA Ops:
  7.2 0.8 fusion.17
  8.5 2.1 %fusion.1 = bf16[1,36,3072]{2,1,0:T(8,128)(2,1)} fusion(bf16[128,3072]{1,0:T(8,128)(2,1)} %param.7, s32[128]{0:T(128)S(1)} %add_reduce_fusion, pred[128]{0:T(512)(128)(4,1)S(1)} %fusion.17), kind=kOutput, calls=%fused_computation.6 | convolution fusion | flops 28431360 | bytes 1008256 | tf_op jit(solution)/shard_map/dot_general | solution.py:33
  11.4 2.2 %fusion.2 = bf16[1,36,3072]{2,1,0:T(8,128)(2,1)} fusion(bf16[128,3072]{1,0:T(8,128)(2,1)} %param.8, f32[128]{0:T(128)S(1)} %select_reduce_fusion, s32[128]{0:T(128)S(1)} %add_reduce_fusion, pred[128]{0:T(512)(128)(4,1)S(1)} %fusion.17), kind=kOutput, calls=%fused_computation.7 | convolution fusion | flops 29611008 | bytes 1008768 | tf_op jit(solution)/shard_map/dot_general | solution.py:34
  13.6 1.3 constant_dynamic-update-slice_fusion.1
  15.6 1.3 constant_dynamic-update-slice_fusion
  16.9 44.2 %all-gather.5.cloned.1.call-done = bf16[8,36,3072]{2,1,0:T(8,128)(2,1)} async-done(((bf16[1,36,3072]{2,1,0:T(8,128)(2,1)}), bf16[8,36,3072]{2,1,0:T(8,128)(2,1)}) %all-gather.5.cloned.1.call-update) | async-done | bytes 1769488 | tf_op jit(solution)/shard_map/all_gather | solution.py:36
  61.0 1.7 reshape.44
  62.7 4.3 %convolution_convert_fusion.6 = bf16[288,512]{1,0:T(8,128)(2,1)} fusion(bf16[288,3072]{1,0:T(8,128)(2,1)S(1)} %reshape.44, bf16[3072,512]{1,0:T(8,128)(2,1)} %constant_dynamic-update-slice_fusion), kind=kOutput, calls=%fused_computation.9 | convolution fusion | flops 906117120 | bytes 5210112 | tf_op jit(solution)/shard_map/dot_general | solution.py:40
  67.1 43.4 %all-gather.7.cloned.1.call-done = bf16[8,36,3072]{2,1,0:T(8,128)(2,1)} async-done(((bf16[1,36,3072]{2,1,0:T(8,128)(2,1)}), bf16[8,36,3072]{2,1,0:T(8,128)(2,1)}) %all-gather.7.cloned.1.call-update) | async-done | bytes 1769488 | tf_op jit(solution)/shard_map/all_gather | solution.py:37
  110.4 1.7 reshape.46
  113.1 0.8 pad_maximum_fusion
  115.2 5.8 %reduce-scatter.4.cloned.1.call-done = bf16[144,768]{1,0:T(8,128)(2,1)} async-done(((bf16[288,768]{1,0:T(8,128)(2,1)}), bf16[144,768]{1,0:T(8,128)(2,1)}) %reduce-scatter.4.cloned.1.call-update) | async-done | bytes 221200 | tf_op jit(solution)/shard_map/reduce_scatter | solution.py:45
  121.0 1.0 convert_element_type.59
  122.0 2.0 all_gather.14
  124.1 4.4 %convolution_convert_fusion.1 = bf16[288,3072]{1,0:T(8,128)(2,1)} fusion(bf16[288,512]{1,0:T(8,128)(2,1)S(1)} %all_gather.14, bf16[3072,512]{1,0:T(8,128)(2,1)} %constant_dynamic-update-slice_fusion), kind=kOutput, calls=%fused_computation.1 | convolution fusion | flops 906854400 | bytes 5210112 | tf_op jit(solution)/shard_map/dot_general | solution.py:54
  128.5 3.5 %convolution_convert_fusion = bf16[3072,512]{1,0:T(8,128)(2,1)} fusion(bf16[288,3072]{1,0:T(8,128)(2,1)S(1)} %copy-done.2, bf16[288,512]{1,0:T(8,128)(2,1)S(1)} %all_gather.14), kind=kOutput, calls=%fused_computation | convolution fusion | flops 907542528 | bytes 5210112 | tf_op jit(solution)/shard_map/dot_general | solution.py:64
  132.0 49.4 %fusion = bf16[40,3072]{1,0:T(8,128)(2,1)} fusion(bf16[288,3072]{1,0:T(8,128)(2,1)} %convolution_convert_fusion.1), kind=kCustom, calls=%all-reduce-scatter | all-reduce-scatter fusion | flops 983041 | bytes 2015744
  181.3 1.0 slice.25
  182.3 2.0 collective-permute-start
  184.3 3.7 %fusion.18 = (bf16[3072,256]{1,0:T(8,128)(2,1)}, bf16[3072,256]{1,0:T(8,128)(2,1)}) fusion(bf16[3072,512]{1,0:T(8,128)(2,1)} %convolution_convert_fusion), kind=kLoop, calls=%fused_computation.36 | loop fusion | bytes 6291456 | tf_op jit(solution)/shard_map/slice | solution.py:70
  188.0 1.9 all_gather.15
  189.9 2.1 %convolution_convert_fusion.2 = bf16[256,3072]{1,0:T(8,128)(2,1)} fusion(bf16[288,256]{1,0:T(8,128)(2,1)S(1)} %all_gather.15, bf16[288,3072]{1,0:T(8,128)(2,1)S(1)} %reshape.46), kind=kOutput, calls=%fused_computation.2 | convolution fusion | flops 453771264 | bytes 3489792 | tf_op jit(solution)/shard_map/dot_general | solution.py:67
  192.1 2.9 %concatenate.13 = bf16[68,3072]{1,0:T(8,128)(2,1)S(1)} concatenate(bf16[28,3072]{1,0:T(8,128)(2,1)} %collective-permute-done, bf16[40,3072]{1,0:T(8,128)(2,1)} %fusion), dimensions={0} | concatenate | bytes 835584
  195.0 1.3 convolution_convert_fusion.3
  (30 shorter events, 3.6 us)
Async XLA Ops:
  7.2 105.0 %copy-start = (bf16[256,3072]{1,0:T(8,128)(2,1)S(1)}, bf16[256,3072]{1,0:T(8,128)(2,1)}, u32[]{:S(2)}) copy-start(bf16[256,3072]{1,0:T(8,128)(2,1)} %param.13) | copy-start | bytes 4718596
  7.2 6.4 %copy-start.3 = (bf16[3072,256]{1,0:T(8,128)(2,1)S(1)}, bf16[3072,256]{1,0:T(8,128)(2,1)}, u32[]{:S(2)}) copy-start(bf16[3072,256]{1,0:T(8,128)(2,1)} %param.11) | copy-start | bytes 4718596
  7.2 53.8 %all-gather.5.cloned.1.call-start = ((), (), s32[]{:S(2)}) async-start(), calls=%async_computation.2 | async-start | bytes 2211840 | tf_op jit(solution)/shard_map/all_gather | solution.py:36
  10.6 99.8 %all-gather.7.cloned.1.call-start = ((), (), s32[]{:S(2)}) async-start(), calls=%async_computation.3 | async-start | bytes 2211840 | tf_op jit(solution)/shard_map/all_gather | solution.py:37
  13.5 107.4 %reduce-scatter.4.cloned.1.call-start = ((), (), s32[]{:S(2)}) async-start(), calls=%async_computation.1 | async-start | bytes 663552 | tf_op jit(solution)/shard_map/reduce_scatter | solution.py:45
  13.6 2.0 copy-start.4
  62.7 4.3 %copy-start.1 = (bf16[288,3072]{1,0:T(8,128)(2,1)}, bf16[288,3072]{1,0:T(8,128)(2,1)S(1)}, u32[]{:S(2)}) copy-start(bf16[288,3072]{1,0:T(8,128)(2,1)S(1)} %reshape.44) | copy-start | bytes 5308420
  112.1 1.0 copy-start.5
  112.1 1.8 copy-start.6
  124.1 4.4 %copy-start.2 = (bf16[288,3072]{1,0:T(8,128)(2,1)S(1)}, bf16[288,3072]{1,0:T(8,128)(2,1)}, u32[]{:S(2)}) copy-start(bf16[288,3072]{1,0:T(8,128)(2,1)} %copy-done.1) | copy-start | bytes 5308420
  182.3 9.8 %collective-permute-start = (bf16[28,3072]{1,0:T(8,128)(2,1)S(1)}, bf16[28,3072]{1,0:T(8,128)(2,1)}, u32[]{:S(2)}, u32[]{:S(2)}) collective-permute-start(bf16[28,3072]{1,0:T(8,128)(2,1)S(1)} %slice.25), channel_id=1, source_target_pairs={{0,2},{2,4},{4,6},{6,8},{8,10},{10,12},{12,14},{1,3},{3,5},{5,7},{... | collective-permute-start | bytes 516104
Sparse Core Ops, SparseCore 0:
  10.8 50.2 all-gather.4
  63.8 46.5 all-gather.6
  114.0 6.8 reduce-scatter.3
where the time goes:
time: 203 us
  waiting for transfers between devices  93.4 us (46%)
  blocking collectives  53.3 us (26%)
  matrix products  20.6 us (10%)
  local copies, waits for them, and re-layouts  15.2 us (7%)
  between operations  14.5 us (7%)
  other arithmetic  3.7 us (2%)
  starting transfers between devices  2.1 us (1%)
    unnamed x1, blocking collectives  49.4 us
    all_gather x1, waiting for transfers between devices, per_device(): lax.all_gather(send_x, 'expert', axis=0, tiled=True)  44.2 us
    all_gather x1, waiting for transfers between devices, per_device(): lax.all_gather(send_dy, 'expert', axis=0, tiled=True)  43.4 us
    unnamed x20, local copies, waits for them, and re-layouts  10.1 us
    reduce_scatter x1, waiting for transfers between devices, per_device(): lax.psum_scatter(partial_value.astype(jnp.bfloat16), 'tensor', scatter_di...  5.81 us
    dot_general x1, matrix products, per_device(): lax.dot_general(d_pre, w_in, (((1,), (1,)), ((), ())), preferred_element_...  4.42 us
    dot_general x1, matrix products, per_device(): front = jnp.dot(rows_x, w_in, preferred_element_type=jnp.float32)  4.32 us
  transfers between devices with their start and end apart: 4, of which 3 were waited for; matrix products, arithmetic and copies ran while one was open for 9% of the time, Pallas kernels for 0%

commit v1 on v0

--- a/solution.py
+++ b/solution.py
@@ -21,8 +21,7 @@
     return (hidden, jnp.concatenate([d_gate, d_up], axis=1))
 
 
-def per_device(tokens, grad_out, expert_ids, gate_probs, w_gate, w_up, w_down):
-    width = w_gate.shape[1]
+def place(tokens, grad_out, expert_ids, gate_probs):
     chosen = expert_ids == window_expert
     weight = jnp.sum(jnp.where(chosen, gate_probs, jnp.zeros_like(gate_probs)), axis=1)
     scaled = (weight[:, None] * grad_out.astype(jnp.float32)).astype(jnp.bfloat16)
@@ -32,6 +31,28 @@
     placing = ((slot_of[None, :] == slot_ids[:, None]) & routed[None, :]).astype(jnp.bfloat16)
     send_x = jnp.dot(placing, tokens, preferred_element_type=jnp.float32).astype(jnp.bfloat16)
     send_dy = jnp.dot(placing, scaled, preferred_element_type=jnp.float32).astype(jnp.bfloat16)
+    return placing, send_x, send_dy
+
+
+def unplace(placing, summed):
+    return lax.dot_general(
+        placing, summed, (((0,), (0,)), ((), ())), preferred_element_type=jnp.float32
+    ).astype(jnp.bfloat16)
+
+
+def weight_grads(rows_x, rows_dy, hidden, d_pre, width):
+    grad_w_in = lax.dot_general(
+        rows_x, d_pre, (((0,), (0,)), ((), ())), preferred_element_type=jnp.float32
+    ).astype(jnp.bfloat16)
+    grad_down = lax.dot_general(
+        hidden, rows_dy, (((0,), (0,)), ((), ())), preferred_element_type=jnp.float32
+    ).astype(jnp.bfloat16)
+    return (grad_w_in[:, :width], grad_w_in[:, width:], grad_down)
+
+
+def any_size(tokens, grad_out, expert_ids, gate_probs, w_gate, w_up, w_down):
+    width = w_gate.shape[1]
+    placing, send_x, send_dy = place(tokens, grad_out, expert_ids, gate_probs)
     rows_x, rows_dy = (
         lax.all_gather(send_x, "expert", axis=0, tiled=True),
         lax.all_gather(send_dy, "expert", axis=0, tiled=True),
@@ -58,16 +79,65 @@
         scatter_dimension=0,
         tiled=True,
     )
-    grad_in = lax.dot_general(
-        placing, summed, (((0,), (0,)), ((), ())), preferred_element_type=jnp.float32
-    ).astype(jnp.bfloat16)
-    grad_w_in = lax.dot_general(
-        rows_x, d_pre, (((0,), (0,)), ((), ())), preferred_element_type=jnp.float32
-    ).astype(jnp.bfloat16)
-    grad_down = lax.dot_general(
-        hidden, rows_dy, (((0,), (0,)), ((), ())), preferred_element_type=jnp.float32
-    ).astype(jnp.bfloat16)
-    return (grad_in, grad_w_in[:, :width], grad_w_in[:, width:], grad_down)
+    grad_in = unplace(placing, summed)
+    return (grad_in,) + weight_grads(rows_x, rows_dy, hidden, d_pre, width)
+
+
+def four_by_two(tokens, grad_out, expert_ids, gate_probs, w_gate, w_up, w_down):
+    width = w_gate.shape[1]
+    bf16, f32 = jnp.bfloat16, jnp.float32
+    line = lax.axis_index("expert") // 2
+    inner = (line == 1) | (line == 2)
+
+    def send(value, pairs):
+        return lax.ppermute(value, "expert", pairs)
+
+    def across(value):
+        return send(value, [(i, i ^ 1) for i in range(8)])
+
+    def along(value, distance):
+        return send(value, [(i, i ^ (2 * distance)) for i in range(8)])
+
+    placing, send_x, send_dy = place(tokens, grad_out, expert_ids, gate_probs)
+    own = jnp.concatenate([send_x, send_dy], axis=0)
+
+    own_y = across(own)
+    two = along(own, 2)
+    one = along(own, 1)
+    middle = send(own, [(2, 4), (3, 5), (4, 2), (5, 3)])
+    ends = send(two, [(4, 6), (5, 7), (2, 0), (3, 1)])
+    one_y = across(one)
+    two_y = across(two)
+    three = jnp.where(inner, middle, ends)
+    three_y = across(three)
+
+    w_in = jnp.concatenate([w_gate, w_up], axis=1)
+
+    def group(mine, other):
+        rows_x = jnp.concatenate([mine[:CAP], other[:CAP]], axis=0)
+        rows_dy = jnp.concatenate([mine[CAP:], other[CAP:]], axis=0)
+        front = jnp.dot(rows_x, w_in, preferred_element_type=f32)
+        back = lax.dot_general(
+            rows_dy, w_down, (((1,), (1,)), ((), ())), preferred_element_type=f32
+        )
+        part = jnp.concatenate([front, back], axis=1)
+        sums = part + lax.ppermute(part.astype(bf16), "tensor", [(0, 1), (1, 0)]).astype(f32)
+        hidden, d_pre = swiglu_grads(sums, width)
+        term = lax.dot_general(
+            d_pre, w_in, (((1,), (1,)), ((), ())), preferred_element_type=f32
+        )
+        arrived = across(term[CAP:].astype(bf16))
+        return rows_x, rows_dy, hidden, d_pre, term[:CAP] + arrived.astype(f32)
+
+    groups = [group(own, own_y), group(one, one_y), group(two, two_y), group(three, three_y)]
+    total = groups[0][4]
+    for distance in (1, 2, 3):
+        total = total + along(groups[distance][4].astype(bf16), distance).astype(f32)
+    grad_in = unplace(placing, total.astype(bf16))
+    rows_x, rows_dy, hidden, d_pre = (
+        jnp.concatenate([g[i] for g in groups], axis=0) for i in range(4)
+    )
+    return (grad_in,) + weight_grads(rows_x, rows_dy, hidden, d_pre, width)
 
 
 def solution(mesh):
@@ -86,6 +156,5 @@
         P(("pipe", "tensor"), "expert"),
         P(("pipe", "expert"), "tensor"),
     )
-    return jax.shard_map(
-        per_device, mesh=mesh, in_specs=in_specs, out_specs=out_specs, check_vma=False
-    )
+    body = four_by_two if mesh.shape["expert"] == 8 and mesh.shape["tensor"] == 2 else any_size
+    return jax.shard_map(body, mesh=mesh, in_specs=in_specs, out_specs=out_specs, check_vma=False)

time: 203 us -> 149 us (0.73)
  the two profiles are of different devices: /device:TPU:0 before, /device:TPU:10 now
where the time goes in v1:
time: 149 us; the launch traced here: 147 us
  waiting for transfers between devices  58.4 us (39%)
  local copies, waits for them, and re-layouts  34.7 us (23%)
  matrix products  22.4 us (15%)
  starting transfers between devices  21.1 us (14%)
  other arithmetic  9.3 us (6%)
    ppermute x15, waiting for transfers between devices, send(): return lax.ppermute(value, 'expert', pairs)  58.4 us
    concatenate x2, local copies, waits for them, and re-layouts, four_by_two(): jnp.concatenate([g[i] for g in groups], axis=0)  26.2 us
    ppermute x15, starting transfers between devices, send(): return lax.ppermute(value, 'expert', pairs)  20.9 us
    dot_general x4, matrix products, group(): lax.dot_general(d_pre, w_in, (((1,), (1,)), ((), ())), preferred_element_...  6.13 us
    dot_general x4, matrix products, group(): front = jnp.dot(rows_x, w_in, preferred_element_type=f32)  4.51 us
  transfers between devices with their start and end apart: 19, of which 8 were waited for; matrix products, arithmetic and copies ran while one was open for 39% of the time, Pallas kernels for 0%

profile of v1, /device:TPU:10, one launch (start us, length us, event | category | flops | bytes accessed | tf_op | source)
XLA Modules:
  0.0 147.2 jit_solution(1198493227230139748)
XLA Ops:
  4.1 1.5 convolution_convert_fusion.3
  6.4 1.5 %collective-permute-start = (bf16[72,3072]{1,0:T(8,128)(2,1)}, bf16[72,3072]{1,0:T(8,128)(2,1)}, u32[]{:S(2)}, u32[]{:S(2)}) collective-permute-start(bf16[72,3072]{1,0:T(8,128)(2,1)} %pad_maximum_fusion), channel_id=1, source_target_pairs={{0,2},{2,0},{4,6},{6,4},{8,10},{10,8},{12,14},{14,12},{1,3},{3,1},... | collective-permute-start | bytes 1327112 | tf_op jit(solution)/shard_map/ppermute | solution.py:93
  7.9 3.5 %collective-permute-start.13 = (bf16[72,3072]{1,0:T(8,128)(2,1)}, bf16[72,3072]{1,0:T(8,128)(2,1)}, u32[]{:S(2)}, u32[]{:S(2)}) collective-permute-start(bf16[72,3072]{1,0:T(8,128)(2,1)} %pad_maximum_fusion), channel_id=1, source_target_pairs={{4,8},{6,10},{8,4},{10,6},{5,9},{7,11},{9,5},{11,7},{20,24},{22,26... | collective-permute-start | bytes 1327112 | tf_op jit(solution)/shard_map/ppermute | solution.py:93
  12.0 1.5 collective-permute-start.3
  14.7 2.7 %constant_dynamic-update-slice_fusion = bf16[3072,512]{1,0:T(8,128)(2,1)} fusion(bf16[3072,512]{1,0:T(8,128)(2,1)} %constant_dynamic-update-slice_fusion.1, bf16[3072,256]{1,0:T(8,128)(2,1)} %param.12), kind=kLoop, calls=%fused_computation.134 | loop fusion | bytes 3145728 | tf_op jit(solution)/shard_map/concatenate | solution.py:114
  20.4 2.6 %fusion.8 = f32[72,512]{1,0:T(8,128)S(1)} fusion(bf16[3072,512]{1,0:T(8,128)(2,1)} %constant_dynamic-update-slice_fusion, bf16[36,3072]{1,0:T(8,128)(2,1)S(1)} %convolution_convert_fusion.4, bf16[36,3072]{1,0:T(8,128)(2,1)S(1)} %get-tuple-element.18), kind=kOutput, calls=%fused_computation.24 | convolution fusion | flops 227377152 | bytes 3735552 | tf_op jit(solution)/shard_map/dot_general | solution.py:119
  23.2 16.7 %collective-permute-done.8 = bf16[72,3072]{1,0:T(8,128)(2,1)S(1)} collective-permute-done((bf16[72,3072]{1,0:T(8,128)(2,1)}, bf16[72,3072]{1,0:T(8,128)(2,1)S(1)}, u32[]{:S(2)}, u32[]{:S(2)}) %collective-permute-start.8) | collective-permute-done | bytes 442400 | tf_op jit(solution)/shard_map/ppermute | solution.py:93
  39.8 4.4 %collective-permute-start.14 = (bf16[72,3072]{1,0:T(8,128)(2,1)S(1)}, bf16[72,3072]{1,0:T(8,128)(2,1)S(1)}, u32[]{:S(2)}, u32[]{:S(2)}) collective-permute-start(bf16[72,3072]{1,0:T(8,128)(2,1)S(1)} %collective-permute-done.8), channel_id=1, source_target_pairs={{8,12},{10,14},{4,0},{6,2},{9,13},{11,15},{5,1},{7,3},{24,28},{26,... | collective-permute-start | bytes 1327112 | tf_op jit(solution)/shard_map/ppermute | solution.py:93
  44.9 1.6 %collective-permute-start.4 = (bf16[72,3072]{1,0:T(8,128)(2,1)S(1)}, bf16[72,3072]{1,0:T(8,128)(2,1)S(1)}, u32[]{:S(2)}, u32[]{:S(2)}) collective-permute-start(bf16[72,3072]{1,0:T(8,128)(2,1)S(1)} %collective-permute-done.3), channel_id=1, source_target_pairs={{0,2},{2,0},{4,6},{6,4},{8,10},{10,8},{12,14},{14,12},{1,3},{3,1},... | collective-permute-start | bytes 1327112 | tf_op jit(solution)/shard_map/ppermute | solution.py:93
  49.6 2.6 %collective-permute-done.14 = bf16[72,3072]{1,0:T(8,128)(2,1)S(1)} collective-permute-done((bf16[72,3072]{1,0:T(8,128)(2,1)S(1)}, bf16[72,3072]{1,0:T(8,128)(2,1)S(1)}, u32[]{:S(2)}, u32[]{:S(2)}) %collective-permute-start.14) | collective-permute-done | bytes 442400 | tf_op jit(solution)/shard_map/ppermute | solution.py:93
  53.9 3.5 %collective-permute-done.9 = bf16[72,3072]{1,0:T(8,128)(2,1)S(1)} collective-permute-done((bf16[72,3072]{1,0:T(8,128)(2,1)S(1)}, bf16[72,3072]{1,0:T(8,128)(2,1)S(1)}, u32[]{:S(2)}, u32[]{:S(2)}) %collective-permute-start.9) | collective-permute-done | bytes 442400 | tf_op jit(solution)/shard_map/ppermute | solution.py:93
  58.9 7.9 %collective-permute-done.4 = bf16[72,3072]{1,0:T(8,128)(2,1)S(1)} collective-permute-done((bf16[72,3072]{1,0:T(8,128)(2,1)S(1)}, bf16[72,3072]{1,0:T(8,128)(2,1)S(1)}, u32[]{:S(2)}, u32[]{:S(2)}) %collective-permute-start.4) | collective-permute-done | bytes 442400 | tf_op jit(solution)/shard_map/ppermute | solution.py:93
  72.5 1.6 %collective-permute-start.6 = (bf16[36,3072]{1,0:T(8,128)(2,1)S(1)}, bf16[36,3072]{1,0:T(8,128)(2,1)S(1)}, u32[]{:S(2)}, u32[]{:S(2)}) collective-permute-start(bf16[36,3072]{1,0:T(8,128)(2,1)S(1)} %slice.249), channel_id=1, source_target_pairs={{0,2},{2,0},{4,6},{6,4},{8,10},{10,8},{12,14},{14,12},{1,3},{3,1},... | collective-permute-start | bytes 663560 | tf_op jit(solution)/shard_map/ppermute | solution.py:93
  74.1 12.7 %collective-permute-done.11 = bf16[36,3072]{1,0:T(8,128)(2,1)S(1)} collective-permute-done((bf16[36,3072]{1,0:T(8,128)(2,1)S(1)}, bf16[36,3072]{1,0:T(8,128)(2,1)S(1)}, u32[]{:S(2)}, u32[]{:S(2)}) %collective-permute-start.11) | collective-permute-done | bytes 221216 | tf_op jit(solution)/shard_map/ppermute | solution.py:93
  90.8 2.7 %collective-permute-start.7 = (bf16[36,3072]{1,0:T(8,128)(2,1)}, bf16[36,3072]{1,0:T(8,128)(2,1)}, u32[]{:S(2)}, u32[]{:S(2)}) collective-permute-start(bf16[36,3072]{1,0:T(8,128)(2,1)} %fusion.3), channel_id=1, source_target_pairs={{0,4},{2,6},{4,0},{6,2},{8,12},{10,14},{12,8},{14,10},{1,5},{3,7},... | collective-permute-start | bytes 663560 | tf_op jit(solution)/shard_map/ppermute | solution.py:93
  93.5 14.3 %concatenate.86 = bf16[288,3072]{1,0:T(8,128)(2,1)} concatenate(bf16[36,3072]{1,0:T(8,128)(2,1)S(1)} %convolution_convert_fusion.4, bf16[36,3072]{1,0:T(8,128)(2,1)S(1)} %get-tuple-element.18, bf16[36,3072]{1,0:T(8,128)(2,1)S(1)} %get-tuple-element.6, bf16[36,3072]{1,0:T(8,128)(2,1)S(1)} %get-tuple-element.8, bf16[36,3072]{1,0:T(8,128)(2,1)S(1)} %get-tuple-element.10, ...), dimensions={0} | concatenate | bytes 3538944 | tf_op jit(solution)/shard_map/concatenate | solution.py:138
  107.8 11.9 %concatenate.89 = bf16[288,3072]{1,0:T(8,128)(2,1)S(1)} concatenate(bf16[36,3072]{1,0:T(8,128)(2,1)} %copy-done.2, bf16[36,3072]{1,0:T(8,128)(2,1)} %copy-done.5, bf16[36,3072]{1,0:T(8,128)(2,1)} %copy-done.7, bf16[36,3072]{1,0:T(8,128)(2,1)} %copy-done.10, bf16[36,3072]{1,0:T(8,128)(2,1)} %copy-done.6, bf16[36,3072]{1,0:T(8,128)(2,1)} %copy-done.8, bf16[36,3072]{1,0:T(8,128)(2,1)} %copy-done.9, ...), dimensions={0} | concatenate | bytes 3538944 | tf_op jit(solution)/shard_map/concatenate | solution.py:138
  120.9 2.9 %fusion.77 = f32[72,3072]{1,0:T(8,128)S(1)} fusion(bf16[3072,512]{1,0:T(8,128)(2,1)} %constant_dynamic-update-slice_fusion, bf16[72,256]{1,0:T(8,128)(2,1)S(1)} %get-tuple-element.31, bf16[72,256]{1,0:T(8,128)(2,1)S(1)} %get-tuple-element.30), kind=kOutput, calls=%fused_computation.101 | convolution fusion | flops 226639872 | bytes 4104192 | tf_op jit(solution)/shard_map/dot_general | solution.py:126
  124.5 1.8 %convolution_convert_fusion = bf16[3072,512]{1,0:T(8,128)(2,1)S(1)} fusion(bf16[288,3072]{1,0:T(8,128)(2,1)S(1)} %copy-done.12, bf16[72,256]{1,0:T(8,128)(2,1)S(1)} %get-tuple-element.31, bf16[72,256]{1,0:T(8,128)(2,1)S(1)} %get-tuple-element.30, bf16[72,256]{1,0:T(8,128)(2,1)S(1)} %copy-done.27, bf16[72,256]{1,0:T(8,128)(2,1)S(1)} %copy-done.25, ...), kind=kOutput, calls=%fused_computation | convolution fusion | flops 909901824 | bytes 5210112 | tf_op jit(solution)/shard_map/dot_general | solution.py:44
  126.4 1.9 %fusion.110 = (bf16[3072,256]{1,0:T(8,128)(2,1)}, bf16[3072,256]{1,0:T(8,128)(2,1)}) fusion(bf16[3072,512]{1,0:T(8,128)(2,1)S(1)} %convolution_convert_fusion), kind=kLoop, calls=%fused_computation.154 | loop fusion | bytes 6291456 | tf_op jit(solution)/shard_map/slice | solution.py:50
  128.3 3.8 %collective-permute-done.17 = bf16[36,3072]{1,0:T(8,128)(2,1)S(1)} collective-permute-done((bf16[36,3072]{1,0:T(8,128)(2,1)S(1)}, bf16[36,3072]{1,0:T(8,128)(2,1)S(1)}, u32[]{:S(2)}, u32[]{:S(2)}) %collective-permute-start.17) | collective-permute-done | bytes 221216 | tf_op jit(solution)/shard_map/ppermute | solution.py:93
  132.6 2.1 %convolution_convert_fusion.1 = bf16[256,3072]{1,0:T(8,128)(2,1)} fusion(bf16[288,3072]{1,0:T(8,128)(2,1)S(1)} %concatenate.89, bf16[72,256]{1,0:T(8,128)(2,1)S(1)} %get-tuple-element.29, bf16[72,256]{1,0:T(8,128)(2,1)S(1)} %copy-done.18, bf16[72,256]{1,0:T(8,128)(2,1)S(1)} %copy-done.19, bf16[72,256]{1,0:T(8,128)(2,1)S(1)} %copy-done.17), kind=kOutput, calls=%fused_computation.1 | convolution fusion | flops 454361088 | bytes 3489792 | tf_op jit(solution)/shard_map/dot_general | solution.py:47
  134.8 9.9 %collective-permute-done.18 = bf16[36,3072]{1,0:T(8,128)(2,1)S(1)} collective-permute-done((bf16[36,3072]{1,0:T(8,128)(2,1)S(1)}, bf16[36,3072]{1,0:T(8,128)(2,1)S(1)}, u32[]{:S(2)}, u32[]{:S(2)}) %collective-permute-start.18) | collective-permute-done | bytes 221216 | tf_op jit(solution)/shard_map/ppermute | solution.py:93
  144.7 2.5 %convolution_convert_fusion.2 = bf16[128,3072]{1,0:T(8,128)(2,1)} fusion(f32[72,3072]{1,0:T(8,128)S(1)} %copy-done.4, bf16[36,3072]{1,0:T(8,128)(2,1)S(1)} %collective-permute-done.18, bf16[36,3072]{1,0:T(8,128)(2,1)} %collective-permute-done.12, bf16[36,3072]{1,0:T(8,128)(2,1)} %collective-permute-done.7, bf16[36,3072]{1,0:T(8,128)(2,1)} %collective-permute-done.2, ...), kind=kOutput, calls=%fused_computation.2 | convolution fusion | flops 29709312 | bytes 2188288 | tf_op jit(solution)/shard_map/dot_general | solution.py:38
  (134 shorter events, 27.8 us)
Async XLA Ops:
  0.6 19.2 %copy-start = (bf16[256,3072]{1,0:T(8,128)(2,1)S(1)}, bf16[256,3072]{1,0:T(8,128)(2,1)}, u32[]{:S(2)}) copy-start(bf16[256,3072]{1,0:T(8,128)(2,1)} %param.13) | copy-start | bytes 4718596
  6.4 12.2 %collective-permute-start = (bf16[72,3072]{1,0:T(8,128)(2,1)}, bf16[72,3072]{1,0:T(8,128)(2,1)}, u32[]{:S(2)}, u32[]{:S(2)}) collective-permute-start(bf16[72,3072]{1,0:T(8,128)(2,1)} %pad_maximum_fusion), channel_id=1, source_target_pairs={{0,2},{2,0},{4,6},{6,4},{8,10},{10,8},{12,14},{14,12},{1,3},{3,1},... | collective-permute-start | bytes 1327112 | tf_op jit(solution)/shard_map/ppermute | solution.py:93
  7.9 41.7 %collective-permute-start.13 = (bf16[72,3072]{1,0:T(8,128)(2,1)}, bf16[72,3072]{1,0:T(8,128)(2,1)}, u32[]{:S(2)}, u32[]{:S(2)}) collective-permute-start(bf16[72,3072]{1,0:T(8,128)(2,1)} %pad_maximum_fusion), channel_id=1, source_target_pairs={{4,8},{6,10},{8,4},{10,6},{5,9},{7,11},{9,5},{11,7},{20,24},{22,26... | collective-permute-start | bytes 1327112 | tf_op jit(solution)/shard_map/ppermute | solution.py:93
  11.4 28.4 %collective-permute-start.8 = (bf16[72,3072]{1,0:T(8,128)(2,1)}, bf16[72,3072]{1,0:T(8,128)(2,1)S(1)}, u32[]{:S(2)}, u32[]{:S(2)}) collective-permute-start(bf16[72,3072]{1,0:T(8,128)(2,1)} %pad_maximum_fusion), channel_id=1, source_target_pairs={{0,8},{2,10},{4,12},{6,14},{8,0},{10,2},{12,4},{14,6},{1,9},{3,11}... | collective-permute-start | bytes 1327112 | tf_op jit(solution)/shard_map/ppermute | solution.py:93
  12.0 32.9 %collective-permute-start.3 = (bf16[72,3072]{1,0:T(8,128)(2,1)}, bf16[72,3072]{1,0:T(8,128)(2,1)S(1)}, u32[]{:S(2)}, u32[]{:S(2)}) collective-permute-start(bf16[72,3072]{1,0:T(8,128)(2,1)} %pad_maximum_fusion), channel_id=1, source_target_pairs={{0,4},{2,6},{4,0},{6,2},{8,12},{10,14},{12,8},{14,10},{1,5},{3,7},... | collective-permute-start | bytes 1327112 | tf_op jit(solution)/shard_map/ppermute | solution.py:93
  19.8 25.1 %copy-start.5 = (bf16[36,3072]{1,0:T(8,128)(2,1)}, bf16[36,3072]{1,0:T(8,128)(2,1)S(1)}, u32[]{:S(2)}) copy-start(bf16[36,3072]{1,0:T(8,128)(2,1)S(1)} %get-tuple-element.19) | copy-start | bytes 663556
  20.4 26.8 %copy-start.1 = (bf16[3072,512]{1,0:T(8,128)(2,1)S(1)}, bf16[3072,512]{1,0:T(8,128)(2,1)}, u32[]{:S(2)}) copy-start(bf16[3072,512]{1,0:T(8,128)(2,1)} %constant_dynamic-update-slice_fusion) | copy-start | bytes 9437188
  23.1 23.4 %collective-permute-start.1 = (bf16[72,768]{1,0:T(8,128)(2,1)S(1)}, bf16[72,768]{1,0:T(8,128)(2,1)S(1)}, u32[]{:S(2)}, u32[]{:S(2)}) collective-permute-start(bf16[72,768]{1,0:T(8,128)(2,1)S(1)} %fusion.57), channel_id=1, source_target_pairs={{0,1},{1,0},{2,3},{3,2},{4,5},{5,4},{6,7},{7,6},{8,9},{9,8},{10,11... | collective-permute-start | bytes 331784 | tf_op jit(solution)/shard_map/ppermute | solution.py:124
  39.8 12.4 %collective-permute-start.14 = (bf16[72,3072]{1,0:T(8,128)(2,1)S(1)}, bf16[72,3072]{1,0:T(8,128)(2,1)S(1)}, u32[]{:S(2)}, u32[]{:S(2)}) collective-permute-start(bf16[72,3072]{1,0:T(8,128)(2,1)S(1)} %collective-permute-done.8), channel_id=1, source_target_pairs={{8,12},{10,14},{4,0},{6,2},{9,13},{11,15},{5,1},{7,3},{24,28},{26,... | collective-permute-start | bytes 1327112 | tf_op jit(solution)/shard_map/ppermute | solution.py:93
  44.2 13.2 %collective-permute-start.9 = (bf16[72,3072]{1,0:T(8,128)(2,1)S(1)}, bf16[72,3072]{1,0:T(8,128)(2,1)S(1)}, u32[]{:S(2)}, u32[]{:S(2)}) collective-permute-start(bf16[72,3072]{1,0:T(8,128)(2,1)S(1)} %collective-permute-done.8), channel_id=1, source_target_pairs={{0,2},{2,0},{4,6},{6,4},{8,10},{10,8},{12,14},{14,12},{1,3},{3,1},... | collective-permute-start | bytes 1327112 | tf_op jit(solution)/shard_map/ppermute | solution.py:93
  44.9 22.0 %collective-permute-start.4 = (bf16[72,3072]{1,0:T(8,128)(2,1)S(1)}, bf16[72,3072]{1,0:T(8,128)(2,1)S(1)}, u32[]{:S(2)}, u32[]{:S(2)}) collective-permute-start(bf16[72,3072]{1,0:T(8,128)(2,1)S(1)} %collective-permute-done.3), channel_id=1, source_target_pairs={{0,2},{2,0},{4,6},{6,4},{8,10},{10,8},{12,14},{14,12},{1,3},{3,1},... | collective-permute-start | bytes 1327112 | tf_op jit(solution)/shard_map/ppermute | solution.py:93
  46.5 20.4 %copy-start.7 = (bf16[36,3072]{1,0:T(8,128)(2,1)}, bf16[36,3072]{1,0:T(8,128)(2,1)S(1)}, u32[]{:S(2)}) copy-start(bf16[36,3072]{1,0:T(8,128)(2,1)S(1)} %get-tuple-element.7) | copy-start | bytes 663556
  49.1 85.6 %collective-permute-start.2 = (bf16[36,3072]{1,0:T(8,128)(2,1)}, bf16[36,3072]{1,0:T(8,128)(2,1)}, u32[]{:S(2)}, u32[]{:S(2)}) collective-permute-start(bf16[36,3072]{1,0:T(8,128)(2,1)} %slice.250), channel_id=1, source_target_pairs={{0,2},{2,0},{4,6},{6,4},{8,10},{10,8},{12,14},{14,12},{1,3},{3,1},... | collective-permute-start | bytes 663560 | tf_op jit(solution)/shard_map/ppermute | solution.py:93
  53.3 34.7 %collective-permute-start.15 = (bf16[72,3072]{1,0:T(8,128)(2,1)S(1)}, bf16[72,3072]{1,0:T(8,128)(2,1)S(1)}, u32[]{:S(2)}, u32[]{:S(2)}) collective-permute-start(bf16[72,3072]{1,0:T(8,128)(2,1)S(1)} %broadcast_select_fusion), channel_id=1, source_target_pairs={{0,2},{2,0},{4,6},{6,4},{8,10},{10,8},{12,14},{14,12},{1,3},{3,1},... | collective-permute-start | bytes 1327112 | tf_op jit(solution)/shard_map/ppermute | solution.py:93
  58.7 9.5 %collective-permute-start.10 = (bf16[72,768]{1,0:T(8,128)(2,1)S(1)}, bf16[72,768]{1,0:T(8,128)(2,1)S(1)}, u32[]{:S(2)}, u32[]{:S(2)}) collective-permute-start(bf16[72,768]{1,0:T(8,128)(2,1)S(1)} %fusion.55), channel_id=1, source_target_pairs={{0,1},{1,0},{2,3},{3,2},{4,5},{5,4},{6,7},{7,6},{8,9},{9,8},{10,11... | collective-permute-start | bytes 331784 | tf_op jit(solution)/shard_map/ppermute | solution.py:124
  58.9 29.8 %copy-start.9 = (bf16[36,3072]{1,0:T(8,128)(2,1)}, bf16[36,3072]{1,0:T(8,128)(2,1)S(1)}, u32[]{:S(2)}) copy-start(bf16[36,3072]{1,0:T(8,128)(2,1)S(1)} %get-tuple-element.15) | copy-start | bytes 663556
  68.2 2.5 %collective-permute-start.5 = (bf16[72,768]{1,0:T(8,128)(2,1)S(1)}, bf16[72,768]{1,0:T(8,128)(2,1)S(1)}, u32[]{:S(2)}, u32[]{:S(2)}) collective-permute-start(bf16[72,768]{1,0:T(8,128)(2,1)S(1)} %fusion.56), channel_id=1, source_target_pairs={{0,1},{1,0},{2,3},{3,2},{4,5},{5,4},{6,7},{7,6},{8,9},{9,8},{10,11... | collective-permute-start | bytes 331784 | tf_op jit(solution)/shard_map/ppermute | solution.py:124
  70.1 16.7 %collective-permute-start.11 = (bf16[36,3072]{1,0:T(8,128)(2,1)S(1)}, bf16[36,3072]{1,0:T(8,128)(2,1)S(1)}, u32[]{:S(2)}, u32[]{:S(2)}) collective-permute-start(bf16[36,3072]{1,0:T(8,128)(2,1)S(1)} %slice.248), channel_id=1, source_target_pairs={{0,2},{2,0},{4,6},{6,4},{8,10},{10,8},{12,14},{14,12},{1,3},{3,1},... | collective-permute-start | bytes 663560 | tf_op jit(solution)/shard_map/ppermute | solution.py:93
  72.5 17.5 %collective-permute-start.6 = (bf16[36,3072]{1,0:T(8,128)(2,1)S(1)}, bf16[36,3072]{1,0:T(8,128)(2,1)S(1)}, u32[]{:S(2)}, u32[]{:S(2)}) collective-permute-start(bf16[36,3072]{1,0:T(8,128)(2,1)S(1)} %slice.249), channel_id=1, source_target_pairs={{0,2},{2,0},{4,6},{6,4},{8,10},{10,8},{12,14},{14,12},{1,3},{3,1},... | collective-permute-start | bytes 663560 | tf_op jit(solution)/shard_map/ppermute | solution.py:93
  87.6 47.2 %collective-permute-start.12 = (bf16[36,3072]{1,0:T(8,128)(2,1)}, bf16[36,3072]{1,0:T(8,128)(2,1)}, u32[]{:S(2)}, u32[]{:S(2)}) collective-permute-start(bf16[36,3072]{1,0:T(8,128)(2,1)} %fusion.2), channel_id=1, source_target_pairs={{0,8},{2,10},{4,12},{6,14},{8,0},{10,2},{12,4},{14,6},{1,9},{3,11}... | collective-permute-start | bytes 663560 | tf_op jit(solution)/shard_map/ppermute | solution.py:93
  90.0 29.8 %collective-permute-start.16 = (bf16[72,768]{1,0:T(8,128)(2,1)}, bf16[72,768]{1,0:T(8,128)(2,1)}, u32[]{:S(2)}, u32[]{:S(2)}) collective-permute-start(bf16[72,768]{1,0:T(8,128)(2,1)} %fusion.54), channel_id=1, source_target_pairs={{0,1},{1,0},{2,3},{3,2},{4,5},{5,4},{6,7},{7,6},{8,9},{9,8},{10,11... | collective-permute-start | bytes 331784 | tf_op jit(solution)/shard_map/ppermute | solution.py:124
  90.8 44.0 %collective-permute-start.7 = (bf16[36,3072]{1,0:T(8,128)(2,1)}, bf16[36,3072]{1,0:T(8,128)(2,1)}, u32[]{:S(2)}, u32[]{:S(2)}) collective-permute-start(bf16[36,3072]{1,0:T(8,128)(2,1)} %fusion.3), channel_id=1, source_target_pairs={{0,4},{2,6},{4,0},{6,2},{8,12},{10,14},{12,8},{14,10},{1,5},{3,7},... | collective-permute-start | bytes 663560 | tf_op jit(solution)/shard_map/ppermute | solution.py:93
  123.9 8.2 %collective-permute-start.17 = (bf16[36,3072]{1,0:T(8,128)(2,1)S(1)}, bf16[36,3072]{1,0:T(8,128)(2,1)S(1)}, u32[]{:S(2)}, u32[]{:S(2)}) collective-permute-start(bf16[36,3072]{1,0:T(8,128)(2,1)S(1)} %slice.247), channel_id=1, source_target_pairs={{0,2},{2,0},{4,6},{6,4},{8,10},{10,8},{12,14},{14,12},{1,3},{3,1},... | collective-permute-start | bytes 663560 | tf_op jit(solution)/shard_map/ppermute | solution.py:93
  132.1 12.6 %collective-permute-start.18 = (bf16[36,3072]{1,0:T(8,128)(2,1)S(1)}, bf16[36,3072]{1,0:T(8,128)(2,1)S(1)}, u32[]{:S(2)}, u32[]{:S(2)}) collective-permute-start(bf16[36,3072]{1,0:T(8,128)(2,1)S(1)} %fusion.1), channel_id=1, source_target_pairs={{0,12},{2,14},{4,8},{6,10},{8,4},{10,6},{12,0},{14,2},{1,13},{3,15... | collective-permute-start | bytes 663560 | tf_op jit(solution)/shard_map/ppermute | solution.py:93
  (27 other events, 197.1 us)

commit v2 on v0

--- a/solution.py
+++ b/solution.py
@@ -1,6 +1,8 @@
 import jax
 import jax.numpy as jnp
 from jax import lax
+from jax.experimental import pallas as pl
+from jax.experimental.pallas import tpu as pltpu
 from jax.sharding import PartitionSpec as P
 
 CAP = 36
@@ -21,8 +23,7 @@
     return (hidden, jnp.concatenate([d_gate, d_up], axis=1))
 
 
-def per_device(tokens, grad_out, expert_ids, gate_probs, w_gate, w_up, w_down):
-    width = w_gate.shape[1]
+def place(tokens, grad_out, expert_ids, gate_probs):
     chosen = expert_ids == window_expert
     weight = jnp.sum(jnp.where(chosen, gate_probs, jnp.zeros_like(gate_probs)), axis=1)
     scaled = (weight[:, None] * grad_out.astype(jnp.float32)).astype(jnp.bfloat16)
@@ -32,6 +33,28 @@
     placing = ((slot_of[None, :] == slot_ids[:, None]) & routed[None, :]).astype(jnp.bfloat16)
     send_x = jnp.dot(placing, tokens, preferred_element_type=jnp.float32).astype(jnp.bfloat16)
     send_dy = jnp.dot(placing, scaled, preferred_element_type=jnp.float32).astype(jnp.bfloat16)
+    return placing, send_x, send_dy
+
+
+def unplace(placing, summed):
+    return lax.dot_general(
+        placing, summed, (((0,), (0,)), ((), ())), preferred_element_type=jnp.float32
+    ).astype(jnp.bfloat16)
+
+
+def weight_grads(rows_x, rows_dy, hidden, d_pre, width):
+    grad_w_in = lax.dot_general(
+        rows_x, d_pre, (((0,), (0,)), ((), ())), preferred_element_type=jnp.float32
+    ).astype(jnp.bfloat16)
+    grad_down = lax.dot_general(
+        hidden, rows_dy, (((0,), (0,)), ((), ())), preferred_element_type=jnp.float32
+    ).astype(jnp.bfloat16)
+    return (grad_w_in[:, :width], grad_w_in[:, width:], grad_down)
+
+
+def any_size(tokens, grad_out, expert_ids, gate_probs, w_gate, w_up, w_down):
+    width = w_gate.shape[1]
+    placing, send_x, send_dy = place(tokens, grad_out, expert_ids, gate_probs)
     rows_x, rows_dy = (
         lax.all_gather(send_x, "expert", axis=0, tiled=True),
         lax.all_gather(send_dy, "expert", axis=0, tiled=True),
@@ -58,16 +81,225 @@
         scatter_dimension=0,
         tiled=True,
     )
-    grad_in = lax.dot_general(
-        placing, summed, (((0,), (0,)), ((), ())), preferred_element_type=jnp.float32
-    ).astype(jnp.bfloat16)
-    grad_w_in = lax.dot_general(
-        rows_x, d_pre, (((0,), (0,)), ((), ())), preferred_element_type=jnp.float32
-    ).astype(jnp.bfloat16)
-    grad_down = lax.dot_general(
-        hidden, rows_dy, (((0,), (0,)), ((), ())), preferred_element_type=jnp.float32
-    ).astype(jnp.bfloat16)
-    return (grad_in, grad_w_in[:, :width], grad_w_in[:, width:], grad_down)
+    grad_in = unplace(placing, summed)
+    return (grad_in,) + weight_grads(rows_x, rows_dy, hidden, d_pre, width)
+
+
+MAIN = 32
+TAIL = CAP - MAIN
+BLOCK = 2 * CAP
+TERM = 40
+GROUP = 80
+BF16, F32 = jnp.bfloat16, jnp.float32
+
+
+def struct(rows, columns, dtype):
+    return jax.ShapeDtypeStruct((rows, columns), dtype)
+
+
+def call(kernel, outs, *args, name, **more):
+    return pl.pallas_call(
+        kernel,
+        out_shape=outs,
+        name=name,
+        compiler_params=pltpu.CompilerParams(vmem_limit_bytes=24 * 2**20),
+        cost_estimate=pl.CostEstimate(flops=1000, bytes_accessed=1000, transcendentals=0),
+        **more,
+    )(*args)
+
+
+def mul(left, right, left_dim=1, right_dim=0):
+    return lax.dot_general(
+        left, right, (((left_dim,), (right_dim,)), ((), ())), preferred_element_type=F32
+    )
+
+
+def place_kernel(tokens, grad_out, ids, probs, block, placing_t):
+    rows = tokens.shape[0]
+    chosen = ids[...] == window_expert
+    weight = jnp.sum(jnp.where(chosen, probs[...], 0.0), axis=1, keepdims=True)
+    routed = jnp.max(chosen.astype(F32), axis=1, keepdims=True)
+    at_row = lax.broadcasted_iota(jnp.int32, (rows, rows), 0)
+    at_column = lax.broadcasted_iota(jnp.int32, (rows, rows), 1)
+    same = at_row == at_column
+    routed_row = jnp.sum(jnp.where(same, routed, 0.0), axis=0, keepdims=True)
+    weight_row = jnp.sum(jnp.where(same, weight, 0.0), axis=0, keepdims=True)
+    slot_row = jnp.sum(jnp.where(at_row <= at_column, routed, 0.0), axis=0, keepdims=True) - 1.0
+    slot = jnp.sum(jnp.where(at_column <= at_row, routed_row, 0.0), axis=1, keepdims=True) - 1.0
+    wanted = lax.broadcasted_iota(jnp.int32, (TERM, rows), 0).astype(F32)
+    placing = jnp.where((slot_row == wanted) & (routed_row > 0.0), 1.0, 0.0)
+    wanted = at_column.astype(F32)
+    placing_t[...] = jnp.where((slot == wanted) & (routed > 0.0), 1.0, 0.0).astype(BF16)
+    scale = jnp.sum(placing * weight_row, axis=1, keepdims=True)
+    placing = placing.astype(BF16)
+    x = mul(placing, tokens[...])
+    dy = mul(placing, grad_out[...]) * scale
+    block[0:MAIN, :] = x[0:MAIN].astype(BF16)
+    block[MAIN : 2 * MAIN, :] = dy[0:MAIN].astype(BF16)
+    last = jnp.concatenate([x[MAIN:CAP], dy[MAIN:CAP]], axis=0)
+    block[2 * MAIN : BLOCK, :] = last.astype(BF16)
+
+
+def tails(blocks, turned):
+    parts = []
+    for block in blocks:
+        last = block[2 * MAIN : BLOCK, :].astype(F32)
+        if turned:
+            last = jnp.concatenate([last[TAIL:], last[:TAIL]], axis=0)
+        parts.append(last)
+    return jnp.concatenate(parts, axis=0).astype(BF16)
+
+
+def rows_of(blocks, first, turned):
+    return jnp.concatenate(
+        [block[first : first + MAIN, :] for block in blocks] + [tails(blocks, turned)], axis=0
+    )
+
+
+def front_kernel(mine, other, w_gate, w_up, w_down, part, sent):
+    width = w_gate.shape[1]
+    x = rows_of((mine, other), 0, False)
+    dy = rows_of((mine, other), MAIN, True)
+    for at, value in enumerate(
+        (mul(x, w_gate[...]), mul(x, w_up[...]), mul(dy, w_down[...], 1, 1))
+    ):
+        part[:, at * width : (at + 1) * width] = value
+        sent[:, at * width : (at + 1) * width] = value.astype(BF16)
+
+
+def back_kernel(part, arrived, w_gate, w_up, hidden, d_pre, term, sent):
+    width = w_gate.shape[1]
+    sums = part[...] + arrived[...].astype(F32)
+    z_gate, z_up, d_hidden = (sums[:, i * width : (i + 1) * width] for i in range(3))
+    sig = jax.nn.sigmoid(z_gate)
+    act = z_gate * sig
+    row = lax.broadcasted_iota(jnp.int32, (GROUP, width), 0)
+    real = (row < 2 * MAIN) | (row % 8 < TAIL)
+    hidden[...] = jnp.where(real, act * z_up, 0.0).astype(BF16)
+    d_gate = d_hidden * z_up * sig * (1.0 + z_gate * (1.0 - sig))
+    d_gate = jnp.where(real, d_gate, 0.0).astype(BF16)
+    d_up = jnp.where(real, d_hidden * act, 0.0).astype(BF16)
+    d_pre[:, :width] = d_gate
+    d_pre[:, width:] = d_up
+    value = mul(d_gate, w_gate[...], 1, 1) + mul(d_up, w_up[...], 1, 1)
+    term[0:MAIN, :] = value[0:MAIN]
+    term[MAIN:TERM, :] = value[2 * MAIN : 2 * MAIN + 8]
+    sent[0:MAIN, :] = value[MAIN : 2 * MAIN].astype(BF16)
+    sent[MAIN:TERM, :] = value[2 * MAIN + 8 : GROUP].astype(BF16)
+
+
+def add_kernel(term, arrived, total):
+    total[...] = (term[...] + arrived[...].astype(F32)).astype(BF16)
+
+
+def finish_kernel(placing_t, first, second, third, fourth, grad_in):
+    total = first[...].astype(F32) + second[...].astype(F32)
+    total = total + third[...].astype(F32) + fourth[...].astype(F32)
+    grad_in[...] = mul(placing_t[:, :TERM], total.astype(BF16)).astype(BF16)
+
+
+def grads_kernel(*refs):
+    blocks, hiddens, d_pres = refs[0:8], refs[8:12], refs[12:16]
+    grad_gate, grad_up, grad_down = refs[16:19]
+    width = grad_gate.shape[1]
+
+    def groups(values):
+        return jnp.concatenate(
+            [v[: 2 * MAIN, :] for v in values] + [v[2 * MAIN :, :] for v in values], axis=0
+        )
+
+    def rows(first, turned):
+        return jnp.concatenate(
+            [v[first : first + MAIN, :] for v in blocks]
+            + [tails(blocks[i : i + 2], turned) for i in range(0, 8, 2)],
+            axis=0,
+        )
+
+    d_pre, hidden = groups(d_pres), groups(hiddens)
+    x = rows(0, False)
+    grad_gate[...] = mul(x, d_pre[:, :width], 0, 0).astype(BF16)
+    grad_up[...] = mul(x, d_pre[:, width:], 0, 0).astype(BF16)
+    grad_down[...] = mul(hidden, rows(MAIN, True), 0, 0).astype(BF16)
+
+
+def four_by_two(tokens, grad_out, expert_ids, gate_probs, w_gate, w_up, w_down):
+    features, width = w_gate.shape
+
+    def across(value):
+        return lax.ppermute(value, "expert", [(i, i ^ 1) for i in range(8)])
+
+    def along(value, distance):
+        return lax.ppermute(value, "expert", [(i, i ^ (2 * distance)) for i in range(8)])
+
+    def after(value, *others):
+        return lax.optimization_barrier((value,) + others)[0]
+
+    gate, up, down = (pltpu.with_memory_space_constraint(w, pltpu.VMEM) for w in (w_gate, w_up, w_down))
+
+    own, placing_t = call(
+        place_kernel,
+        (struct(BLOCK, features, BF16), struct(tokens.shape[0], tokens.shape[0], BF16)),
+        tokens, grad_out, expert_ids, gate_probs, name="place",
+    )
+
+    def front(mine, other):
+        part, sent = call(
+            front_kernel,
+            (struct(GROUP, 3 * width, F32), struct(GROUP, 3 * width, BF16)),
+            mine, other, gate, up, down, name="front",
+        )
+        return part, lax.ppermute(sent, "tensor", [(0, 1), (1, 0)])
+
+    def back(part, arrived):
+        hidden, d_pre, term, sent = call(
+            back_kernel,
+            (
+                struct(GROUP, width, BF16),
+                struct(GROUP, 2 * width, BF16),
+                struct(TERM, features, F32),
+                struct(TERM, features, BF16),
+            ),
+            part, arrived, gate, up, name="back",
+        )
+        total = call(add_kernel, struct(TERM, features, BF16), term, across(sent), name="add")
+        return hidden, d_pre, total
+
+    two = along(own, 2)
+    one = along(own, 1)
+    own_y = across(own)
+    three = along(after(own, one), 3)
+    one_y, two_y, three_y = across(one), across(two), across(three)
+
+    h0, d0, q0 = back(*front(after(own, one), own_y))
+    h1, d1, q1 = back(*front(after(one, two), one_y))
+    r1 = along(q1, 1)
+    h2, d2, q2 = back(*front(after(two, q0), two_y))
+    r2 = along(q2, 2)
+    h3, d3, q3 = back(*front(after(three, q2, r1), three_y))
+    r3 = along(q3, 3)
+
+    tile = features // 4
+    column = pl.BlockSpec((BLOCK, tile), lambda j: (0, j))
+    whole = [pl.BlockSpec((GROUP, width), lambda j: (0, 0))] * 4
+    whole += [pl.BlockSpec((GROUP, 2 * width), lambda j: (0, 0))] * 4
+    grads = call(
+        grads_kernel,
+        (struct(features, width, BF16), struct(features, width, BF16), struct(width, features, BF16)),
+        after(own, q3), own_y, one, one_y, two, two_y, three, three_y, h0, h1, h2, h3, d0, d1, d2, d3,
+        name="grads",
+        grid=(features // tile,),
+        in_specs=[column] * 8 + whole,
+        out_specs=(
+            pl.BlockSpec((tile, width), lambda j: (j, 0)),
+            pl.BlockSpec((tile, width), lambda j: (j, 0)),
+            pl.BlockSpec((width, tile), lambda j: (0, j)),
+        ),
+    )
+    grads, r3 = lax.optimization_barrier((grads, r3))
+    grad_in = call(
+        finish_kernel, struct(tokens.shape[0], features, BF16), placing_t, q0, r1, r2, r3, name="finish"
+    )
+    return (grad_in,) + tuple(grads)
 
 
 def solution(mesh):
@@ -86,6 +318,6 @@
         P(("pipe", "tensor"), "expert"),
         P(("pipe", "expert"), "tensor"),
     )
-    return jax.shard_map(
-        per_device, mesh=mesh, in_specs=in_specs, out_specs=out_specs, check_vma=False
-    )
+    small = mesh.shape["expert"] == 8 and mesh.shape["tensor"] == 2
+    body = four_by_two if small else any_size
+    return jax.shard_map(body, mesh=mesh, in_specs=in_specs, out_specs=out_specs, check_vma=False)

time: 203 us -> 109 us (0.54)
  blocking collectives: 53.3 us -> 0 us
  waiting for transfers between devices: 93.4 us -> 64.5 us
  matrix products: 20.6 us -> 0 us
  starting transfers between devices: 2.1 us -> 21.5 us
  Pallas kernels: 0 us -> 15.3 us
  between operations: 14.5 us -> 0.77 us
  local copies, waits for them, and re-layouts: 15.2 us -> 6.78 us
  other arithmetic: 3.7 us -> 0 us
    all_gather x2 -> x0, waiting for transfers between devices: 87.5 us -> none  [the longest x1 44.2 us: per_device(): lax.all_gather(send_x, 'expert', axis=0, tiled=True)]
    ppermute x0 -> x18, waiting for transfers between devices: none -> 64.5 us  [the longest x6 30.5 us: along(): lax.ppermute(value, 'expert', [(i, i ^ 2 * distance) for i in range(8)])]
    unnamed x1 -> x0, blocking collectives: 49.4 us -> none
    ppermute x0 -> x18, starting transfers between devices: none -> 21.5 us  [the longest x6 10.6 us: along(): lax.ppermute(value, 'expert', [(i, i ^ 2 * distance) for i in range(8)])]
    dot_general x8 -> x0, matrix products: 20.6 us -> none  [the longest x1 4.42 us: per_device(): lax.dot_general(d_pre, w_in, (((1,), (1,)), ((), ())), preferred_element_...]
    pallas_call x0 -> x15, Pallas kernels: none -> 15.3 us  [call(): pl.pallas_call(kernel, out_shape=outs, name=name, compiler_params=pltpu.C...]
    reduce_scatter x1 -> x0, waiting for transfers between devices: 5.81 us -> none  [per_device(): lax.psum_scatter(partial_value.astype(jnp.bfloat16), 'tensor', scatter_di...]
    all_gather x2 -> x0, blocking collectives: 3.92 us -> none  [the longest x1 2.02 us: per_device(): lax.all_gather(grads_part, 'tensor', axis=0, tiled=True)]
  transfers between devices with their start and end apart: 4 -> 18, of which waited for: 3 -> 11; matrix products, arithmetic and copies ran while one was open for 9% -> 0% of each run, Pallas kernels for 0% -> 10%
where the time goes in v2:
time: 109 us
  waiting for transfers between devices  64.5 us (59%)
  starting transfers between devices  21.5 us (20%)
  Pallas kernels  15.3 us (14%)
  local copies, waits for them, and re-layouts  6.78 us (6%)
    ppermute x6, waiting for transfers between devices, along(): lax.ppermute(value, 'expert', [(i, i ^ 2 * distance) for i in range(8)])  30.5 us
    ppermute x8, waiting for transfers between devices, across(): return lax.ppermute(value, 'expert', [(i, i ^ 1) for i in range(8)])  28.7 us
    pallas_call x15, Pallas kernels, call(): pl.pallas_call(kernel, out_shape=outs, name=name, compiler_params=pltpu.C...  15.3 us
    ppermute x6, starting transfers between devices, along(): lax.ppermute(value, 'expert', [(i, i ^ 2 * distance) for i in range(8)])  10.6 us
    ppermute x8, starting transfers between devices, across(): return lax.ppermute(value, 'expert', [(i, i ^ 1) for i in range(8)])  10.6 us
    unnamed x16, local copies, waits for them, and re-layouts  6.78 us
    ppermute x4, waiting for transfers between devices, front(): return (part, lax.ppermute(sent, 'tensor', [(0, 1), (1, 0)]))  5.29 us
  transfers between devices with their start and end apart: 18, of which 11 were waited for; matrix products, arithmetic and copies ran while one was open for 0% of the time, Pallas kernels for 10%

profile of v2, /device:TPU:0, one launch (start us, length us, event | category | flops | bytes accessed | tf_op | source)
XLA Modules:
  0.0 108.9 jit_solution(12354194973075214575)
XLA Ops:
  5.0 3.1 %collective-permute-start = (bf16[72,3072]{1,0:T(8,128)(2,1)S(1)}, bf16[72,3072]{1,0:T(8,128)(2,1)S(1)}, u32[]{:S(2)}, u32[]{:S(2)}) collective-permute-start(bf16[72,3072]{1,0:T(8,128)(2,1)S(1)} %get-tuple-element.64.mine.refs_0_), channel_id=1, source_target_pairs={{0,4},{2,6},{4,0},{6,2},{8,12},{10,14},{12,8},{14,10},{1,5},{3,7},... | collective-permute-start | bytes 1327112 | tf_op jit(solution)/shard_map/ppermute | solution.py:232
  8.1 2.6 %collective-permute-start.4 = (bf16[72,3072]{1,0:T(8,128)(2,1)S(1)}, bf16[72,3072]{1,0:T(8,128)(2,1)S(1)}, u32[]{:S(2)}, u32[]{:S(2)}) collective-permute-start(bf16[72,3072]{1,0:T(8,128)(2,1)S(1)} %get-tuple-element.64.mine.refs_0_), channel_id=1, source_target_pairs={{0,8},{2,10},{4,12},{6,14},{8,0},{10,2},{12,4},{14,6},{1,9},{3,11}... | collective-permute-start | bytes 1327112 | tf_op jit(solution)/shard_map/ppermute | solution.py:232
  10.7 1.5 %collective-permute-start.1 = (bf16[72,3072]{1,0:T(8,128)(2,1)S(1)}, bf16[72,3072]{1,0:T(8,128)(2,1)S(1)}, u32[]{:S(2)}, u32[]{:S(2)}) collective-permute-start(bf16[72,3072]{1,0:T(8,128)(2,1)S(1)} %get-tuple-element.64.mine.refs_0_), channel_id=1, source_target_pairs={{0,2},{2,0},{4,6},{6,4},{8,10},{10,8},{12,14},{14,12},{1,3},{3,1},... | collective-permute-start | bytes 1327112 | tf_op jit(solution)/shard_map/ppermute | solution.py:229
  12.2 15.4 %collective-permute-done.mine.refs_2_ = bf16[72,3072]{1,0:T(8,128)(2,1)S(1)} collective-permute-done((bf16[72,3072]{1,0:T(8,128)(2,1)S(1)}, bf16[72,3072]{1,0:T(8,128)(2,1)S(1)}, u32[]{:S(2)}, u32[]{:S(2)}) %collective-permute-start) | collective-permute-done | bytes 442400 | tf_op jit(solution)/shard_map/ppermute | solution.py:232
  27.7 1.7 %collective-permute-start.5 = (bf16[72,3072]{1,0:T(8,128)(2,1)S(1)}, bf16[72,3072]{1,0:T(8,128)(2,1)S(1)}, u32[]{:S(2)}, u32[]{:S(2)}) collective-permute-start(bf16[72,3072]{1,0:T(8,128)(2,1)S(1)} %collective-permute-done.mine.refs_2_), channel_id=1, source_target_pairs={{0,2},{2,0},{4,6},{6,4},{8,10},{10,8},{12,14},{14,12},{1,3},{3,1},... | collective-permute-start | bytes 1327112 | tf_op jit(solution)/shard_map/ppermute | solution.py:229
  29.4 2.5 %collective-permute-start.13 = (bf16[72,3072]{1,0:T(8,128)(2,1)S(1)}, bf16[72,3072]{1,0:T(8,128)(2,1)S(1)}, u32[]{:S(2)}, u32[]{:S(2)}) collective-permute-start(bf16[72,3072]{1,0:T(8,128)(2,1)S(1)} %get-tuple-element.64.mine.refs_0_), channel_id=1, source_target_pairs={{0,12},{2,14},{4,8},{6,10},{8,4},{10,6},{12,0},{14,2},{1,13},{3,15... | collective-permute-start | bytes 1327112 | tf_op jit(solution)/shard_map/ppermute | solution.py:232
  32.3 1.4 %copy-done.1 = bf16[3072,256]{1,0:T(8,128)(2,1)S(1)} copy-done((bf16[3072,256]{1,0:T(8,128)(2,1)S(1)}, bf16[3072,256]{1,0:T(8,128)(2,1)}, u32[]{:S(2)}) %copy-start.1) | copy-done | bytes 1572888
  33.8 1.4 %copy-done.3 = bf16[256,3072]{1,0:T(8,128)(2,1)S(1)} copy-done((bf16[256,3072]{1,0:T(8,128)(2,1)S(1)}, bf16[256,3072]{1,0:T(8,128)(2,1)}, u32[]{:S(2)}) %copy-start.3) | copy-done | bytes 1572888
  36.4 1.3 %collective-permute-done.2.arrived = bf16[80,768]{1,0:T(8,128)(2,1)S(1)} collective-permute-done((bf16[80,768]{1,0:T(8,128)(2,1)S(1)}, bf16[80,768]{1,0:T(8,128)(2,1)S(1)}, u32[]{:S(2)}, u32[]{:S(2)}) %collective-permute-start.2) | collective-permute-done | bytes 122912 | tf_op jit(solution)/shard_map/ppermute | solution.py:251
  38.8 1.6 %collective-permute-start.3 = (bf16[40,3072]{1,0:T(8,128)(2,1)S(1)}, bf16[40,3072]{1,0:T(8,128)(2,1)S(1)}, u32[]{:S(2)}, u32[]{:S(2)}) collective-permute-start(bf16[40,3072]{1,0:T(8,128)(2,1)S(1)} %get-tuple-element.48), channel_id=1, source_target_pairs={{0,2},{2,0},{4,6},{6,4},{8,10},{10,8},{12,14},{14,12},{1,3},{3,1},... | collective-permute-start | bytes 737288 | tf_op jit(solution)/shard_map/ppermute | solution.py:229
  42.0 1.3 %collective-permute-done.6.arrived = bf16[80,768]{1,0:T(8,128)(2,1)S(1)} collective-permute-done((bf16[80,768]{1,0:T(8,128)(2,1)S(1)}, bf16[80,768]{1,0:T(8,128)(2,1)S(1)}, u32[]{:S(2)}, u32[]{:S(2)}) %collective-permute-start.6) | collective-permute-done | bytes 122912 | tf_op jit(solution)/shard_map/ppermute | solution.py:251
  44.4 1.7 %collective-permute-start.7 = (bf16[40,3072]{1,0:T(8,128)(2,1)S(1)}, bf16[40,3072]{1,0:T(8,128)(2,1)S(1)}, u32[]{:S(2)}, u32[]{:S(2)}) collective-permute-start(bf16[40,3072]{1,0:T(8,128)(2,1)S(1)} %get-tuple-element.53), channel_id=1, source_target_pairs={{0,2},{2,0},{4,6},{6,4},{8,10},{10,8},{12,14},{14,12},{1,3},{3,1},... | collective-permute-start | bytes 737288 | tf_op jit(solution)/shard_map/ppermute | solution.py:229
  46.5 9.0 %collective-permute-done.3.arrived = bf16[40,3072]{1,0:T(8,128)(2,1)S(1)} collective-permute-done((bf16[40,3072]{1,0:T(8,128)(2,1)S(1)}, bf16[40,3072]{1,0:T(8,128)(2,1)S(1)}, u32[]{:S(2)}, u32[]{:S(2)}) %collective-permute-start.3) | collective-permute-done | bytes 245792 | tf_op jit(solution)/shard_map/ppermute | solution.py:229
  56.8 1.3 %collective-permute-done.10.arrived = bf16[80,768]{1,0:T(8,128)(2,1)S(1)} collective-permute-done((bf16[80,768]{1,0:T(8,128)(2,1)S(1)}, bf16[80,768]{1,0:T(8,128)(2,1)S(1)}, u32[]{:S(2)}, u32[]{:S(2)}) %collective-permute-start.10) | collective-permute-done | bytes 122912 | tf_op jit(solution)/shard_map/ppermute | solution.py:251
  59.2 1.8 %collective-permute-start.11 = (bf16[40,3072]{1,0:T(8,128)(2,1)S(1)}, bf16[40,3072]{1,0:T(8,128)(2,1)S(1)}, u32[]{:S(2)}, u32[]{:S(2)}) collective-permute-start(bf16[40,3072]{1,0:T(8,128)(2,1)S(1)} %get-tuple-element.58), channel_id=1, source_target_pairs={{0,2},{2,0},{4,6},{6,4},{8,10},{10,8},{12,14},{14,12},{1,3},{3,1},... | collective-permute-start | bytes 737288 | tf_op jit(solution)/shard_map/ppermute | solution.py:229
  61.1 12.7 %collective-permute-done.11.arrived = bf16[40,3072]{1,0:T(8,128)(2,1)S(1)} collective-permute-done((bf16[40,3072]{1,0:T(8,128)(2,1)S(1)}, bf16[40,3072]{1,0:T(8,128)(2,1)S(1)}, u32[]{:S(2)}, u32[]{:S(2)}) %collective-permute-start.11) | collective-permute-done | bytes 245792 | tf_op jit(solution)/shard_map/ppermute | solution.py:229
  75.1 1.3 %collective-permute-done.15.arrived = bf16[80,768]{1,0:T(8,128)(2,1)S(1)} collective-permute-done((bf16[80,768]{1,0:T(8,128)(2,1)S(1)}, bf16[80,768]{1,0:T(8,128)(2,1)S(1)}, u32[]{:S(2)}, u32[]{:S(2)}) %collective-permute-start.15) | collective-permute-done | bytes 122912 | tf_op jit(solution)/shard_map/ppermute | solution.py:251
  77.5 1.4 %collective-permute-start.16 = (bf16[40,3072]{1,0:T(8,128)(2,1)S(1)}, bf16[40,3072]{1,0:T(8,128)(2,1)S(1)}, u32[]{:S(2)}, u32[]{:S(2)}) collective-permute-start(bf16[40,3072]{1,0:T(8,128)(2,1)S(1)} %get-tuple-element.63), channel_id=1, source_target_pairs={{0,2},{2,0},{4,6},{6,4},{8,10},{10,8},{12,14},{14,12},{1,3},{3,1},... | collective-permute-start | bytes 737288 | tf_op jit(solution)/shard_map/ppermute | solution.py:229
  78.9 6.6 %collective-permute-done.16.arrived = bf16[40,3072]{1,0:T(8,128)(2,1)S(1)} collective-permute-done((bf16[40,3072]{1,0:T(8,128)(2,1)S(1)}, bf16[40,3072]{1,0:T(8,128)(2,1)S(1)}, u32[]{:S(2)}, u32[]{:S(2)}) %collective-permute-start.16) | collective-permute-done | bytes 245792 | tf_op jit(solution)/shard_map/ppermute | solution.py:229
  85.6 2.4 %collective-permute-start.17 = (bf16[40,3072]{1,0:T(8,128)(2,1)S(1)}, bf16[40,3072]{1,0:T(8,128)(2,1)S(1)}, u32[]{:S(2)}, u32[]{:S(2)}) collective-permute-start(bf16[40,3072]{1,0:T(8,128)(2,1)S(1)} %add.7), channel_id=1, source_target_pairs={{0,12},{2,14},{4,8},{6,10},{8,4},{10,6},{12,0},{14,2},{1,13},{3,15... | collective-permute-start | bytes 737288 | tf_op jit(solution)/shard_map/ppermute | solution.py:232
  88.0 4.6 %grads.1 = (bf16[3072,256]{1,0:T(8,128)(2,1)}, bf16[3072,256]{1,0:T(8,128)(2,1)}, bf16[256,3072]{1,0:T(8,128)(2,1)}) custom-call(bf16[72,3072]{1,0:T(8,128)(2,1)S(1)} %get-tuple-element.64.mine.refs_0_, bf16[72,3072]{1,0:T(8,128)(2,1)S(1)} %collective-permute-done.1.other.refs_1_, bf16[72,3072]{1,0:T(8,128)(2,1)S(1)} %collective-permute-done.mine.refs_2_, ...), custom_call_target="tpu_custom_call" | custom-call | flops 1000 | bytes 1000 | tf_op jit(solution)/shard_map/grads/pallas_call | solution.py:101
  92.6 3.9 %collective-permute-done.17.fourth = bf16[40,3072]{1,0:T(8,128)(2,1)S(1)} collective-permute-done((bf16[40,3072]{1,0:T(8,128)(2,1)S(1)}, bf16[40,3072]{1,0:T(8,128)(2,1)S(1)}, u32[]{:S(2)}, u32[]{:S(2)}) %collective-permute-start.17) | collective-permute-done | bytes 245792 | tf_op jit(solution)/shard_map/ppermute | solution.py:232
  96.4 11.2 %collective-permute-done.12.third = bf16[40,3072]{1,0:T(8,128)(2,1)S(1)} collective-permute-done((bf16[40,3072]{1,0:T(8,128)(2,1)S(1)}, bf16[40,3072]{1,0:T(8,128)(2,1)S(1)}, u32[]{:S(2)}, u32[]{:S(2)}) %collective-permute-start.12) | collective-permute-done | bytes 245792 | tf_op jit(solution)/shard_map/ppermute | solution.py:232
  107.6 1.2 %finish.1 = bf16[128,3072]{1,0:T(8,128)(2,1)} custom-call(bf16[128,128]{1,0:T(8,128)(2,1)S(1)} %get-tuple-element.42.placing_t, bf16[40,3072]{1,0:T(8,128)(2,1)S(1)} %add.4.first, bf16[40,3072]{1,0:T(8,128)(2,1)S(1)} %collective-permute-done.8.second, bf16[40,3072]{1,0:T(8,128)(2,1)S(1)} %collective-permute-done.12.third, ...), custom_call_target="tpu_custom_call" | custom-call | flops 1000 | bytes 1000 | tf_op jit(solution)/shard_map/finish/pallas_call | solution.py:101
  (43 shorter events, 15.1 us)
Async XLA Ops:
  0.6 31.7 %copy-start = (bf16[3072,256]{1,0:T(8,128)(2,1)S(1)}, bf16[3072,256]{1,0:T(8,128)(2,1)}, u32[]{:S(2)}) copy-start(bf16[3072,256]{1,0:T(8,128)(2,1)} %w_gate.15) | copy-start | bytes 4718596
  2.3 1.1 %copy-start.5 = (bf16[128,3072]{1,0:T(8,128)(2,1)S(1)}, bf16[128,3072]{1,0:T(8,128)(2,1)}, u32[]{:S(2)}) copy-start(bf16[128,3072]{1,0:T(8,128)(2,1)} %tokens.1) | copy-start | bytes 2359300
  5.0 22.6 %collective-permute-start = (bf16[72,3072]{1,0:T(8,128)(2,1)S(1)}, bf16[72,3072]{1,0:T(8,128)(2,1)S(1)}, u32[]{:S(2)}, u32[]{:S(2)}) collective-permute-start(bf16[72,3072]{1,0:T(8,128)(2,1)S(1)} %get-tuple-element.64.mine.refs_0_), channel_id=1, source_target_pairs={{0,4},{2,6},{4,0},{6,2},{8,12},{10,14},{12,8},{14,10},{1,5},{3,7},... | collective-permute-start | bytes 1327112 | tf_op jit(solution)/shard_map/ppermute | solution.py:232
  8.1 23.7 %collective-permute-start.4 = (bf16[72,3072]{1,0:T(8,128)(2,1)S(1)}, bf16[72,3072]{1,0:T(8,128)(2,1)S(1)}, u32[]{:S(2)}, u32[]{:S(2)}) collective-permute-start(bf16[72,3072]{1,0:T(8,128)(2,1)S(1)} %get-tuple-element.64.mine.refs_0_), channel_id=1, source_target_pairs={{0,8},{2,10},{4,12},{6,14},{8,0},{10,2},{12,4},{14,6},{1,9},{3,11}... | collective-permute-start | bytes 1327112 | tf_op jit(solution)/shard_map/ppermute | solution.py:232
  10.7 21.6 %collective-permute-start.1 = (bf16[72,3072]{1,0:T(8,128)(2,1)S(1)}, bf16[72,3072]{1,0:T(8,128)(2,1)S(1)}, u32[]{:S(2)}, u32[]{:S(2)}) collective-permute-start(bf16[72,3072]{1,0:T(8,128)(2,1)S(1)} %get-tuple-element.64.mine.refs_0_), channel_id=1, source_target_pairs={{0,2},{2,0},{4,6},{6,4},{8,10},{10,8},{12,14},{14,12},{1,3},{3,1},... | collective-permute-start | bytes 1327112 | tf_op jit(solution)/shard_map/ppermute | solution.py:229
  27.7 13.1 %collective-permute-start.5 = (bf16[72,3072]{1,0:T(8,128)(2,1)S(1)}, bf16[72,3072]{1,0:T(8,128)(2,1)S(1)}, u32[]{:S(2)}, u32[]{:S(2)}) collective-permute-start(bf16[72,3072]{1,0:T(8,128)(2,1)S(1)} %collective-permute-done.mine.refs_2_), channel_id=1, source_target_pairs={{0,2},{2,0},{4,6},{6,4},{8,10},{10,8},{12,14},{14,12},{1,3},{3,1},... | collective-permute-start | bytes 1327112 | tf_op jit(solution)/shard_map/ppermute | solution.py:229
  29.4 16.8 %collective-permute-start.13 = (bf16[72,3072]{1,0:T(8,128)(2,1)S(1)}, bf16[72,3072]{1,0:T(8,128)(2,1)S(1)}, u32[]{:S(2)}, u32[]{:S(2)}) collective-permute-start(bf16[72,3072]{1,0:T(8,128)(2,1)S(1)} %get-tuple-element.64.mine.refs_0_), channel_id=1, source_target_pairs={{0,12},{2,14},{4,8},{6,10},{8,4},{10,6},{12,0},{14,2},{1,13},{3,15... | collective-permute-start | bytes 1327112 | tf_op jit(solution)/shard_map/ppermute | solution.py:232
  31.8 23.7 %collective-permute-start.9 = (bf16[72,3072]{1,0:T(8,128)(2,1)S(1)}, bf16[72,3072]{1,0:T(8,128)(2,1)S(1)}, u32[]{:S(2)}, u32[]{:S(2)}) collective-permute-start(bf16[72,3072]{1,0:T(8,128)(2,1)S(1)} %collective-permute-done.4.mine.refs_4_), channel_id=1, source_target_pairs={{0,2},{2,0},{4,6},{6,4},{8,10},{10,8},{12,14},{14,12},{1,3},{3,1},... | collective-permute-start | bytes 1327112 | tf_op jit(solution)/shard_map/ppermute | solution.py:229
  32.3 1.4 %copy-start.1 = (bf16[3072,256]{1,0:T(8,128)(2,1)S(1)}, bf16[3072,256]{1,0:T(8,128)(2,1)}, u32[]{:S(2)}) copy-start(bf16[3072,256]{1,0:T(8,128)(2,1)} %w_up.15) | copy-start | bytes 4718596
  33.8 1.4 %copy-start.3 = (bf16[256,3072]{1,0:T(8,128)(2,1)S(1)}, bf16[256,3072]{1,0:T(8,128)(2,1)}, u32[]{:S(2)}) copy-start(bf16[256,3072]{1,0:T(8,128)(2,1)} %w_down.7) | copy-start | bytes 4718596
  36.3 1.4 %collective-permute-start.2 = (bf16[80,768]{1,0:T(8,128)(2,1)S(1)}, bf16[80,768]{1,0:T(8,128)(2,1)S(1)}, u32[]{:S(2)}, u32[]{:S(2)}) collective-permute-start(bf16[80,768]{1,0:T(8,128)(2,1)S(1)} %get-tuple-element.46), channel_id=1, source_target_pairs={{0,1},{1,0},{2,3},{3,2},{4,5},{5,4},{6,7},{7,6},{8,9},{9,8},{10,11... | collective-permute-start | bytes 368648 | tf_op jit(solution)/shard_map/ppermute | solution.py:251
  37.7 3.0 %copy-start.4 = (bf16[256,3072]{1,0:T(8,128)(2,1)S(1)}, bf16[256,3072]{1,0:T(8,128)(2,1)}, u32[]{:S(2)}) copy-start(bf16[256,3072]{1,0:T(8,128)(2,1)} %w_down.7) | copy-start | bytes 4718596
  38.8 16.7 %collective-permute-start.3 = (bf16[40,3072]{1,0:T(8,128)(2,1)S(1)}, bf16[40,3072]{1,0:T(8,128)(2,1)S(1)}, u32[]{:S(2)}, u32[]{:S(2)}) collective-permute-start(bf16[40,3072]{1,0:T(8,128)(2,1)S(1)} %get-tuple-element.48), channel_id=1, source_target_pairs={{0,2},{2,0},{4,6},{6,4},{8,10},{10,8},{12,14},{14,12},{1,3},{3,1},... | collective-permute-start | bytes 737288 | tf_op jit(solution)/shard_map/ppermute | solution.py:229
  41.9 1.4 %collective-permute-start.6 = (bf16[80,768]{1,0:T(8,128)(2,1)S(1)}, bf16[80,768]{1,0:T(8,128)(2,1)S(1)}, u32[]{:S(2)}, u32[]{:S(2)}) collective-permute-start(bf16[80,768]{1,0:T(8,128)(2,1)S(1)} %get-tuple-element.51), channel_id=1, source_target_pairs={{0,1},{1,0},{2,3},{3,2},{4,5},{5,4},{6,7},{7,6},{8,9},{9,8},{10,11... | collective-permute-start | bytes 368648 | tf_op jit(solution)/shard_map/ppermute | solution.py:251
  43.3 12.2 %copy-start.2 = (bf16[3072,256]{1,0:T(8,128)(2,1)S(1)}, bf16[3072,256]{1,0:T(8,128)(2,1)}, u32[]{:S(2)}) copy-start(bf16[3072,256]{1,0:T(8,128)(2,1)} %w_up.15) | copy-start | bytes 4718596
  44.4 16.6 %collective-permute-start.7 = (bf16[40,3072]{1,0:T(8,128)(2,1)S(1)}, bf16[40,3072]{1,0:T(8,128)(2,1)S(1)}, u32[]{:S(2)}, u32[]{:S(2)}) collective-permute-start(bf16[40,3072]{1,0:T(8,128)(2,1)S(1)} %get-tuple-element.53), channel_id=1, source_target_pairs={{0,2},{2,0},{4,6},{6,4},{8,10},{10,8},{12,14},{14,12},{1,3},{3,1},... | collective-permute-start | bytes 737288 | tf_op jit(solution)/shard_map/ppermute | solution.py:229
  46.2 27.7 %collective-permute-start.14 = (bf16[72,3072]{1,0:T(8,128)(2,1)S(1)}, bf16[72,3072]{1,0:T(8,128)(2,1)S(1)}, u32[]{:S(2)}, u32[]{:S(2)}) collective-permute-start(bf16[72,3072]{1,0:T(8,128)(2,1)S(1)} %collective-permute-done.13.mine.refs_6_), channel_id=1, source_target_pairs={{0,2},{2,0},{4,6},{6,4},{8,10},{10,8},{12,14},{14,12},{1,3},{3,1},... | collective-permute-start | bytes 1327112 | tf_op jit(solution)/shard_map/ppermute | solution.py:229
  56.7 1.4 %collective-permute-start.10 = (bf16[80,768]{1,0:T(8,128)(2,1)S(1)}, bf16[80,768]{1,0:T(8,128)(2,1)S(1)}, u32[]{:S(2)}, u32[]{:S(2)}) collective-permute-start(bf16[80,768]{1,0:T(8,128)(2,1)S(1)} %get-tuple-element.56), channel_id=1, source_target_pairs={{0,1},{1,0},{2,3},{3,2},{4,5},{5,4},{6,7},{7,6},{8,9},{9,8},{10,11... | collective-permute-start | bytes 368648 | tf_op jit(solution)/shard_map/ppermute | solution.py:251
  59.2 14.6 %collective-permute-start.11 = (bf16[40,3072]{1,0:T(8,128)(2,1)S(1)}, bf16[40,3072]{1,0:T(8,128)(2,1)S(1)}, u32[]{:S(2)}, u32[]{:S(2)}) collective-permute-start(bf16[40,3072]{1,0:T(8,128)(2,1)S(1)} %get-tuple-element.58), channel_id=1, source_target_pairs={{0,2},{2,0},{4,6},{6,4},{8,10},{10,8},{12,14},{14,12},{1,3},{3,1},... | collective-permute-start | bytes 737288 | tf_op jit(solution)/shard_map/ppermute | solution.py:229
  61.0 12.8 %collective-permute-start.8 = (bf16[40,3072]{1,0:T(8,128)(2,1)S(1)}, bf16[40,3072]{1,0:T(8,128)(2,1)S(1)}, u32[]{:S(2)}, u32[]{:S(2)}) collective-permute-start(bf16[40,3072]{1,0:T(8,128)(2,1)S(1)} %add.5), channel_id=1, source_target_pairs={{0,4},{2,6},{4,0},{6,2},{8,12},{10,14},{12,8},{14,10},{1,5},{3,7},... | collective-permute-start | bytes 737288 | tf_op jit(solution)/shard_map/ppermute | solution.py:232
  75.0 1.4 %collective-permute-start.15 = (bf16[80,768]{1,0:T(8,128)(2,1)S(1)}, bf16[80,768]{1,0:T(8,128)(2,1)S(1)}, u32[]{:S(2)}, u32[]{:S(2)}) collective-permute-start(bf16[80,768]{1,0:T(8,128)(2,1)S(1)} %get-tuple-element.61), channel_id=1, source_target_pairs={{0,1},{1,0},{2,3},{3,2},{4,5},{5,4},{6,7},{7,6},{8,9},{9,8},{10,11... | collective-permute-start | bytes 368648 | tf_op jit(solution)/shard_map/ppermute | solution.py:251
  77.5 8.1 %collective-permute-start.16 = (bf16[40,3072]{1,0:T(8,128)(2,1)S(1)}, bf16[40,3072]{1,0:T(8,128)(2,1)S(1)}, u32[]{:S(2)}, u32[]{:S(2)}) collective-permute-start(bf16[40,3072]{1,0:T(8,128)(2,1)S(1)} %get-tuple-element.63), channel_id=1, source_target_pairs={{0,2},{2,0},{4,6},{6,4},{8,10},{10,8},{12,14},{14,12},{1,3},{3,1},... | collective-permute-start | bytes 737288 | tf_op jit(solution)/shard_map/ppermute | solution.py:229
  85.6 10.8 %collective-permute-start.17 = (bf16[40,3072]{1,0:T(8,128)(2,1)S(1)}, bf16[40,3072]{1,0:T(8,128)(2,1)S(1)}, u32[]{:S(2)}, u32[]{:S(2)}) collective-permute-start(bf16[40,3072]{1,0:T(8,128)(2,1)S(1)} %add.7), channel_id=1, source_target_pairs={{0,12},{2,14},{4,8},{6,10},{8,4},{10,6},{12,0},{14,2},{1,13},{3,15... | collective-permute-start | bytes 737288 | tf_op jit(solution)/shard_map/ppermute | solution.py:232
  88.0 19.6 %collective-permute-start.12 = (bf16[40,3072]{1,0:T(8,128)(2,1)S(1)}, bf16[40,3072]{1,0:T(8,128)(2,1)S(1)}, u32[]{:S(2)}, u32[]{:S(2)}) collective-permute-start(bf16[40,3072]{1,0:T(8,128)(2,1)S(1)} %add.6), channel_id=1, source_target_pairs={{0,8},{2,10},{4,12},{6,14},{8,0},{10,2},{12,4},{14,6},{1,9},{3,11}... | collective-permute-start | bytes 737288 | tf_op jit(solution)/shard_map/ppermute | solution.py:232
  (1 other events, 1.1 us)

commit v3 on v2

--- a/solution.py
+++ b/solution.py
@@ -114,16 +114,23 @@
     )
 
 
-def place_kernel(tokens, grad_out, ids, probs, block, placing_t):
+def place_kernel(
+    tokens_at, grad_out_at, ids_at, probs_at, block, placing_t, tokens, grad_out, ids, probs, done
+):
+    pairs = ((ids_at, ids), (probs_at, probs), (tokens_at, tokens), (grad_out_at, grad_out))
+    copies = [pltpu.make_async_copy(a, b, done.at[i]) for i, (a, b) in enumerate(pairs)]
+    for copy in copies:
+        copy.start()
     rows = tokens.shape[0]
+    copies[0].wait()
+    copies[1].wait()
     chosen = ids[...] == window_expert
-    weight = jnp.sum(jnp.where(chosen, probs[...], 0.0), axis=1, keepdims=True)
-    routed = jnp.max(chosen.astype(F32), axis=1, keepdims=True)
+    weight_row = jnp.sum(jnp.where(chosen, probs[...], 0.0), axis=0, keepdims=True)
+    routed_row = jnp.max(chosen.astype(F32), axis=0, keepdims=True)
     at_row = lax.broadcasted_iota(jnp.int32, (rows, rows), 0)
     at_column = lax.broadcasted_iota(jnp.int32, (rows, rows), 1)
     same = at_row == at_column
-    routed_row = jnp.sum(jnp.where(same, routed, 0.0), axis=0, keepdims=True)
-    weight_row = jnp.sum(jnp.where(same, weight, 0.0), axis=0, keepdims=True)
+    routed = jnp.sum(jnp.where(same, routed_row, 0.0), axis=1, keepdims=True)
     slot_row = jnp.sum(jnp.where(at_row <= at_column, routed, 0.0), axis=0, keepdims=True) - 1.0
     slot = jnp.sum(jnp.where(at_column <= at_row, routed_row, 0.0), axis=1, keepdims=True) - 1.0
     wanted = lax.broadcasted_iota(jnp.int32, (TERM, rows), 0).astype(F32)
@@ -132,7 +139,9 @@
     placing_t[...] = jnp.where((slot == wanted) & (routed > 0.0), 1.0, 0.0).astype(BF16)
     scale = jnp.sum(placing * weight_row, axis=1, keepdims=True)
     placing = placing.astype(BF16)
+    copies[2].wait()
     x = mul(placing, tokens[...])
+    copies[3].wait()
     dy = mul(placing, grad_out[...]) * scale
     block[0:MAIN, :] = x[0:MAIN].astype(BF16)
     block[MAIN : 2 * MAIN, :] = dy[0:MAIN].astype(BF16)
@@ -165,6 +174,11 @@
     ):
         part[:, at * width : (at + 1) * width] = value
         sent[:, at * width : (at + 1) * width] = value.astype(BF16)
+
+
+def folded(main, last):
+    half = main.shape[1] // 2
+    return jnp.concatenate([main[:, :half], last[:, :half], main[:, half:], last[:, half:]], axis=0)
 
 
 def back_kernel(part, arrived, w_gate, w_up, hidden, d_pre, term, sent):
@@ -182,10 +196,8 @@
     d_pre[:, :width] = d_gate
     d_pre[:, width:] = d_up
     value = mul(d_gate, w_gate[...], 1, 1) + mul(d_up, w_up[...], 1, 1)
-    term[0:MAIN, :] = value[0:MAIN]
-    term[MAIN:TERM, :] = value[2 * MAIN : 2 * MAIN + 8]
-    sent[0:MAIN, :] = value[MAIN : 2 * MAIN].astype(BF16)
-    sent[MAIN:TERM, :] = value[2 * MAIN + 8 : GROUP].astype(BF16)
+    term[...] = folded(value[0:MAIN], value[2 * MAIN : 2 * MAIN + TAIL])
+    sent[...] = folded(value[MAIN : 2 * MAIN], value[2 * MAIN + 8 : 2 * MAIN + 8 + TAIL]).astype(BF16)
 
 
 def add_kernel(term, arrived, total):
@@ -195,7 +207,10 @@
 def finish_kernel(placing_t, first, second, third, fourth, grad_in):
     total = first[...].astype(F32) + second[...].astype(F32)
     total = total + third[...].astype(F32) + fourth[...].astype(F32)
-    grad_in[...] = mul(placing_t[:, :TERM], total.astype(BF16)).astype(BF16)
+    half = total.shape[1]
+    placing = placing_t[:, :CAP]
+    grad_in[:, :half] = mul(placing, total[:CAP].astype(BF16)).astype(BF16)
+    grad_in[:, half:] = mul(placing, total[CAP:].astype(BF16)).astype(BF16)
 
 
 def grads_kernel(*refs):
@@ -239,7 +254,15 @@
     own, placing_t = call(
         place_kernel,
         (struct(BLOCK, features, BF16), struct(tokens.shape[0], tokens.shape[0], BF16)),
-        tokens, grad_out, expert_ids, gate_probs, name="place",
+        tokens, grad_out, expert_ids.T, gate_probs.T, name="place",
+        in_specs=[pl.BlockSpec(memory_space=pltpu.HBM)] * 4,
+        scratch_shapes=[
+            pltpu.VMEM(tokens.shape, BF16),
+            pltpu.VMEM(tokens.shape, BF16),
+            pltpu.VMEM(expert_ids.shape[::-1], jnp.int32),
+            pltpu.VMEM(gate_probs.shape[::-1], F32),
+            pltpu.SemaphoreType.DMA((4,)),
+        ],
     )
 
     def front(mine, other):
@@ -256,26 +279,36 @@
             (
                 struct(GROUP, width, BF16),
                 struct(GROUP, 2 * width, BF16),
-                struct(TERM, features, F32),
-                struct(TERM, features, BF16),
+                struct(BLOCK, features // 2, F32),
+                struct(BLOCK, features // 2, BF16),
             ),
             part, arrived, gate, up, name="back",
         )
-        total = call(add_kernel, struct(TERM, features, BF16), term, across(sent), name="add")
-        return hidden, d_pre, total
-
+        return hidden, d_pre, term, sent
+
+    def add(term, sent):
+        return call(add_kernel, struct(BLOCK, features // 2, BF16), term, across(sent), name="add")
+
+    own_y = across(own)
     two = along(own, 2)
     one = along(own, 1)
-    own_y = across(own)
-    three = along(after(own, one), 3)
-    one_y, two_y, three_y = across(one), across(two), across(three)
-
-    h0, d0, q0 = back(*front(after(own, one), own_y))
-    h1, d1, q1 = back(*front(after(one, two), one_y))
+    h0, d0, t0, s0 = back(*front(own, own_y))
+    two, one, s0 = lax.optimization_barrier((two, one, s0))
+    middle = lax.ppermute(after(own, two), "expert", [(2, 4), (3, 5), (4, 2), (5, 3)])
+    ends = lax.ppermute(two, "expert", [(4, 6), (5, 7), (2, 0), (3, 1)])
+    two_y = across(two)
+    q0 = add(t0, s0)
+    three = after(middle + ends, q0)
+    three_y = across(three)
+    one_y = along(after(own_y, three), 1)
+    h2, d2, t2, s2 = back(*front(after(two, three), two_y))
+    q2 = add(t2, s2)
+    r2 = along(q2, 2)
+    h1, d1, t1, s1 = back(*front(one, one_y))
+    q1 = add(t1, s1)
     r1 = along(q1, 1)
-    h2, d2, q2 = back(*front(after(two, q0), two_y))
-    r2 = along(q2, 2)
-    h3, d3, q3 = back(*front(after(three, q2, r1), three_y))
+    h3, d3, t3, s3 = back(*front(after(three, q2, s1), three_y))
+    q3 = add(after(t3, r2), s3)
     r3 = along(q3, 3)
 
     tile = features // 4
@@ -285,7 +318,7 @@
     grads = call(
         grads_kernel,
         (struct(features, width, BF16), struct(features, width, BF16), struct(width, features, BF16)),
-        after(own, q3), own_y, one, one_y, two, two_y, three, three_y, h0, h1, h2, h3, d0, d1, d2, d3,
+        after(own, q3, r1), own_y, one, one_y, two, two_y, three, three_y, h0, h1, h2, h3, d0, d1, d2, d3,
         name="grads",
         grid=(features // tile,),
         in_specs=[column] * 8 + whole,

time: 109 us -> 95.4 us (0.88)
  waiting for transfers between devices: 64.5 us -> 45.4 us
  starting transfers between devices: 21.5 us -> 26.5 us
    ppermute x6, waiting for transfers between devices: 30.5 us -> 18.9 us  [along(): lax.ppermute(value, 'expert', [(i, i ^ 2 * distance) for i in range(8)])]
    ppermute x8 -> x7, waiting for transfers between devices: 28.7 us -> 21.6 us  [across(): return lax.ppermute(value, 'expert', [(i, i ^ 1) for i in range(8)])]
    ppermute x6, starting transfers between devices: 10.6 us -> 15.4 us  [along(): lax.ppermute(value, 'expert', [(i, i ^ 2 * distance) for i in range(8)])]
    ppermute x4, waiting for transfers between devices: 5.29 us -> 2.65 us  [front(): return (part, lax.ppermute(sent, 'tensor', [(0, 1), (1, 0)]))]
    ppermute x0 -> x2, waiting for transfers between devices: none -> 2.26 us  [the longest x1 2.26 us: four_by_two(): ends = lax.ppermute(two, 'expert', [(4, 6), (5, 7), (2, 0), (3, 1)])]
    ppermute x0 -> x2, starting transfers between devices: none -> 1.97 us  [the longest x1 1.29 us: four_by_two(): ends = lax.ppermute(two, 'expert', [(4, 6), (5, 7), (2, 0), (3, 1)])]
    ppermute x8 -> x7, starting transfers between devices: 10.6 us -> 8.86 us  [across(): return lax.ppermute(value, 'expert', [(i, i ^ 1) for i in range(8)])]
  transfers between devices with their start and end apart: 18 -> 19, of which waited for: 11 -> 12; matrix products, arithmetic and copies ran while one was open for 0% -> 0% of each run, Pallas kernels for 10% -> 13%
where the time goes in v3:
time: 95.4 us; the launch traced here: 95.1 us
  waiting for transfers between devices  45.4 us (48%)
  starting transfers between devices  26.5 us (28%)
  Pallas kernels  15.8 us (17%)
  local copies, waits for them, and re-layouts  6.56 us (7%)
    ppermute x7, waiting for transfers between devices, across(): return lax.ppermute(value, 'expert', [(i, i ^ 1) for i in range(8)])  21.6 us
    ppermute x6, waiting for transfers between devices, along(): lax.ppermute(value, 'expert', [(i, i ^ 2 * distance) for i in range(8)])  18.9 us
    pallas_call x15, Pallas kernels, call(): pl.pallas_call(kernel, out_shape=outs, name=name, compiler_params=pltpu.C...  15.8 us
    ppermute x6, starting transfers between devices, along(): lax.ppermute(value, 'expert', [(i, i ^ 2 * distance) for i in range(8)])  15.4 us
    ppermute x7, starting transfers between devices, across(): return lax.ppermute(value, 'expert', [(i, i ^ 1) for i in range(8)])  8.86 us
    unnamed x16, local copies, waits for them, and re-layouts  6.56 us
    ppermute x4, waiting for transfers between devices, front(): return (part, lax.ppermute(sent, 'tensor', [(0, 1), (1, 0)]))  2.65 us
    ppermute x1, waiting for transfers between devices, four_by_two(): ends = lax.ppermute(two, 'expert', [(4, 6), (5, 7), (2, 0), (3, 1)])  2.26 us
  transfers between devices with their start and end apart: 19, of which 12 were waited for; matrix products, arithmetic and copies ran while one was open for 0% of the time, Pallas kernels for 13%

profile of v3, /device:TPU:0, one launch (start us, length us, event | category | flops | bytes accessed | tf_op | source)
XLA Modules:
  0.0 95.1 jit_solution(12799789821675118447)
XLA Ops:
  5.2 3.0 %collective-permute-start = (bf16[72,3072]{1,0:T(8,128)(2,1)S(1)}, bf16[72,3072]{1,0:T(8,128)(2,1)S(1)}, u32[]{:S(2)}, u32[]{:S(2)}) collective-permute-start(bf16[72,3072]{1,0:T(8,128)(2,1)S(1)} %get-tuple-element.74.mine.refs_0_), channel_id=1, source_target_pairs={{0,2},{2,0},{4,6},{6,4},{8,10},{10,8},{12,14},{14,12},{1,3},{3,1},... | collective-permute-start | bytes 1327112 | tf_op jit(solution)/shard_map/ppermute | solution.py:244
  8.3 1.6 %collective-permute-start.3 = (bf16[72,3072]{1,0:T(8,128)(2,1)S(1)}, bf16[72,3072]{1,0:T(8,128)(2,1)S(1)}, u32[]{:S(2)}, u32[]{:S(2)}) collective-permute-start(bf16[72,3072]{1,0:T(8,128)(2,1)S(1)} %get-tuple-element.74.mine.refs_0_), channel_id=1, source_target_pairs={{0,4},{2,6},{4,0},{6,2},{8,12},{10,14},{12,8},{14,10},{1,5},{3,7},... | collective-permute-start | bytes 1327112 | tf_op jit(solution)/shard_map/ppermute | solution.py:247
  9.9 2.6 %collective-permute-start.2 = (bf16[72,3072]{1,0:T(8,128)(2,1)S(1)}, bf16[72,3072]{1,0:T(8,128)(2,1)S(1)}, u32[]{:S(2)}, u32[]{:S(2)}) collective-permute-start(bf16[72,3072]{1,0:T(8,128)(2,1)S(1)} %get-tuple-element.74.mine.refs_0_), channel_id=1, source_target_pairs={{0,8},{2,10},{4,12},{6,14},{8,0},{10,2},{12,4},{14,6},{1,9},{3,11}... | collective-permute-start | bytes 1327112 | tf_op jit(solution)/shard_map/ppermute | solution.py:247
  12.4 6.0 %collective-permute-done.other.refs_1_ = bf16[72,3072]{1,0:T(8,128)(2,1)S(1)} collective-permute-done((bf16[72,3072]{1,0:T(8,128)(2,1)S(1)}, bf16[72,3072]{1,0:T(8,128)(2,1)S(1)}, u32[]{:S(2)}, u32[]{:S(2)}) %collective-permute-start) | collective-permute-done | bytes 442400 | tf_op jit(solution)/shard_map/ppermute | solution.py:244
  18.5 1.4 %copy-done.1 = bf16[3072,256]{1,0:T(8,128)(2,1)S(1)} copy-done((bf16[3072,256]{1,0:T(8,128)(2,1)S(1)}, bf16[3072,256]{1,0:T(8,128)(2,1)}, u32[]{:S(2)}) %copy-start.1) | copy-done | bytes 1572888
  19.9 1.4 %copy-done.2 = bf16[256,3072]{1,0:T(8,128)(2,1)S(1)} copy-done((bf16[256,3072]{1,0:T(8,128)(2,1)S(1)}, bf16[256,3072]{1,0:T(8,128)(2,1)}, u32[]{:S(2)}) %copy-start.2) | copy-done | bytes 1572888
  22.5 1.3 %collective-permute-done.1.arrived = bf16[80,768]{1,0:T(8,128)(2,1)S(1)} collective-permute-done((bf16[80,768]{1,0:T(8,128)(2,1)S(1)}, bf16[80,768]{1,0:T(8,128)(2,1)S(1)}, u32[]{:S(2)}, u32[]{:S(2)}) %collective-permute-start.1) | collective-permute-done | bytes 122912 | tf_op jit(solution)/shard_map/ppermute | solution.py:274
  24.9 4.4 %collective-permute-done.3.mine.refs_2_ = bf16[72,3072]{1,0:T(8,128)(2,1)S(1)} collective-permute-done((bf16[72,3072]{1,0:T(8,128)(2,1)S(1)}, bf16[72,3072]{1,0:T(8,128)(2,1)S(1)}, u32[]{:S(2)}, u32[]{:S(2)}) %collective-permute-start.3) | collective-permute-done | bytes 442400 | tf_op jit(solution)/shard_map/ppermute | solution.py:247
  29.3 2.3 %collective-permute-done.2.mine.refs_4_ = bf16[72,3072]{1,0:T(8,128)(2,1)S(1)} collective-permute-done((bf16[72,3072]{1,0:T(8,128)(2,1)S(1)}, bf16[72,3072]{1,0:T(8,128)(2,1)S(1)}, u32[]{:S(2)}, u32[]{:S(2)}) %collective-permute-start.2) | collective-permute-done | bytes 442400 | tf_op jit(solution)/shard_map/ppermute | solution.py:247
  32.3 1.3 %collective-permute-start.6 = (bf16[72,3072]{1,0:T(8,128)(2,1)S(1)}, bf16[72,3072]{1,0:T(8,128)(2,1)S(1)}, u32[]{:S(2)}, u32[]{:S(2)}) collective-permute-start(bf16[72,3072]{1,0:T(8,128)(2,1)S(1)} %collective-permute-done.2.mine.refs_4_), channel_id=1, source_target_pairs={{8,12},{10,14},{4,0},{6,2},{9,13},{11,15},{5,1},{7,3},{24,28},{26,... | collective-permute-start | bytes 1327112 | tf_op jit(solution)/shard_map/ppermute | solution.py:298
  34.2 1.5 %collective-permute-start.11 = (bf16[72,3072]{1,0:T(8,128)(2,1)S(1)}, bf16[72,3072]{1,0:T(8,128)(2,1)S(1)}, u32[]{:S(2)}, u32[]{:S(2)}) collective-permute-start(bf16[72,3072]{1,0:T(8,128)(2,1)S(1)} %collective-permute-done.2.mine.refs_4_), channel_id=1, source_target_pairs={{0,2},{2,0},{4,6},{6,4},{8,10},{10,8},{12,14},{14,12},{1,3},{3,1},... | collective-permute-start | bytes 1327112 | tf_op jit(solution)/shard_map/ppermute | solution.py:244
  35.7 6.3 %collective-permute-done.4.arrived = bf16[72,1536]{1,0:T(8,128)(2,1)S(1)} collective-permute-done((bf16[72,1536]{1,0:T(8,128)(2,1)S(1)}, bf16[72,1536]{1,0:T(8,128)(2,1)S(1)}, u32[]{:S(2)}, u32[]{:S(2)}) %collective-permute-start.4) | collective-permute-done | bytes 221216 | tf_op jit(solution)/shard_map/ppermute | solution.py:244
  42.1 2.3 %collective-permute-done.6 = bf16[72,3072]{1,0:T(8,128)(2,1)S(1)} collective-permute-done((bf16[72,3072]{1,0:T(8,128)(2,1)S(1)}, bf16[72,3072]{1,0:T(8,128)(2,1)S(1)}, u32[]{:S(2)}, u32[]{:S(2)}) %collective-permute-start.6) | collective-permute-done | bytes 442400 | tf_op jit(solution)/shard_map/ppermute | solution.py:298
  45.5 3.2 %collective-permute-done.11.other.refs_5_ = bf16[72,3072]{1,0:T(8,128)(2,1)S(1)} collective-permute-done((bf16[72,3072]{1,0:T(8,128)(2,1)S(1)}, bf16[72,3072]{1,0:T(8,128)(2,1)S(1)}, u32[]{:S(2)}, u32[]{:S(2)}) %collective-permute-start.11) | collective-permute-done | bytes 442400 | tf_op jit(solution)/shard_map/ppermute | solution.py:244
  50.0 1.3 %collective-permute-done.12.arrived = bf16[80,768]{1,0:T(8,128)(2,1)S(1)} collective-permute-done((bf16[80,768]{1,0:T(8,128)(2,1)S(1)}, bf16[80,768]{1,0:T(8,128)(2,1)S(1)}, u32[]{:S(2)}, u32[]{:S(2)}) %collective-permute-start.12) | collective-permute-done | bytes 122912 | tf_op jit(solution)/shard_map/ppermute | solution.py:274
  55.1 6.0 %collective-permute-done.13.arrived = bf16[72,1536]{1,0:T(8,128)(2,1)S(1)} collective-permute-done((bf16[72,1536]{1,0:T(8,128)(2,1)S(1)}, bf16[72,1536]{1,0:T(8,128)(2,1)S(1)}, u32[]{:S(2)}, u32[]{:S(2)}) %collective-permute-start.13) | collective-permute-done | bytes 221216 | tf_op jit(solution)/shard_map/ppermute | solution.py:244
  64.1 5.2 %collective-permute-start.14 = (bf16[72,1536]{1,0:T(8,128)(2,1)S(1)}, bf16[72,1536]{1,0:T(8,128)(2,1)S(1)}, u32[]{:S(2)}, u32[]{:S(2)}) collective-permute-start(bf16[72,1536]{1,0:T(8,128)(2,1)S(1)} %add.10), channel_id=1, source_target_pairs={{0,8},{2,10},{4,12},{6,14},{8,0},{10,2},{12,4},{14,6},{1,9},{3,11}... | collective-permute-start | bytes 663560 | tf_op jit(solution)/shard_map/ppermute | solution.py:247
  70.4 1.6 %collective-permute-start.17 = (bf16[72,1536]{1,0:T(8,128)(2,1)S(1)}, bf16[72,1536]{1,0:T(8,128)(2,1)S(1)}, u32[]{:S(2)}, u32[]{:S(2)}) collective-permute-start(bf16[72,1536]{1,0:T(8,128)(2,1)S(1)} %get-tuple-element.73), channel_id=1, source_target_pairs={{0,2},{2,0},{4,6},{6,4},{8,10},{10,8},{12,14},{14,12},{1,3},{3,1},... | collective-permute-start | bytes 663560 | tf_op jit(solution)/shard_map/ppermute | solution.py:244
  72.1 4.1 %collective-permute-start.10 = (bf16[72,1536]{1,0:T(8,128)(2,1)S(1)}, bf16[72,1536]{1,0:T(8,128)(2,1)S(1)}, u32[]{:S(2)}, u32[]{:S(2)}) collective-permute-start(bf16[72,1536]{1,0:T(8,128)(2,1)S(1)} %add.9), channel_id=1, source_target_pairs={{0,4},{2,6},{4,0},{6,2},{8,12},{10,14},{12,8},{14,10},{1,5},{3,7},... | collective-permute-start | bytes 663560 | tf_op jit(solution)/shard_map/ppermute | solution.py:247
  76.2 3.8 %collective-permute-done.14.third = bf16[72,1536]{1,0:T(8,128)(2,1)S(1)} collective-permute-done((bf16[72,1536]{1,0:T(8,128)(2,1)S(1)}, bf16[72,1536]{1,0:T(8,128)(2,1)S(1)}, u32[]{:S(2)}, u32[]{:S(2)}) %collective-permute-start.14) | collective-permute-done | bytes 221216 | tf_op jit(solution)/shard_map/ppermute | solution.py:247
  80.0 1.4 %collective-permute-start.18 = (bf16[72,1536]{1,0:T(8,128)(2,1)S(1)}, bf16[72,1536]{1,0:T(8,128)(2,1)S(1)}, u32[]{:S(2)}, u32[]{:S(2)}) collective-permute-start(bf16[72,1536]{1,0:T(8,128)(2,1)S(1)} %add.11), channel_id=1, source_target_pairs={{0,12},{2,14},{4,8},{6,10},{8,4},{10,6},{12,0},{14,2},{1,13},{3,15... | collective-permute-start | bytes 663560 | tf_op jit(solution)/shard_map/ppermute | solution.py:247
  81.4 7.9 %collective-permute-done.10.second = bf16[72,1536]{1,0:T(8,128)(2,1)S(1)} collective-permute-done((bf16[72,1536]{1,0:T(8,128)(2,1)S(1)}, bf16[72,1536]{1,0:T(8,128)(2,1)S(1)}, u32[]{:S(2)}, u32[]{:S(2)}) %collective-permute-start.10) | collective-permute-done | bytes 221216 | tf_op jit(solution)/shard_map/ppermute | solution.py:247
  89.3 4.6 %grads.1 = (bf16[3072,256]{1,0:T(8,128)(2,1)}, bf16[3072,256]{1,0:T(8,128)(2,1)}, bf16[256,3072]{1,0:T(8,128)(2,1)}) custom-call(bf16[72,3072]{1,0:T(8,128)(2,1)S(1)} %get-tuple-element.74.mine.refs_0_, bf16[72,3072]{1,0:T(8,128)(2,1)S(1)} %collective-permute-done.other.refs_1_, bf16[72,3072]{1,0:T(8,128)(2,1)S(1)} %collective-permute-done.3.mine.refs_2_, ...), custom_call_target="tpu_custom_call" | custom-call | flops 1000 | bytes 1000 | tf_op jit(solution)/shard_map/grads/pallas_call | solution.py:101
  93.9 1.3 %finish.1 = bf16[128,3072]{1,0:T(8,128)(2,1)} custom-call(bf16[128,128]{1,0:T(8,128)(2,1)S(1)} %get-tuple-element.47.placing_t, bf16[72,1536]{1,0:T(8,128)(2,1)S(1)} %add.8.first, bf16[72,1536]{1,0:T(8,128)(2,1)S(1)} %collective-permute-done.10.second, bf16[72,1536]{1,0:T(8,128)(2,1)S(1)} %collective-permute-done.14.third, ...), custom_call_target="tpu_custom_call" | custom-call | flops 1000 | bytes 1000 | tf_op jit(solution)/shard_map/finish/pallas_call | solution.py:101
  (46 shorter events, 18.6 us)
Async XLA Ops:
  0.6 17.8 %copy-start = (bf16[3072,256]{1,0:T(8,128)(2,1)S(1)}, bf16[3072,256]{1,0:T(8,128)(2,1)}, u32[]{:S(2)}) copy-start(bf16[3072,256]{1,0:T(8,128)(2,1)} %w_gate.15) | copy-start | bytes 4718596
  0.6 1.3 %copy-start.4 = (bf16[128,3072]{1,0:T(8,128)(2,1)S(1)}, bf16[128,3072]{1,0:T(8,128)(2,1)}, u32[]{:S(2)}) copy-start(bf16[128,3072]{1,0:T(8,128)(2,1)} %tokens_at.1) | copy-start | bytes 2359300
  5.2 13.2 %collective-permute-start = (bf16[72,3072]{1,0:T(8,128)(2,1)S(1)}, bf16[72,3072]{1,0:T(8,128)(2,1)S(1)}, u32[]{:S(2)}, u32[]{:S(2)}) collective-permute-start(bf16[72,3072]{1,0:T(8,128)(2,1)S(1)} %get-tuple-element.74.mine.refs_0_), channel_id=1, source_target_pairs={{0,2},{2,0},{4,6},{6,4},{8,10},{10,8},{12,14},{14,12},{1,3},{3,1},... | collective-permute-start | bytes 1327112 | tf_op jit(solution)/shard_map/ppermute | solution.py:244
  8.3 21.0 %collective-permute-start.3 = (bf16[72,3072]{1,0:T(8,128)(2,1)S(1)}, bf16[72,3072]{1,0:T(8,128)(2,1)S(1)}, u32[]{:S(2)}, u32[]{:S(2)}) collective-permute-start(bf16[72,3072]{1,0:T(8,128)(2,1)S(1)} %get-tuple-element.74.mine.refs_0_), channel_id=1, source_target_pairs={{0,4},{2,6},{4,0},{6,2},{8,12},{10,14},{12,8},{14,10},{1,5},{3,7},... | collective-permute-start | bytes 1327112 | tf_op jit(solution)/shard_map/ppermute | solution.py:247
  9.9 21.8 %collective-permute-start.2 = (bf16[72,3072]{1,0:T(8,128)(2,1)S(1)}, bf16[72,3072]{1,0:T(8,128)(2,1)S(1)}, u32[]{:S(2)}, u32[]{:S(2)}) collective-permute-start(bf16[72,3072]{1,0:T(8,128)(2,1)S(1)} %get-tuple-element.74.mine.refs_0_), channel_id=1, source_target_pairs={{0,8},{2,10},{4,12},{6,14},{8,0},{10,2},{12,4},{14,6},{1,9},{3,11}... | collective-permute-start | bytes 1327112 | tf_op jit(solution)/shard_map/ppermute | solution.py:247
  18.4 1.4 %copy-start.1 = (bf16[3072,256]{1,0:T(8,128)(2,1)S(1)}, bf16[3072,256]{1,0:T(8,128)(2,1)}, u32[]{:S(2)}) copy-start(bf16[3072,256]{1,0:T(8,128)(2,1)} %w_up.15) | copy-start | bytes 4718596
  19.9 1.4 %copy-start.2 = (bf16[256,3072]{1,0:T(8,128)(2,1)S(1)}, bf16[256,3072]{1,0:T(8,128)(2,1)}, u32[]{:S(2)}) copy-start(bf16[256,3072]{1,0:T(8,128)(2,1)} %w_down.7) | copy-start | bytes 4718596
  22.4 1.4 %collective-permute-start.1 = (bf16[80,768]{1,0:T(8,128)(2,1)S(1)}, bf16[80,768]{1,0:T(8,128)(2,1)S(1)}, u32[]{:S(2)}, u32[]{:S(2)}) collective-permute-start(bf16[80,768]{1,0:T(8,128)(2,1)S(1)} %get-tuple-element.50), channel_id=1, source_target_pairs={{0,1},{1,0},{2,3},{3,2},{4,5},{5,4},{6,7},{7,6},{8,9},{9,8},{10,11... | collective-permute-start | bytes 368648 | tf_op jit(solution)/shard_map/ppermute | solution.py:274
  24.9 23.8 %copy-start.3 = (bf16[256,3072]{1,0:T(8,128)(2,1)S(1)}, bf16[256,3072]{1,0:T(8,128)(2,1)}, u32[]{:S(2)}) copy-start(bf16[256,3072]{1,0:T(8,128)(2,1)} %w_down.7) | copy-start | bytes 4718596
  31.6 10.5 %collective-permute-start.5 = (bf16[72,3072]{1,0:T(8,128)(2,1)S(1)}, bf16[72,3072]{1,0:T(8,128)(2,1)S(1)}, u32[]{:S(2)}, u32[]{:S(2)}) collective-permute-start(bf16[72,3072]{1,0:T(8,128)(2,1)S(1)} %get-tuple-element.74.mine.refs_0_), channel_id=1, source_target_pairs={{4,8},{6,10},{8,4},{10,6},{5,9},{7,11},{9,5},{11,7},{20,24},{22,26... | collective-permute-start | bytes 1327112 | tf_op jit(solution)/shard_map/ppermute | solution.py:297
  32.3 12.1 %collective-permute-start.6 = (bf16[72,3072]{1,0:T(8,128)(2,1)S(1)}, bf16[72,3072]{1,0:T(8,128)(2,1)S(1)}, u32[]{:S(2)}, u32[]{:S(2)}) collective-permute-start(bf16[72,3072]{1,0:T(8,128)(2,1)S(1)} %collective-permute-done.2.mine.refs_4_), channel_id=1, source_target_pairs={{8,12},{10,14},{4,0},{6,2},{9,13},{11,15},{5,1},{7,3},{24,28},{26,... | collective-permute-start | bytes 1327112 | tf_op jit(solution)/shard_map/ppermute | solution.py:298
  33.6 8.4 %collective-permute-start.4 = (bf16[72,1536]{1,0:T(8,128)(2,1)S(1)}, bf16[72,1536]{1,0:T(8,128)(2,1)S(1)}, u32[]{:S(2)}, u32[]{:S(2)}) collective-permute-start(bf16[72,1536]{1,0:T(8,128)(2,1)S(1)} %get-tuple-element.53), channel_id=1, source_target_pairs={{0,2},{2,0},{4,6},{6,4},{8,10},{10,8},{12,14},{14,12},{1,3},{3,1},... | collective-permute-start | bytes 663560 | tf_op jit(solution)/shard_map/ppermute | solution.py:244
  34.2 14.5 %collective-permute-start.11 = (bf16[72,3072]{1,0:T(8,128)(2,1)S(1)}, bf16[72,3072]{1,0:T(8,128)(2,1)S(1)}, u32[]{:S(2)}, u32[]{:S(2)}) collective-permute-start(bf16[72,3072]{1,0:T(8,128)(2,1)S(1)} %collective-permute-done.2.mine.refs_4_), channel_id=1, source_target_pairs={{0,2},{2,0},{4,6},{6,4},{8,10},{10,8},{12,14},{14,12},{1,3},{3,1},... | collective-permute-start | bytes 1327112 | tf_op jit(solution)/shard_map/ppermute | solution.py:244
  44.5 9.3 %collective-permute-start.7 = (bf16[72,3072]{1,0:T(8,128)(2,1)S(1)}, bf16[72,3072]{1,0:T(8,128)(2,1)S(1)}, u32[]{:S(2)}, u32[]{:S(2)}) collective-permute-start(bf16[72,3072]{1,0:T(8,128)(2,1)S(1)} %collective-permute-done.other.refs_1_), channel_id=1, source_target_pairs={{0,4},{2,6},{4,0},{6,2},{8,12},{10,14},{12,8},{14,10},{1,5},{3,7},... | collective-permute-start | bytes 1327112 | tf_op jit(solution)/shard_map/ppermute | solution.py:247
  45.0 17.2 %collective-permute-start.15 = (bf16[72,3072]{1,0:T(8,128)(2,1)S(1)}, bf16[72,3072]{1,0:T(8,128)(2,1)S(1)}, u32[]{:S(2)}, u32[]{:S(2)}) collective-permute-start(bf16[72,3072]{1,0:T(8,128)(2,1)S(1)} %add.7.mine.refs_6_), channel_id=1, source_target_pairs={{0,2},{2,0},{4,6},{6,4},{8,10},{10,8},{12,14},{14,12},{1,3},{3,1},... | collective-permute-start | bytes 1327112 | tf_op jit(solution)/shard_map/ppermute | solution.py:244
  49.9 1.4 %collective-permute-start.12 = (bf16[80,768]{1,0:T(8,128)(2,1)S(1)}, bf16[80,768]{1,0:T(8,128)(2,1)S(1)}, u32[]{:S(2)}, u32[]{:S(2)}) collective-permute-start(bf16[80,768]{1,0:T(8,128)(2,1)S(1)} %get-tuple-element.65), channel_id=1, source_target_pairs={{0,1},{1,0},{2,3},{3,2},{4,5},{5,4},{6,7},{7,6},{8,9},{9,8},{10,11... | collective-permute-start | bytes 368648 | tf_op jit(solution)/shard_map/ppermute | solution.py:274
  52.4 8.6 %collective-permute-start.13 = (bf16[72,1536]{1,0:T(8,128)(2,1)S(1)}, bf16[72,1536]{1,0:T(8,128)(2,1)S(1)}, u32[]{:S(2)}, u32[]{:S(2)}) collective-permute-start(bf16[72,1536]{1,0:T(8,128)(2,1)S(1)} %get-tuple-element.67), channel_id=1, source_target_pairs={{0,2},{2,0},{4,6},{6,4},{8,10},{10,8},{12,14},{14,12},{1,3},{3,1},... | collective-permute-start | bytes 663560 | tf_op jit(solution)/shard_map/ppermute | solution.py:244
  55.0 6.1 %collective-permute-start.8 = (bf16[80,768]{1,0:T(8,128)(2,1)S(1)}, bf16[80,768]{1,0:T(8,128)(2,1)S(1)}, u32[]{:S(2)}, u32[]{:S(2)}) collective-permute-start(bf16[80,768]{1,0:T(8,128)(2,1)S(1)} %get-tuple-element.60), channel_id=1, source_target_pairs={{0,1},{1,0},{2,3},{3,2},{4,5},{5,4},{6,7},{7,6},{8,9},{9,8},{10,11... | collective-permute-start | bytes 368648 | tf_op jit(solution)/shard_map/ppermute | solution.py:274
  63.3 6.0 %collective-permute-start.16 = (bf16[80,768]{1,0:T(8,128)(2,1)S(1)}, bf16[80,768]{1,0:T(8,128)(2,1)S(1)}, u32[]{:S(2)}, u32[]{:S(2)}) collective-permute-start(bf16[80,768]{1,0:T(8,128)(2,1)S(1)} %get-tuple-element.70), channel_id=1, source_target_pairs={{0,1},{1,0},{2,3},{3,2},{4,5},{5,4},{6,7},{7,6},{8,9},{9,8},{10,11... | collective-permute-start | bytes 368648 | tf_op jit(solution)/shard_map/ppermute | solution.py:274
  63.4 8.6 %collective-permute-start.9 = (bf16[72,1536]{1,0:T(8,128)(2,1)S(1)}, bf16[72,1536]{1,0:T(8,128)(2,1)S(1)}, u32[]{:S(2)}, u32[]{:S(2)}) collective-permute-start(bf16[72,1536]{1,0:T(8,128)(2,1)S(1)} %get-tuple-element.62), channel_id=1, source_target_pairs={{0,2},{2,0},{4,6},{6,4},{8,10},{10,8},{12,14},{14,12},{1,3},{3,1},... | collective-permute-start | bytes 663560 | tf_op jit(solution)/shard_map/ppermute | solution.py:244
  64.1 15.8 %collective-permute-start.14 = (bf16[72,1536]{1,0:T(8,128)(2,1)S(1)}, bf16[72,1536]{1,0:T(8,128)(2,1)S(1)}, u32[]{:S(2)}, u32[]{:S(2)}) collective-permute-start(bf16[72,1536]{1,0:T(8,128)(2,1)S(1)} %add.10), channel_id=1, source_target_pairs={{0,8},{2,10},{4,12},{6,14},{8,0},{10,2},{12,4},{14,6},{1,9},{3,11}... | collective-permute-start | bytes 663560 | tf_op jit(solution)/shard_map/ppermute | solution.py:247
  70.4 9.5 %collective-permute-start.17 = (bf16[72,1536]{1,0:T(8,128)(2,1)S(1)}, bf16[72,1536]{1,0:T(8,128)(2,1)S(1)}, u32[]{:S(2)}, u32[]{:S(2)}) collective-permute-start(bf16[72,1536]{1,0:T(8,128)(2,1)S(1)} %get-tuple-element.73), channel_id=1, source_target_pairs={{0,2},{2,0},{4,6},{6,4},{8,10},{10,8},{12,14},{14,12},{1,3},{3,1},... | collective-permute-start | bytes 663560 | tf_op jit(solution)/shard_map/ppermute | solution.py:244
  72.1 17.2 %collective-permute-start.10 = (bf16[72,1536]{1,0:T(8,128)(2,1)S(1)}, bf16[72,1536]{1,0:T(8,128)(2,1)S(1)}, u32[]{:S(2)}, u32[]{:S(2)}) collective-permute-start(bf16[72,1536]{1,0:T(8,128)(2,1)S(1)} %add.9), channel_id=1, source_target_pairs={{0,4},{2,6},{4,0},{6,2},{8,12},{10,14},{12,8},{14,10},{1,5},{3,7},... | collective-permute-start | bytes 663560 | tf_op jit(solution)/shard_map/ppermute | solution.py:247
  80.0 13.9 %collective-permute-start.18 = (bf16[72,1536]{1,0:T(8,128)(2,1)S(1)}, bf16[72,1536]{1,0:T(8,128)(2,1)S(1)}, u32[]{:S(2)}, u32[]{:S(2)}) collective-permute-start(bf16[72,1536]{1,0:T(8,128)(2,1)S(1)} %add.11), channel_id=1, source_target_pairs={{0,12},{2,14},{4,8},{6,10},{8,4},{10,6},{12,0},{14,2},{1,13},{3,15... | collective-permute-start | bytes 663560 | tf_op jit(solution)/shard_map/ppermute | solution.py:247
  (3 other events, 2.5 us)

commit v4 on v3

--- a/solution.py
+++ b/solution.py
@@ -143,35 +143,32 @@
     x = mul(placing, tokens[...])
     copies[3].wait()
     dy = mul(placing, grad_out[...]) * scale
-    block[0:MAIN, :] = x[0:MAIN].astype(BF16)
-    block[MAIN : 2 * MAIN, :] = dy[0:MAIN].astype(BF16)
     last = jnp.concatenate([x[MAIN:CAP], dy[MAIN:CAP]], axis=0)
-    block[2 * MAIN : BLOCK, :] = last.astype(BF16)
-
-
-def tails(blocks, turned):
+    for at, value in ((0, x[0:MAIN]), (MAIN, dy[0:MAIN]), (2 * MAIN, last)):
+        block[at : at + value.shape[0], :] = value.astype(BF16)
+
+
+def tails(blocks, turned, columns):
     parts = []
     for block in blocks:
-        last = block[2 * MAIN : BLOCK, :].astype(F32)
+        last = block[2 * MAIN : BLOCK, columns].astype(F32)
         if turned:
             last = jnp.concatenate([last[TAIL:], last[:TAIL]], axis=0)
         parts.append(last)
     return jnp.concatenate(parts, axis=0).astype(BF16)
 
 
-def rows_of(blocks, first, turned):
-    return jnp.concatenate(
-        [block[first : first + MAIN, :] for block in blocks] + [tails(blocks, turned)], axis=0
-    )
+def rows_of(blocks, first, turned, columns):
+    main = [block[first : first + MAIN, columns] for block in blocks]
+    last = [tails(blocks[i : i + 2], turned, columns) for i in range(0, len(blocks), 2)]
+    return jnp.concatenate(main + last, axis=0)
 
 
 def front_kernel(mine, other, w_gate, w_up, w_down, part, sent):
     width = w_gate.shape[1]
-    x = rows_of((mine, other), 0, False)
-    dy = rows_of((mine, other), MAIN, True)
-    for at, value in enumerate(
-        (mul(x, w_gate[...]), mul(x, w_up[...]), mul(dy, w_down[...], 1, 1))
-    ):
+    x = rows_of((mine, other), 0, False, slice(None))
+    dy = rows_of((mine, other), MAIN, True, slice(None))
+    for at, value in enumerate((mul(x, w_gate[...]), mul(x, w_up[...]), mul(dy, w_down[...], 1, 1))):
         part[:, at * width : (at + 1) * width] = value
         sent[:, at * width : (at + 1) * width] = value.astype(BF16)
 
@@ -204,9 +201,12 @@
     total[...] = (term[...] + arrived[...].astype(F32)).astype(BF16)
 
 
-def finish_kernel(placing_t, first, second, third, fourth, grad_in):
-    total = first[...].astype(F32) + second[...].astype(F32)
-    total = total + third[...].astype(F32) + fourth[...].astype(F32)
+def near_kernel(first, second, third, total):
+    total[...] = first[...].astype(F32) + second[...].astype(F32) + third[...].astype(F32)
+
+
+def finish_kernel(placing_t, near, last, grad_in):
+    total = near[...] + last[...].astype(F32)
     half = total.shape[1]
     placing = placing_t[:, :CAP]
     grad_in[:, :half] = mul(placing, total[:CAP].astype(BF16)).astype(BF16)
@@ -214,31 +214,43 @@
 
 
 def grads_kernel(*refs):
-    blocks, hiddens, d_pres = refs[0:8], refs[8:12], refs[12:16]
-    grad_gate, grad_up, grad_down = refs[16:19]
-    width = grad_gate.shape[1]
+    blocks, hiddens, d_pres, outs, tiles, done = refs[:8], refs[8:12], refs[12:16], refs[16:19], refs[19:22], refs[22]
+    features, width = outs[0].shape
+    size = features // 4
 
     def groups(values):
         return jnp.concatenate(
             [v[: 2 * MAIN, :] for v in values] + [v[2 * MAIN :, :] for v in values], axis=0
         )
 
-    def rows(first, turned):
-        return jnp.concatenate(
-            [v[first : first + MAIN, :] for v in blocks]
-            + [tails(blocks[i : i + 2], turned) for i in range(0, 8, 2)],
-            axis=0,
-        )
-
     d_pre, hidden = groups(d_pres), groups(hiddens)
-    x = rows(0, False)
-    grad_gate[...] = mul(x, d_pre[:, :width], 0, 0).astype(BF16)
-    grad_up[...] = mul(x, d_pre[:, width:], 0, 0).astype(BF16)
-    grad_down[...] = mul(hidden, rows(MAIN, True), 0, 0).astype(BF16)
+    copies = []
+    for step in range(4):
+        at = slice(step * size, (step + 1) * size)
+        x = rows_of(blocks, 0, False, at)
+        tiles[0][at, :] = mul(x, d_pre[:, :width], 0, 0).astype(BF16)
+        tiles[1][at, :] = mul(x, d_pre[:, width:], 0, 0).astype(BF16)
+        tiles[2][:, at] = mul(hidden, rows_of(blocks, MAIN, True, at), 0, 0).astype(BF16)
+        for i, place in enumerate(((at, slice(None)), (at, slice(None)), (slice(None), at))):
+            copy = pltpu.make_async_copy(tiles[i].at[place], outs[i].at[place], done.at[3 * step + i])
+            copy.start()
+            copies.append(copy)
+    for copy in copies:
+        copy.wait()
+
+
+def load_kernel(*refs):
+    copies = [pltpu.make_async_copy(refs[i], refs[3 + i], refs[6].at[i]) for i in range(3)]
+    for copy in copies:
+        copy.start()
+    for copy in copies:
+        copy.wait()
 
 
 def four_by_two(tokens, grad_out, expert_ids, gate_probs, w_gate, w_up, w_down):
     features, width = w_gate.shape
+    half = features // 2
+    in_hbm = pl.BlockSpec(memory_space=pltpu.HBM)
 
     def across(value):
         return lax.ppermute(value, "expert", [(i, i ^ 1) for i in range(8)])
@@ -249,13 +261,17 @@
     def after(value, *others):
         return lax.optimization_barrier((value,) + others)[0]
 
-    gate, up, down = (pltpu.with_memory_space_constraint(w, pltpu.VMEM) for w in (w_gate, w_up, w_down))
+    def hbm(value):
+        return pltpu.with_memory_space_constraint(value, pltpu.HBM)
 
     own, placing_t = call(
         place_kernel,
-        (struct(BLOCK, features, BF16), struct(tokens.shape[0], tokens.shape[0], BF16)),
-        tokens, grad_out, expert_ids.T, gate_probs.T, name="place",
-        in_specs=[pl.BlockSpec(memory_space=pltpu.HBM)] * 4,
+        (
+            struct(BLOCK, features, BF16),
+            struct(tokens.shape[0], tokens.shape[0], BF16),
+        ),
+        hbm(tokens), hbm(grad_out), hbm(expert_ids.T), hbm(gate_probs.T), name="place",
+        in_specs=[in_hbm] * 4,
         scratch_shapes=[
             pltpu.VMEM(tokens.shape, BF16),
             pltpu.VMEM(tokens.shape, BF16),
@@ -264,6 +280,14 @@
             pltpu.SemaphoreType.DMA((4,)),
         ],
     )
+    w_gate, w_up, w_down, _ = lax.optimization_barrier((w_gate, w_up, w_down, own))
+    gate, up, down = call(
+        load_kernel,
+        tuple(struct(*w.shape, BF16) for w in (w_gate, w_up, w_down)),
+        hbm(w_gate), hbm(w_up), hbm(w_down), name="load",
+        in_specs=[in_hbm] * 3,
+        scratch_shapes=[pltpu.SemaphoreType.DMA((3,))],
+    )
 
     def front(mine, other):
         part, sent = call(
@@ -274,63 +298,69 @@
         return part, lax.ppermute(sent, "tensor", [(0, 1), (1, 0)])
 
     def back(part, arrived):
-        hidden, d_pre, term, sent = call(
+        return call(
             back_kernel,
             (
                 struct(GROUP, width, BF16),
                 struct(GROUP, 2 * width, BF16),
-                struct(BLOCK, features // 2, F32),
-                struct(BLOCK, features // 2, BF16),
+                struct(BLOCK, half, F32),
+                struct(BLOCK, half, BF16),
             ),
             part, arrived, gate, up, name="back",
         )
-        return hidden, d_pre, term, sent
 
     def add(term, sent):
-        return call(add_kernel, struct(BLOCK, features // 2, BF16), term, across(sent), name="add")
+        return call(add_kernel, struct(BLOCK, half, BF16), term, across(sent), name="add")
+
+    def middle(value):
+        return lax.ppermute(value, "expert", [(2, 4), (3, 5), (4, 2), (5, 3)])
+
+    def ends(value):
+        return lax.ppermute(value, "expert", [(4, 6), (5, 7), (2, 0), (3, 1)])
 
     own_y = across(own)
     two = along(own, 2)
     one = along(own, 1)
     h0, d0, t0, s0 = back(*front(own, own_y))
-    two, one, s0 = lax.optimization_barrier((two, one, s0))
-    middle = lax.ppermute(after(own, two), "expert", [(2, 4), (3, 5), (4, 2), (5, 3)])
-    ends = lax.ppermute(two, "expert", [(4, 6), (5, 7), (2, 0), (3, 1)])
+    one_y = along(own_y, 1)
+    q0 = add(t0, s0)
+    two, one, q0 = lax.optimization_barrier((two, one, q0))
+    inner = middle(after(own, two))
+    outer = ends(two)
     two_y = across(two)
-    q0 = add(t0, s0)
-    three = after(middle + ends, q0)
-    three_y = across(three)
-    one_y = along(after(own_y, three), 1)
-    h2, d2, t2, s2 = back(*front(after(two, three), two_y))
+    h1, d1, t1, s1 = back(*front(one, one_y))
+    q1 = add(t1, s1)
+    inner, two_y, s1 = lax.optimization_barrier((inner, two_y, s1))
+    inner_y = middle(after(own_y, inner))
+    outer_y = ends(two_y)
+    three = inner + outer
+    three_y = inner_y + outer_y
+    part2, swap2 = front(two, two_y)
+    h2, d2, t2, s2 = back(after(part2, three, q1), swap2)
     q2 = add(t2, s2)
     r2 = along(q2, 2)
-    h1, d1, t1, s1 = back(*front(one, one_y))
-    q1 = add(t1, s1)
-    r1 = along(q1, 1)
-    h3, d3, t3, s3 = back(*front(after(three, q2, s1), three_y))
+    h3, d3, t3, s3 = back(*front(after(three, q2), three_y))
+    r1 = along(after(q1, s3), 1)
     q3 = add(after(t3, r2), s3)
     r3 = along(q3, 3)
 
-    tile = features // 4
-    column = pl.BlockSpec((BLOCK, tile), lambda j: (0, j))
-    whole = [pl.BlockSpec((GROUP, width), lambda j: (0, 0))] * 4
-    whole += [pl.BlockSpec((GROUP, 2 * width), lambda j: (0, 0))] * 4
     grads = call(
         grads_kernel,
         (struct(features, width, BF16), struct(features, width, BF16), struct(width, features, BF16)),
-        after(own, q3, r1), own_y, one, one_y, two, two_y, three, three_y, h0, h1, h2, h3, d0, d1, d2, d3,
+        after(own, q3), own_y, one, one_y, two, two_y, three, three_y, h0, h1, h2, h3, d0, d1, d2, d3,
         name="grads",
-        grid=(features // tile,),
-        in_specs=[column] * 8 + whole,
-        out_specs=(
-            pl.BlockSpec((tile, width), lambda j: (j, 0)),
-            pl.BlockSpec((tile, width), lambda j: (j, 0)),
-            pl.BlockSpec((width, tile), lambda j: (0, j)),
-        ),
-    )
-    grads, r3 = lax.optimization_barrier((grads, r3))
+        out_specs=(pl.BlockSpec(memory_space=pltpu.HBM),) * 3,
+        scratch_shapes=[
+            pltpu.VMEM(w_gate.shape, BF16),
+            pltpu.VMEM(w_up.shape, BF16),
+            pltpu.VMEM(w_down.shape, BF16),
+            pltpu.SemaphoreType.DMA((12,)),
+        ],
+    )
+    grads, r2, r1 = lax.optimization_barrier((grads, r2, r1))
+    near = call(near_kernel, struct(BLOCK, half, F32), q0, r1, r2, name="near")
     grad_in = call(
-        finish_kernel, struct(tokens.shape[0], features, BF16), placing_t, q0, r1, r2, r3, name="finish"
+        finish_kernel, struct(tokens.shape[0], features, BF16), placing_t, near, after(r3, near), name="finish"
     )
     return (grad_in,) + tuple(grads)
 

time: 95.4 us -> 82.5 us (0.86)
  waiting for transfers between devices: 45.4 us -> 38.6 us
  local copies, waits for them, and re-layouts: 6.56 us -> 0 us
  Pallas kernels: 15.8 us -> 18 us
  starting transfers between devices: 26.5 us -> 24.4 us
    unnamed x16 -> x0, local copies, waits for them, and re-layouts: 6.56 us -> none
    ppermute x7 -> x6, waiting for transfers between devices: 21.6 us -> 18.3 us  [across(): return lax.ppermute(value, 'expert', [(i, i ^ 1) for i in range(8)])]
    ppermute x6, starting transfers between devices: 15.4 us -> 12.5 us  [along(): lax.ppermute(value, 'expert', [(i, i ^ 2 * distance) for i in range(8)])]
    pallas_call x15 -> x17, Pallas kernels: 15.8 us -> 18 us  [call(): pl.pallas_call(kernel, out_shape=outs, name=name, compiler_params=pltpu.C...]
    ppermute x2 -> x4, waiting for transfers between devices: 2.26 us -> 0.19 us  [the longest x2 0.19 us: ends(): return lax.ppermute(value, 'expert', [(4, 6), (5, 7), (2, 0), (3, 1)])]
    ppermute x2 -> x4, starting transfers between devices: 1.97 us -> 3.93 us  [the longest x2 2.57 us: ends(): return lax.ppermute(value, 'expert', [(4, 6), (5, 7), (2, 0), (3, 1)])]
    ppermute x6, waiting for transfers between devices: 18.9 us -> 17.5 us  [along(): lax.ppermute(value, 'expert', [(i, i ^ 2 * distance) for i in range(8)])]
    ppermute x7 -> x6, starting transfers between devices: 8.86 us -> 7.65 us  [across(): return lax.ppermute(value, 'expert', [(i, i ^ 1) for i in range(8)])]
  transfers between devices with their start and end apart: 19 -> 20, of which waited for: 12 -> 11; matrix products, arithmetic and copies ran while one was open for 0% -> 0% of each run, Pallas kernels for 13% -> 17%
where the time goes in v4:
time: 82.5 us; the launch traced here: 82 us
  waiting for transfers between devices  38.6 us (47%)
  starting transfers between devices  24.4 us (30%)
  Pallas kernels  18 us (22%)
    ppermute x6, waiting for transfers between devices, across(): return lax.ppermute(value, 'expert', [(i, i ^ 1) for i in range(8)])  18.3 us
    pallas_call x17, Pallas kernels, call(): pl.pallas_call(kernel, out_shape=outs, name=name, compiler_params=pltpu.C...  18 us
    ppermute x6, waiting for transfers between devices, along(): lax.ppermute(value, 'expert', [(i, i ^ 2 * distance) for i in range(8)])  17.5 us
    ppermute x6, starting transfers between devices, along(): lax.ppermute(value, 'expert', [(i, i ^ 2 * distance) for i in range(8)])  12.5 us
    ppermute x6, starting transfers between devices, across(): return lax.ppermute(value, 'expert', [(i, i ^ 1) for i in range(8)])  7.65 us
    ppermute x4, waiting for transfers between devices, front(): return (part, lax.ppermute(sent, 'tensor', [(0, 1), (1, 0)]))  2.65 us
    ppermute x2, starting transfers between devices, ends(): return lax.ppermute(value, 'expert', [(4, 6), (5, 7), (2, 0), (3, 1)])  2.57 us
  transfers between devices with their start and end apart: 20, of which 11 were waited for; matrix products, arithmetic and copies ran while one was open for 0% of the time, Pallas kernels for 17%

profile of v4, /device:TPU:0, one launch (start us, length us, event | category | flops | bytes accessed | tf_op | source)
XLA Modules:
  0.0 82.0 jit_solution(8351965504957658688)
XLA Ops:
  0.6 1.7 %place.1 = (bf16[72,3072]{1,0:T(8,128)(2,1)S(1)}, bf16[128,128]{1,0:T(8,128)(2,1)S(1)}) custom-call(bf16[128,3072]{1,0:T(8,128)(2,1)} %tokens_at.1, bf16[128,3072]{1,0:T(8,128)(2,1)} %grad_out_at.1, s32[2,128]{1,0:T(2,128)} %bitcast.2, f32[2,128]{1,0:T(2,128)} %bitcast.3), custom_call_target="tpu_custom_call" | custom-call | flops 1000 | bytes 1000 | tf_op jit(solution)/shard_map/place/pallas_call | solution.py:101
  2.3 3.0 %collective-permute-start.2 = (bf16[72,3072]{1,0:T(8,128)(2,1)S(1)}, bf16[72,3072]{1,0:T(8,128)(2,1)S(1)}, u32[]{:S(2)}, u32[]{:S(2)}) collective-permute-start(bf16[72,3072]{1,0:T(8,128)(2,1)S(1)} %get-tuple-element.91.mine.refs_0_), channel_id=1, source_target_pairs={{0,2},{2,0},{4,6},{6,4},{8,10},{10,8},{12,14},{14,12},{1,3},{3,1},... | collective-permute-start | bytes 1327112 | tf_op jit(solution)/shard_map/ppermute | solution.py:256
  5.4 1.6 %collective-permute-start.1 = (bf16[72,3072]{1,0:T(8,128)(2,1)S(1)}, bf16[72,3072]{1,0:T(8,128)(2,1)S(1)}, u32[]{:S(2)}, u32[]{:S(2)}) collective-permute-start(bf16[72,3072]{1,0:T(8,128)(2,1)S(1)} %get-tuple-element.91.mine.refs_0_), channel_id=1, source_target_pairs={{0,4},{2,6},{4,0},{6,2},{8,12},{10,14},{12,8},{14,10},{1,5},{3,7},... | collective-permute-start | bytes 1327112 | tf_op jit(solution)/shard_map/ppermute | solution.py:259
  7.0 2.6 %collective-permute-start = (bf16[72,3072]{1,0:T(8,128)(2,1)S(1)}, bf16[72,3072]{1,0:T(8,128)(2,1)S(1)}, u32[]{:S(2)}, u32[]{:S(2)}) collective-permute-start(bf16[72,3072]{1,0:T(8,128)(2,1)S(1)} %get-tuple-element.91.mine.refs_0_), channel_id=1, source_target_pairs={{0,8},{2,10},{4,12},{6,14},{8,0},{10,2},{12,4},{14,6},{1,9},{3,11}... | collective-permute-start | bytes 1327112 | tf_op jit(solution)/shard_map/ppermute | solution.py:259
  9.6 2.4 %load.1 = (bf16[3072,256]{1,0:T(8,128)(2,1)S(1)}, bf16[3072,256]{1,0:T(8,128)(2,1)S(1)}, bf16[256,3072]{1,0:T(8,128)(2,1)S(1)}) custom-call(bf16[3072,256]{1,0:T(8,128)(2,1)} %refs_0_, bf16[3072,256]{1,0:T(8,128)(2,1)} %refs_1_, bf16[256,3072]{1,0:T(8,128)(2,1)} %refs_2_), custom_call_target="tpu_custom_call" | custom-call | flops 1000 | bytes 1000 | tf_op jit(solution)/shard_map/load/pallas_call | solution.py:101
  11.9 3.6 %collective-permute-done.2.other.refs_1_ = bf16[72,3072]{1,0:T(8,128)(2,1)S(1)} collective-permute-done((bf16[72,3072]{1,0:T(8,128)(2,1)S(1)}, bf16[72,3072]{1,0:T(8,128)(2,1)S(1)}, u32[]{:S(2)}, u32[]{:S(2)}) %collective-permute-start.2) | collective-permute-done | bytes 442400 | tf_op jit(solution)/shard_map/ppermute | solution.py:256
  16.8 1.3 %collective-permute-done.3.arrived = bf16[80,768]{1,0:T(8,128)(2,1)S(1)} collective-permute-done((bf16[80,768]{1,0:T(8,128)(2,1)S(1)}, bf16[80,768]{1,0:T(8,128)(2,1)S(1)}, u32[]{:S(2)}, u32[]{:S(2)}) %collective-permute-start.3) | collective-permute-done | bytes 122912 | tf_op jit(solution)/shard_map/ppermute | solution.py:298
  19.2 1.8 %collective-permute-start.4 = (bf16[72,1536]{1,0:T(8,128)(2,1)S(1)}, bf16[72,1536]{1,0:T(8,128)(2,1)S(1)}, u32[]{:S(2)}, u32[]{:S(2)}) collective-permute-start(bf16[72,1536]{1,0:T(8,128)(2,1)S(1)} %get-tuple-element.68), channel_id=1, source_target_pairs={{0,2},{2,0},{4,6},{6,4},{8,10},{10,8},{12,14},{14,12},{1,3},{3,1},... | collective-permute-start | bytes 663560 | tf_op jit(solution)/shard_map/ppermute | solution.py:256
  21.0 1.6 %collective-permute-start.7 = (bf16[72,3072]{1,0:T(8,128)(2,1)S(1)}, bf16[72,3072]{1,0:T(8,128)(2,1)S(1)}, u32[]{:S(2)}, u32[]{:S(2)}) collective-permute-start(bf16[72,3072]{1,0:T(8,128)(2,1)S(1)} %collective-permute-done.2.other.refs_1_), channel_id=1, source_target_pairs={{0,4},{2,6},{4,0},{6,2},{8,12},{10,14},{12,8},{14,10},{1,5},{3,7},... | collective-permute-start | bytes 1327112 | tf_op jit(solution)/shard_map/ppermute | solution.py:259
  22.6 4.2 %collective-permute-done.4.arrived = bf16[72,1536]{1,0:T(8,128)(2,1)S(1)} collective-permute-done((bf16[72,1536]{1,0:T(8,128)(2,1)S(1)}, bf16[72,1536]{1,0:T(8,128)(2,1)S(1)}, u32[]{:S(2)}, u32[]{:S(2)}) %collective-permute-start.4) | collective-permute-done | bytes 221216 | tf_op jit(solution)/shard_map/ppermute | solution.py:256
  26.8 1.2 %collective-permute-done.1.mine.refs_2_ = bf16[72,3072]{1,0:T(8,128)(2,1)S(1)} collective-permute-done((bf16[72,3072]{1,0:T(8,128)(2,1)S(1)}, bf16[72,3072]{1,0:T(8,128)(2,1)S(1)}, u32[]{:S(2)}, u32[]{:S(2)}) %collective-permute-start.1) | collective-permute-done | bytes 442400 | tf_op jit(solution)/shard_map/ppermute | solution.py:259
  29.3 1.3 %collective-permute-start.9 = (bf16[72,3072]{1,0:T(8,128)(2,1)S(1)}, bf16[72,3072]{1,0:T(8,128)(2,1)S(1)}, u32[]{:S(2)}, u32[]{:S(2)}) collective-permute-start(bf16[72,3072]{1,0:T(8,128)(2,1)S(1)} %collective-permute-done.mine.refs_4_), channel_id=1, source_target_pairs={{8,12},{10,14},{4,0},{6,2},{9,13},{11,15},{5,1},{7,3},{24,28},{26,... | collective-permute-start | bytes 1327112 | tf_op jit(solution)/shard_map/ppermute | solution.py:319
  30.6 6.7 %collective-permute-done.7.other.refs_3_ = bf16[72,3072]{1,0:T(8,128)(2,1)S(1)} collective-permute-done((bf16[72,3072]{1,0:T(8,128)(2,1)S(1)}, bf16[72,3072]{1,0:T(8,128)(2,1)S(1)}, u32[]{:S(2)}, u32[]{:S(2)}) %collective-permute-start.7) | collective-permute-done | bytes 442400 | tf_op jit(solution)/shard_map/ppermute | solution.py:259
  38.6 1.3 %collective-permute-done.8.arrived = bf16[80,768]{1,0:T(8,128)(2,1)S(1)} collective-permute-done((bf16[80,768]{1,0:T(8,128)(2,1)S(1)}, bf16[80,768]{1,0:T(8,128)(2,1)S(1)}, u32[]{:S(2)}, u32[]{:S(2)}) %collective-permute-start.8) | collective-permute-done | bytes 122912 | tf_op jit(solution)/shard_map/ppermute | solution.py:298
  41.9 1.3 %collective-permute-start.14 = (bf16[72,3072]{1,0:T(8,128)(2,1)S(1)}, bf16[72,3072]{1,0:T(8,128)(2,1)S(1)}, u32[]{:S(2)}, u32[]{:S(2)}) collective-permute-start(bf16[72,3072]{1,0:T(8,128)(2,1)S(1)} %collective-permute-done.6.other.refs_5_), channel_id=1, source_target_pairs={{8,12},{10,14},{4,0},{6,2},{9,13},{11,15},{5,1},{7,3},{24,28},{26,... | collective-permute-start | bytes 1327112 | tf_op jit(solution)/shard_map/ppermute | solution.py:319
  44.4 4.1 %collective-permute-done.10.arrived = bf16[72,1536]{1,0:T(8,128)(2,1)S(1)} collective-permute-done((bf16[72,1536]{1,0:T(8,128)(2,1)S(1)}, bf16[72,1536]{1,0:T(8,128)(2,1)S(1)}, u32[]{:S(2)}, u32[]{:S(2)}) %collective-permute-start.10) | collective-permute-done | bytes 221216 | tf_op jit(solution)/shard_map/ppermute | solution.py:256
  50.1 6.4 %collective-permute-done.12.arrived = bf16[72,1536]{1,0:T(8,128)(2,1)S(1)} collective-permute-done((bf16[72,1536]{1,0:T(8,128)(2,1)S(1)}, bf16[72,1536]{1,0:T(8,128)(2,1)S(1)}, u32[]{:S(2)}, u32[]{:S(2)}) %collective-permute-start.12) | collective-permute-done | bytes 221216 | tf_op jit(solution)/shard_map/ppermute | solution.py:256
  58.1 2.8 %collective-permute-start.16 = (bf16[72,1536]{1,0:T(8,128)(2,1)S(1)}, bf16[72,1536]{1,0:T(8,128)(2,1)S(1)}, u32[]{:S(2)}, u32[]{:S(2)}) collective-permute-start(bf16[72,1536]{1,0:T(8,128)(2,1)S(1)} %add.14), channel_id=1, source_target_pairs={{0,8},{2,10},{4,12},{6,14},{8,0},{10,2},{12,4},{14,6},{1,9},{3,11}... | collective-permute-start | bytes 663560 | tf_op jit(solution)/shard_map/ppermute | solution.py:259
  61.9 1.6 %collective-permute-start.17 = (bf16[72,1536]{1,0:T(8,128)(2,1)S(1)}, bf16[72,1536]{1,0:T(8,128)(2,1)S(1)}, u32[]{:S(2)}, u32[]{:S(2)}) collective-permute-start(bf16[72,1536]{1,0:T(8,128)(2,1)S(1)} %get-tuple-element.90), channel_id=1, source_target_pairs={{0,2},{2,0},{4,6},{6,4},{8,10},{10,8},{12,14},{14,12},{1,3},{3,1},... | collective-permute-start | bytes 663560 | tf_op jit(solution)/shard_map/ppermute | solution.py:256
  64.2 7.6 %collective-permute-done.16.third = bf16[72,1536]{1,0:T(8,128)(2,1)S(1)} collective-permute-done((bf16[72,1536]{1,0:T(8,128)(2,1)S(1)}, bf16[72,1536]{1,0:T(8,128)(2,1)S(1)}, u32[]{:S(2)}, u32[]{:S(2)}) %collective-permute-start.16) | collective-permute-done | bytes 221216 | tf_op jit(solution)/shard_map/ppermute | solution.py:259
  71.8 3.3 %collective-permute-start.19 = (bf16[72,1536]{1,0:T(8,128)(2,1)S(1)}, bf16[72,1536]{1,0:T(8,128)(2,1)S(1)}, u32[]{:S(2)}, u32[]{:S(2)}) collective-permute-start(bf16[72,1536]{1,0:T(8,128)(2,1)S(1)} %add.15), channel_id=1, source_target_pairs={{0,12},{2,14},{4,8},{6,10},{8,4},{10,6},{12,0},{14,2},{1,13},{3,15... | collective-permute-start | bytes 663560 | tf_op jit(solution)/shard_map/ppermute | solution.py:259
  75.1 3.5 %grads.1 = (bf16[3072,256]{1,0:T(8,128)(2,1)}, bf16[3072,256]{1,0:T(8,128)(2,1)}, bf16[256,3072]{1,0:T(8,128)(2,1)}) custom-call(bf16[72,3072]{1,0:T(8,128)(2,1)S(1)} %get-tuple-element.91.mine.refs_0_, bf16[72,3072]{1,0:T(8,128)(2,1)S(1)} %collective-permute-done.2.other.refs_1_, bf16[72,3072]{1,0:T(8,128)(2,1)S(1)} %collective-permute-done.1.mine.refs_2_, ...), custom_call_target="tpu_custom_call" | custom-call | flops 1000 | bytes 1000 | tf_op jit(solution)/shard_map/grads/pallas_call | solution.py:101
  78.7 2.0 %collective-permute-done.19.last = bf16[72,1536]{1,0:T(8,128)(2,1)S(1)} collective-permute-done((bf16[72,1536]{1,0:T(8,128)(2,1)S(1)}, bf16[72,1536]{1,0:T(8,128)(2,1)S(1)}, u32[]{:S(2)}, u32[]{:S(2)}) %collective-permute-start.19) | collective-permute-done | bytes 221216 | tf_op jit(solution)/shard_map/ppermute | solution.py:259
  80.7 1.2 %finish.1 = bf16[128,3072]{1,0:T(8,128)(2,1)} custom-call(bf16[128,128]{1,0:T(8,128)(2,1)S(1)} %get-tuple-element.57.placing_t, f32[72,1536]{1,0:T(8,128)S(1)} %near.1, bf16[72,1536]{1,0:T(8,128)(2,1)S(1)} %collective-permute-done.19.last), custom_call_target="tpu_custom_call" | custom-call | flops 1000 | bytes 1000 | tf_op jit(solution)/shard_map/finish/pallas_call | solution.py:101
  (35 shorter events, 13.2 us)
Async XLA Ops:
  2.3 13.2 %collective-permute-start.2 = (bf16[72,3072]{1,0:T(8,128)(2,1)S(1)}, bf16[72,3072]{1,0:T(8,128)(2,1)S(1)}, u32[]{:S(2)}, u32[]{:S(2)}) collective-permute-start(bf16[72,3072]{1,0:T(8,128)(2,1)S(1)} %get-tuple-element.91.mine.refs_0_), channel_id=1, source_target_pairs={{0,2},{2,0},{4,6},{6,4},{8,10},{10,8},{12,14},{14,12},{1,3},{3,1},... | collective-permute-start | bytes 1327112 | tf_op jit(solution)/shard_map/ppermute | solution.py:256
  5.4 22.6 %collective-permute-start.1 = (bf16[72,3072]{1,0:T(8,128)(2,1)S(1)}, bf16[72,3072]{1,0:T(8,128)(2,1)S(1)}, u32[]{:S(2)}, u32[]{:S(2)}) collective-permute-start(bf16[72,3072]{1,0:T(8,128)(2,1)S(1)} %get-tuple-element.91.mine.refs_0_), channel_id=1, source_target_pairs={{0,4},{2,6},{4,0},{6,2},{8,12},{10,14},{12,8},{14,10},{1,5},{3,7},... | collective-permute-start | bytes 1327112 | tf_op jit(solution)/shard_map/ppermute | solution.py:259
  7.0 21.0 %collective-permute-start = (bf16[72,3072]{1,0:T(8,128)(2,1)S(1)}, bf16[72,3072]{1,0:T(8,128)(2,1)S(1)}, u32[]{:S(2)}, u32[]{:S(2)}) collective-permute-start(bf16[72,3072]{1,0:T(8,128)(2,1)S(1)} %get-tuple-element.91.mine.refs_0_), channel_id=1, source_target_pairs={{0,8},{2,10},{4,12},{6,14},{8,0},{10,2},{12,4},{14,6},{1,9},{3,11}... | collective-permute-start | bytes 1327112 | tf_op jit(solution)/shard_map/ppermute | solution.py:259
  16.7 1.4 %collective-permute-start.3 = (bf16[80,768]{1,0:T(8,128)(2,1)S(1)}, bf16[80,768]{1,0:T(8,128)(2,1)S(1)}, u32[]{:S(2)}, u32[]{:S(2)}) collective-permute-start(bf16[80,768]{1,0:T(8,128)(2,1)S(1)} %get-tuple-element.66), channel_id=1, source_target_pairs={{0,1},{1,0},{2,3},{3,2},{4,5},{5,4},{6,7},{7,6},{8,9},{9,8},{10,11... | collective-permute-start | bytes 368648 | tf_op jit(solution)/shard_map/ppermute | solution.py:298
  19.2 7.6 %collective-permute-start.4 = (bf16[72,1536]{1,0:T(8,128)(2,1)S(1)}, bf16[72,1536]{1,0:T(8,128)(2,1)S(1)}, u32[]{:S(2)}, u32[]{:S(2)}) collective-permute-start(bf16[72,1536]{1,0:T(8,128)(2,1)S(1)} %get-tuple-element.68), channel_id=1, source_target_pairs={{0,2},{2,0},{4,6},{6,4},{8,10},{10,8},{12,14},{14,12},{1,3},{3,1},... | collective-permute-start | bytes 663560 | tf_op jit(solution)/shard_map/ppermute | solution.py:256
  21.0 16.3 %collective-permute-start.7 = (bf16[72,3072]{1,0:T(8,128)(2,1)S(1)}, bf16[72,3072]{1,0:T(8,128)(2,1)S(1)}, u32[]{:S(2)}, u32[]{:S(2)}) collective-permute-start(bf16[72,3072]{1,0:T(8,128)(2,1)S(1)} %collective-permute-done.2.other.refs_1_), channel_id=1, source_target_pairs={{0,4},{2,6},{4,0},{6,2},{8,12},{10,14},{12,8},{14,10},{1,5},{3,7},... | collective-permute-start | bytes 1327112 | tf_op jit(solution)/shard_map/ppermute | solution.py:259
  28.0 13.2 %collective-permute-start.5 = (bf16[72,3072]{1,0:T(8,128)(2,1)S(1)}, bf16[72,3072]{1,0:T(8,128)(2,1)S(1)}, u32[]{:S(2)}, u32[]{:S(2)}) collective-permute-start(bf16[72,3072]{1,0:T(8,128)(2,1)S(1)} %get-tuple-element.91.mine.refs_0_), channel_id=1, source_target_pairs={{4,8},{6,10},{8,4},{10,6},{5,9},{7,11},{9,5},{11,7},{20,24},{22,26... | collective-permute-start | bytes 1327112 | tf_op jit(solution)/shard_map/ppermute | solution.py:316
  28.6 12.5 %collective-permute-start.6 = (bf16[72,3072]{1,0:T(8,128)(2,1)S(1)}, bf16[72,3072]{1,0:T(8,128)(2,1)S(1)}, u32[]{:S(2)}, u32[]{:S(2)}) collective-permute-start(bf16[72,3072]{1,0:T(8,128)(2,1)S(1)} %collective-permute-done.mine.refs_4_), channel_id=1, source_target_pairs={{0,2},{2,0},{4,6},{6,4},{8,10},{10,8},{12,14},{14,12},{1,3},{3,1},... | collective-permute-start | bytes 1327112 | tf_op jit(solution)/shard_map/ppermute | solution.py:256
  29.3 19.2 %collective-permute-start.9 = (bf16[72,3072]{1,0:T(8,128)(2,1)S(1)}, bf16[72,3072]{1,0:T(8,128)(2,1)S(1)}, u32[]{:S(2)}, u32[]{:S(2)}) collective-permute-start(bf16[72,3072]{1,0:T(8,128)(2,1)S(1)} %collective-permute-done.mine.refs_4_), channel_id=1, source_target_pairs={{8,12},{10,14},{4,0},{6,2},{9,13},{11,15},{5,1},{7,3},{24,28},{26,... | collective-permute-start | bytes 1327112 | tf_op jit(solution)/shard_map/ppermute | solution.py:319
  38.5 1.4 %collective-permute-start.8 = (bf16[80,768]{1,0:T(8,128)(2,1)S(1)}, bf16[80,768]{1,0:T(8,128)(2,1)S(1)}, u32[]{:S(2)}, u32[]{:S(2)}) collective-permute-start(bf16[80,768]{1,0:T(8,128)(2,1)S(1)} %get-tuple-element.74), channel_id=1, source_target_pairs={{0,1},{1,0},{2,3},{3,2},{4,5},{5,4},{6,7},{7,6},{8,9},{9,8},{10,11... | collective-permute-start | bytes 368648 | tf_op jit(solution)/shard_map/ppermute | solution.py:298
  41.0 7.5 %collective-permute-start.10 = (bf16[72,1536]{1,0:T(8,128)(2,1)S(1)}, bf16[72,1536]{1,0:T(8,128)(2,1)S(1)}, u32[]{:S(2)}, u32[]{:S(2)}) collective-permute-start(bf16[72,1536]{1,0:T(8,128)(2,1)S(1)} %get-tuple-element.75), channel_id=1, source_target_pairs={{0,2},{2,0},{4,6},{6,4},{8,10},{10,8},{12,14},{14,12},{1,3},{3,1},... | collective-permute-start | bytes 663560 | tf_op jit(solution)/shard_map/ppermute | solution.py:256
  41.2 15.4 %collective-permute-start.13 = (bf16[72,3072]{1,0:T(8,128)(2,1)S(1)}, bf16[72,3072]{1,0:T(8,128)(2,1)S(1)}, u32[]{:S(2)}, u32[]{:S(2)}) collective-permute-start(bf16[72,3072]{1,0:T(8,128)(2,1)S(1)} %collective-permute-done.2.other.refs_1_), channel_id=1, source_target_pairs={{4,8},{6,10},{8,4},{10,6},{5,9},{7,11},{9,5},{11,7},{20,24},{22,26... | collective-permute-start | bytes 1327112 | tf_op jit(solution)/shard_map/ppermute | solution.py:316
  41.9 14.9 %collective-permute-start.14 = (bf16[72,3072]{1,0:T(8,128)(2,1)S(1)}, bf16[72,3072]{1,0:T(8,128)(2,1)S(1)}, u32[]{:S(2)}, u32[]{:S(2)}) collective-permute-start(bf16[72,3072]{1,0:T(8,128)(2,1)S(1)} %collective-permute-done.6.other.refs_5_), channel_id=1, source_target_pairs={{8,12},{10,14},{4,0},{6,2},{9,13},{11,15},{5,1},{7,3},{24,28},{26,... | collective-permute-start | bytes 1327112 | tf_op jit(solution)/shard_map/ppermute | solution.py:319
  44.3 4.4 %collective-permute-start.11 = (bf16[80,768]{1,0:T(8,128)(2,1)S(1)}, bf16[80,768]{1,0:T(8,128)(2,1)S(1)}, u32[]{:S(2)}, u32[]{:S(2)}) collective-permute-start(bf16[80,768]{1,0:T(8,128)(2,1)S(1)} %get-tuple-element.81), channel_id=1, source_target_pairs={{0,1},{1,0},{2,3},{3,2},{4,5},{5,4},{6,7},{7,6},{8,9},{9,8},{10,11... | collective-permute-start | bytes 368648 | tf_op jit(solution)/shard_map/ppermute | solution.py:298
  49.8 6.7 %collective-permute-start.12 = (bf16[72,1536]{1,0:T(8,128)(2,1)S(1)}, bf16[72,1536]{1,0:T(8,128)(2,1)S(1)}, u32[]{:S(2)}, u32[]{:S(2)}) collective-permute-start(bf16[72,1536]{1,0:T(8,128)(2,1)S(1)} %get-tuple-element.83), channel_id=1, source_target_pairs={{0,2},{2,0},{4,6},{6,4},{8,10},{10,8},{12,14},{14,12},{1,3},{3,1},... | collective-permute-start | bytes 663560 | tf_op jit(solution)/shard_map/ppermute | solution.py:256
  58.0 2.9 %collective-permute-start.15 = (bf16[80,768]{1,0:T(8,128)(2,1)S(1)}, bf16[80,768]{1,0:T(8,128)(2,1)S(1)}, u32[]{:S(2)}, u32[]{:S(2)}) collective-permute-start(bf16[80,768]{1,0:T(8,128)(2,1)S(1)} %get-tuple-element.87), channel_id=1, source_target_pairs={{0,1},{1,0},{2,3},{3,2},{4,5},{5,4},{6,7},{7,6},{8,9},{9,8},{10,11... | collective-permute-start | bytes 368648 | tf_op jit(solution)/shard_map/ppermute | solution.py:298
  58.1 13.6 %collective-permute-start.16 = (bf16[72,1536]{1,0:T(8,128)(2,1)S(1)}, bf16[72,1536]{1,0:T(8,128)(2,1)S(1)}, u32[]{:S(2)}, u32[]{:S(2)}) collective-permute-start(bf16[72,1536]{1,0:T(8,128)(2,1)S(1)} %add.14), channel_id=1, source_target_pairs={{0,8},{2,10},{4,12},{6,14},{8,0},{10,2},{12,4},{14,6},{1,9},{3,11}... | collective-permute-start | bytes 663560 | tf_op jit(solution)/shard_map/ppermute | solution.py:259
  61.9 9.8 %collective-permute-start.17 = (bf16[72,1536]{1,0:T(8,128)(2,1)S(1)}, bf16[72,1536]{1,0:T(8,128)(2,1)S(1)}, u32[]{:S(2)}, u32[]{:S(2)}) collective-permute-start(bf16[72,1536]{1,0:T(8,128)(2,1)S(1)} %get-tuple-element.90), channel_id=1, source_target_pairs={{0,2},{2,0},{4,6},{6,4},{8,10},{10,8},{12,14},{14,12},{1,3},{3,1},... | collective-permute-start | bytes 663560 | tf_op jit(solution)/shard_map/ppermute | solution.py:256
  63.5 15.1 %collective-permute-start.18 = (bf16[72,1536]{1,0:T(8,128)(2,1)S(1)}, bf16[72,1536]{1,0:T(8,128)(2,1)S(1)}, u32[]{:S(2)}, u32[]{:S(2)}) collective-permute-start(bf16[72,1536]{1,0:T(8,128)(2,1)S(1)} %add.13), channel_id=1, source_target_pairs={{0,4},{2,6},{4,0},{6,2},{8,12},{10,14},{12,8},{14,10},{1,5},{3,7},... | collective-permute-start | bytes 663560 | tf_op jit(solution)/shard_map/ppermute | solution.py:259
  71.8 9.0 %collective-permute-start.19 = (bf16[72,1536]{1,0:T(8,128)(2,1)S(1)}, bf16[72,1536]{1,0:T(8,128)(2,1)S(1)}, u32[]{:S(2)}, u32[]{:S(2)}) collective-permute-start(bf16[72,1536]{1,0:T(8,128)(2,1)S(1)} %add.15), channel_id=1, source_target_pairs={{0,12},{2,14},{4,8},{6,10},{8,4},{10,6},{12,0},{14,2},{1,13},{3,15... | collective-permute-start | bytes 663560 | tf_op jit(solution)/shard_map/ppermute | solution.py:259

commit v5 on v4

--- a/solution.py
+++ b/solution.py
@@ -201,8 +201,19 @@
     total[...] = (term[...] + arrived[...].astype(F32)).astype(BF16)
 
 
-def near_kernel(first, second, third, total):
-    total[...] = first[...].astype(F32) + second[...].astype(F32) + third[...].astype(F32)
+def is_inner():
+    line = lax.axis_index("expert") // 2
+    return (line == 1) | (line == 2)
+
+
+def last_kernel(term, arrived, passed, total):
+    value = term[...] + arrived[...].astype(F32)
+    total[...] = jnp.where(is_inner(), value + passed[...].astype(F32), value).astype(BF16)
+
+
+def near_kernel(first, second, passed, total):
+    value = first[...].astype(F32) + second[...].astype(F32)
+    total[...] = jnp.where(is_inner(), value, value + passed[...].astype(F32))
 
 
 def finish_kernel(placing_t, near, last, grad_in):
@@ -317,6 +328,10 @@
 
     def ends(value):
         return lax.ppermute(value, "expert", [(4, 6), (5, 7), (2, 0), (3, 1)])
+
+    def relay(value):
+        pairs = [(0, 2), (1, 3), (2, 6), (3, 7), (4, 0), (5, 1), (6, 4), (7, 5)]
+        return lax.ppermute(value, "expert", pairs)
 
     own_y = across(own)
     two = along(own, 2)
@@ -338,10 +353,10 @@
     part2, swap2 = front(two, two_y)
     h2, d2, t2, s2 = back(after(part2, three, q1), swap2)
     q2 = add(t2, s2)
-    r2 = along(q2, 2)
+    got = relay(q2)
     h3, d3, t3, s3 = back(*front(after(three, q2), three_y))
     r1 = along(after(q1, s3), 1)
-    q3 = add(after(t3, r2), s3)
+    q3 = call(last_kernel, struct(BLOCK, half, BF16), t3, across(s3), got, name="last")
     r3 = along(q3, 3)
 
     grads = call(
@@ -357,8 +372,8 @@
             pltpu.SemaphoreType.DMA((12,)),
         ],
     )
-    grads, r2, r1 = lax.optimization_barrier((grads, r2, r1))
-    near = call(near_kernel, struct(BLOCK, half, F32), q0, r1, r2, name="near")
+    grads, r1 = lax.optimization_barrier((grads, r1))
+    near = call(near_kernel, struct(BLOCK, half, F32), q0, r1, got, name="near")
     grad_in = call(
         finish_kernel, struct(tokens.shape[0], features, BF16), placing_t, near, after(r3, near), name="finish"
     )

time: 82.5 us -> 80.6 us (0.977)
  the two profiles are of different devices: /device:TPU:0 before, /device:TPU:8 now
where the time goes in v5:
time: 80.6 us; the launch traced here: 80.4 us
  waiting for transfers between devices  39.8 us (49%)
  starting transfers between devices  21.5 us (27%)
  Pallas kernels  18.1 us (22%)
  between operations  0.81 us (1%)
    ppermute x6, waiting for transfers between devices, across(): return lax.ppermute(value, 'expert', [(i, i ^ 1) for i in range(8)])  21.2 us
    pallas_call x17, Pallas kernels, call(): pl.pallas_call(kernel, out_shape=outs, name=name, compiler_params=pltpu.C...  18.1 us
    ppermute x5, waiting for transfers between devices, along(): lax.ppermute(value, 'expert', [(i, i ^ 2 * distance) for i in range(8)])  11.7 us
    ppermute x6, starting transfers between devices, across(): return lax.ppermute(value, 'expert', [(i, i ^ 1) for i in range(8)])  7.12 us
    ppermute x2, starting transfers between devices, middle(): return lax.ppermute(value, 'expert', [(2, 4), (3, 5), (4, 2), (5, 3)])  4.69 us
    ppermute x5, starting transfers between devices, along(): lax.ppermute(value, 'expert', [(i, i ^ 2 * distance) for i in range(8)])  4.36 us
    ppermute x1, waiting for transfers between devices, relay(): return lax.ppermute(value, 'expert', pairs)  3.53 us
    ppermute x4, waiting for transfers between devices, front(): return (part, lax.ppermute(sent, 'tensor', [(0, 1), (1, 0)]))  3.2 us
  transfers between devices with their start and end apart: 20, of which 14 were waited for; matrix products, arithmetic and copies ran while one was open for 0% of the time, Pallas kernels for 17%

profile of v5, /device:TPU:8, one launch (start us, length us, event | category | flops | bytes accessed | tf_op | source)
XLA Modules:
  0.0 80.4 jit_solution(15572706232952518808)
XLA Ops:
  0.6 1.7 %place.1 = (bf16[72,3072]{1,0:T(8,128)(2,1)S(1)}, bf16[128,128]{1,0:T(8,128)(2,1)S(1)}) custom-call(bf16[128,3072]{1,0:T(8,128)(2,1)} %tokens_at.1, bf16[128,3072]{1,0:T(8,128)(2,1)} %grad_out_at.1, s32[2,128]{1,0:T(2,128)} %bitcast.2, f32[2,128]{1,0:T(2,128)} %bitcast.3), custom_call_target="tpu_custom_call" | custom-call | flops 1000 | bytes 1000 | tf_op jit(solution)/shard_map/place/pallas_call | solution.py:101
  2.4 1.6 %collective-permute-start.2 = (bf16[72,3072]{1,0:T(8,128)(2,1)S(1)}, bf16[72,3072]{1,0:T(8,128)(2,1)S(1)}, u32[]{:S(2)}, u32[]{:S(2)}) collective-permute-start(bf16[72,3072]{1,0:T(8,128)(2,1)S(1)} %get-tuple-element.88.mine.refs_0_), channel_id=1, source_target_pairs={{0,2},{2,0},{4,6},{6,4},{8,10},{10,8},{12,14},{14,12},{1,3},{3,1},... | collective-permute-start | bytes 1327112 | tf_op jit(solution)/shard_map/ppermute | solution.py:267
  4.4 2.6 %collective-permute-start = (bf16[72,3072]{1,0:T(8,128)(2,1)S(1)}, bf16[72,3072]{1,0:T(8,128)(2,1)S(1)}, u32[]{:S(2)}, u32[]{:S(2)}) collective-permute-start(bf16[72,3072]{1,0:T(8,128)(2,1)S(1)} %get-tuple-element.88.mine.refs_0_), channel_id=1, source_target_pairs={{0,8},{2,10},{4,12},{6,14},{8,0},{10,2},{12,4},{14,6},{1,9},{3,11}... | collective-permute-start | bytes 1327112 | tf_op jit(solution)/shard_map/ppermute | solution.py:270
  7.0 2.4 %load.1 = (bf16[3072,256]{1,0:T(8,128)(2,1)S(1)}, bf16[3072,256]{1,0:T(8,128)(2,1)S(1)}, bf16[256,3072]{1,0:T(8,128)(2,1)S(1)}) custom-call(bf16[3072,256]{1,0:T(8,128)(2,1)} %refs_0_, bf16[3072,256]{1,0:T(8,128)(2,1)} %refs_1_, bf16[256,3072]{1,0:T(8,128)(2,1)} %refs_2_), custom_call_target="tpu_custom_call" | custom-call | flops 1000 | bytes 1000 | tf_op jit(solution)/shard_map/load/pallas_call | solution.py:101
  9.4 5.0 %collective-permute-done.2.other.refs_1_ = bf16[72,3072]{1,0:T(8,128)(2,1)S(1)} collective-permute-done((bf16[72,3072]{1,0:T(8,128)(2,1)S(1)}, bf16[72,3072]{1,0:T(8,128)(2,1)S(1)}, u32[]{:S(2)}, u32[]{:S(2)}) %collective-permute-start.2) | collective-permute-done | bytes 442400 | tf_op jit(solution)/shard_map/ppermute | solution.py:267
  15.6 1.3 %collective-permute-done.3.arrived = bf16[80,768]{1,0:T(8,128)(2,1)S(1)} collective-permute-done((bf16[80,768]{1,0:T(8,128)(2,1)S(1)}, bf16[80,768]{1,0:T(8,128)(2,1)S(1)}, u32[]{:S(2)}, u32[]{:S(2)}) %collective-permute-start.3) | collective-permute-done | bytes 122912 | tf_op jit(solution)/shard_map/ppermute | solution.py:309
  18.0 1.6 %collective-permute-start.4 = (bf16[72,1536]{1,0:T(8,128)(2,1)S(1)}, bf16[72,1536]{1,0:T(8,128)(2,1)S(1)}, u32[]{:S(2)}, u32[]{:S(2)}) collective-permute-start(bf16[72,1536]{1,0:T(8,128)(2,1)S(1)} %get-tuple-element.66), channel_id=1, source_target_pairs={{0,2},{2,0},{4,6},{6,4},{8,10},{10,8},{12,14},{14,12},{1,3},{3,1},... | collective-permute-start | bytes 663560 | tf_op jit(solution)/shard_map/ppermute | solution.py:267
  20.0 5.5 %collective-permute-done.4.arrived = bf16[72,1536]{1,0:T(8,128)(2,1)S(1)} collective-permute-done((bf16[72,1536]{1,0:T(8,128)(2,1)S(1)}, bf16[72,1536]{1,0:T(8,128)(2,1)S(1)}, u32[]{:S(2)}, u32[]{:S(2)}) %collective-permute-start.4) | collective-permute-done | bytes 221216 | tf_op jit(solution)/shard_map/ppermute | solution.py:267
  25.6 2.0 %collective-permute-done.mine.refs_4_ = bf16[72,3072]{1,0:T(8,128)(2,1)S(1)} collective-permute-done((bf16[72,3072]{1,0:T(8,128)(2,1)S(1)}, bf16[72,3072]{1,0:T(8,128)(2,1)S(1)}, u32[]{:S(2)}, u32[]{:S(2)}) %collective-permute-start) | collective-permute-done | bytes 442400 | tf_op jit(solution)/shard_map/ppermute | solution.py:270
  27.6 2.3 %collective-permute-start.5 = (bf16[72,3072]{1,0:T(8,128)(2,1)S(1)}, bf16[72,3072]{1,0:T(8,128)(2,1)S(1)}, u32[]{:S(2)}, u32[]{:S(2)}) collective-permute-start(bf16[72,3072]{1,0:T(8,128)(2,1)S(1)} %get-tuple-element.88.mine.refs_0_), channel_id=1, source_target_pairs={{4,8},{6,10},{8,4},{10,6},{5,9},{7,11},{9,5},{11,7},{20,24},{22,26... | collective-permute-start | bytes 1327112 | tf_op jit(solution)/shard_map/ppermute | solution.py:327
  30.7 1.3 %collective-permute-start.9 = (bf16[72,3072]{1,0:T(8,128)(2,1)S(1)}, bf16[72,3072]{1,0:T(8,128)(2,1)S(1)}, u32[]{:S(2)}, u32[]{:S(2)}) collective-permute-start(bf16[72,3072]{1,0:T(8,128)(2,1)S(1)} %collective-permute-done.mine.refs_4_), channel_id=1, source_target_pairs={{8,12},{10,14},{4,0},{6,2},{9,13},{11,15},{5,1},{7,3},{24,28},{26,... | collective-permute-start | bytes 1327112 | tf_op jit(solution)/shard_map/ppermute | solution.py:330
  32.0 2.6 %collective-permute-done.7.other.refs_3_ = bf16[72,3072]{1,0:T(8,128)(2,1)S(1)} collective-permute-done((bf16[72,3072]{1,0:T(8,128)(2,1)S(1)}, bf16[72,3072]{1,0:T(8,128)(2,1)S(1)}, u32[]{:S(2)}, u32[]{:S(2)}) %collective-permute-start.7) | collective-permute-done | bytes 442400 | tf_op jit(solution)/shard_map/ppermute | solution.py:270
  35.8 1.3 %collective-permute-done.8.arrived = bf16[80,768]{1,0:T(8,128)(2,1)S(1)} collective-permute-done((bf16[80,768]{1,0:T(8,128)(2,1)S(1)}, bf16[80,768]{1,0:T(8,128)(2,1)S(1)}, u32[]{:S(2)}, u32[]{:S(2)}) %collective-permute-start.8) | collective-permute-done | bytes 122912 | tf_op jit(solution)/shard_map/ppermute | solution.py:309
  38.9 1.4 %collective-permute-done.6.other.refs_5_ = bf16[72,3072]{1,0:T(8,128)(2,1)S(1)} collective-permute-done((bf16[72,3072]{1,0:T(8,128)(2,1)S(1)}, bf16[72,3072]{1,0:T(8,128)(2,1)S(1)}, u32[]{:S(2)}, u32[]{:S(2)}) %collective-permute-start.6) | collective-permute-done | bytes 442400 | tf_op jit(solution)/shard_map/ppermute | solution.py:267
  40.3 2.3 %collective-permute-start.13 = (bf16[72,3072]{1,0:T(8,128)(2,1)S(1)}, bf16[72,3072]{1,0:T(8,128)(2,1)S(1)}, u32[]{:S(2)}, u32[]{:S(2)}) collective-permute-start(bf16[72,3072]{1,0:T(8,128)(2,1)S(1)} %collective-permute-done.2.other.refs_1_), channel_id=1, source_target_pairs={{4,8},{6,10},{8,4},{10,6},{5,9},{7,11},{9,5},{11,7},{20,24},{22,26... | collective-permute-start | bytes 1327112 | tf_op jit(solution)/shard_map/ppermute | solution.py:327
  42.6 1.3 %collective-permute-start.14 = (bf16[72,3072]{1,0:T(8,128)(2,1)S(1)}, bf16[72,3072]{1,0:T(8,128)(2,1)S(1)}, u32[]{:S(2)}, u32[]{:S(2)}) collective-permute-start(bf16[72,3072]{1,0:T(8,128)(2,1)S(1)} %collective-permute-done.6.other.refs_5_), channel_id=1, source_target_pairs={{8,12},{10,14},{4,0},{6,2},{9,13},{11,15},{5,1},{7,3},{24,28},{26,... | collective-permute-start | bytes 1327112 | tf_op jit(solution)/shard_map/ppermute | solution.py:330
  47.6 1.6 %collective-permute-start.12 = (bf16[72,1536]{1,0:T(8,128)(2,1)S(1)}, bf16[72,1536]{1,0:T(8,128)(2,1)S(1)}, u32[]{:S(2)}, u32[]{:S(2)}) collective-permute-start(bf16[72,1536]{1,0:T(8,128)(2,1)S(1)} %get-tuple-element.81), channel_id=1, source_target_pairs={{0,2},{2,0},{4,6},{6,4},{8,10},{10,8},{12,14},{14,12},{1,3},{3,1},... | collective-permute-start | bytes 663560 | tf_op jit(solution)/shard_map/ppermute | solution.py:267
  49.2 6.0 %collective-permute-done.12.arrived = bf16[72,1536]{1,0:T(8,128)(2,1)S(1)} collective-permute-done((bf16[72,1536]{1,0:T(8,128)(2,1)S(1)}, bf16[72,1536]{1,0:T(8,128)(2,1)S(1)}, u32[]{:S(2)}, u32[]{:S(2)}) %collective-permute-start.12) | collective-permute-done | bytes 221216 | tf_op jit(solution)/shard_map/ppermute | solution.py:267
  56.5 2.5 %collective-permute-start.17 = (bf16[72,1536]{1,0:T(8,128)(2,1)S(1)}, bf16[72,1536]{1,0:T(8,128)(2,1)S(1)}, u32[]{:S(2)}, u32[]{:S(2)}) collective-permute-start(bf16[72,1536]{1,0:T(8,128)(2,1)S(1)} %add.13), channel_id=1, source_target_pairs={{0,4},{2,6},{4,12},{6,14},{8,0},{10,2},{12,8},{14,10},{1,5},{3,7},... | collective-permute-start | bytes 663560 | tf_op jit(solution)/shard_map/ppermute | solution.py:334
  61.3 3.5 %collective-permute-done.17.passed = bf16[72,1536]{1,0:T(8,128)(2,1)S(1)} collective-permute-done((bf16[72,1536]{1,0:T(8,128)(2,1)S(1)}, bf16[72,1536]{1,0:T(8,128)(2,1)S(1)}, u32[]{:S(2)}, u32[]{:S(2)}) %collective-permute-start.17) | collective-permute-done | bytes 221216 | tf_op jit(solution)/shard_map/ppermute | solution.py:334
  64.8 2.8 %collective-permute-done.16.arrived = bf16[72,1536]{1,0:T(8,128)(2,1)S(1)} collective-permute-done((bf16[72,1536]{1,0:T(8,128)(2,1)S(1)}, bf16[72,1536]{1,0:T(8,128)(2,1)S(1)}, u32[]{:S(2)}, u32[]{:S(2)}) %collective-permute-start.16) | collective-permute-done | bytes 221216 | tf_op jit(solution)/shard_map/ppermute | solution.py:267
  68.4 3.5 %grads.1 = (bf16[3072,256]{1,0:T(8,128)(2,1)}, bf16[3072,256]{1,0:T(8,128)(2,1)}, bf16[256,3072]{1,0:T(8,128)(2,1)}) custom-call(bf16[72,3072]{1,0:T(8,128)(2,1)S(1)} %get-tuple-element.88.mine.refs_0_, bf16[72,3072]{1,0:T(8,128)(2,1)S(1)} %collective-permute-done.2.other.refs_1_, bf16[72,3072]{1,0:T(8,128)(2,1)S(1)} %collective-permute-done.1.mine.refs_2_, ...), custom_call_target="tpu_custom_call" | custom-call | flops 1000 | bytes 1000 | tf_op jit(solution)/shard_map/grads/pallas_call | solution.py:101
  72.1 7.1 %collective-permute-done.19.last = bf16[72,1536]{1,0:T(8,128)(2,1)S(1)} collective-permute-done((bf16[72,1536]{1,0:T(8,128)(2,1)S(1)}, bf16[72,1536]{1,0:T(8,128)(2,1)S(1)}, u32[]{:S(2)}, u32[]{:S(2)}) %collective-permute-start.19) | collective-permute-done | bytes 221216 | tf_op jit(solution)/shard_map/ppermute | solution.py:270
  79.2 1.2 %finish.1 = bf16[128,3072]{1,0:T(8,128)(2,1)} custom-call(bf16[128,128]{1,0:T(8,128)(2,1)S(1)} %get-tuple-element.55.placing_t, f32[72,1536]{1,0:T(8,128)S(1)} %near.1, bf16[72,1536]{1,0:T(8,128)(2,1)S(1)} %collective-permute-done.19.last), custom_call_target="tpu_custom_call" | custom-call | flops 1000 | bytes 1000 | tf_op jit(solution)/shard_map/finish/pallas_call | solution.py:101
  (35 shorter events, 15.1 us)
Async XLA Ops:
  2.4 12.0 %collective-permute-start.2 = (bf16[72,3072]{1,0:T(8,128)(2,1)S(1)}, bf16[72,3072]{1,0:T(8,128)(2,1)S(1)}, u32[]{:S(2)}, u32[]{:S(2)}) collective-permute-start(bf16[72,3072]{1,0:T(8,128)(2,1)S(1)} %get-tuple-element.88.mine.refs_0_), channel_id=1, source_target_pairs={{0,2},{2,0},{4,6},{6,4},{8,10},{10,8},{12,14},{14,12},{1,3},{3,1},... | collective-permute-start | bytes 1327112 | tf_op jit(solution)/shard_map/ppermute | solution.py:267
  3.9 21.6 %collective-permute-start.1 = (bf16[72,3072]{1,0:T(8,128)(2,1)S(1)}, bf16[72,3072]{1,0:T(8,128)(2,1)S(1)}, u32[]{:S(2)}, u32[]{:S(2)}) collective-permute-start(bf16[72,3072]{1,0:T(8,128)(2,1)S(1)} %get-tuple-element.88.mine.refs_0_), channel_id=1, source_target_pairs={{0,4},{2,6},{4,0},{6,2},{8,12},{10,14},{12,8},{14,10},{1,5},{3,7},... | collective-permute-start | bytes 1327112 | tf_op jit(solution)/shard_map/ppermute | solution.py:270
  4.4 23.2 %collective-permute-start = (bf16[72,3072]{1,0:T(8,128)(2,1)S(1)}, bf16[72,3072]{1,0:T(8,128)(2,1)S(1)}, u32[]{:S(2)}, u32[]{:S(2)}) collective-permute-start(bf16[72,3072]{1,0:T(8,128)(2,1)S(1)} %get-tuple-element.88.mine.refs_0_), channel_id=1, source_target_pairs={{0,8},{2,10},{4,12},{6,14},{8,0},{10,2},{12,4},{14,6},{1,9},{3,11}... | collective-permute-start | bytes 1327112 | tf_op jit(solution)/shard_map/ppermute | solution.py:270
  15.5 1.4 %collective-permute-start.3 = (bf16[80,768]{1,0:T(8,128)(2,1)S(1)}, bf16[80,768]{1,0:T(8,128)(2,1)S(1)}, u32[]{:S(2)}, u32[]{:S(2)}) collective-permute-start(bf16[80,768]{1,0:T(8,128)(2,1)S(1)} %get-tuple-element.64), channel_id=1, source_target_pairs={{0,1},{1,0},{2,3},{3,2},{4,5},{5,4},{6,7},{7,6},{8,9},{9,8},{10,11... | collective-permute-start | bytes 368648 | tf_op jit(solution)/shard_map/ppermute | solution.py:309
  18.0 7.5 %collective-permute-start.4 = (bf16[72,1536]{1,0:T(8,128)(2,1)S(1)}, bf16[72,1536]{1,0:T(8,128)(2,1)S(1)}, u32[]{:S(2)}, u32[]{:S(2)}) collective-permute-start(bf16[72,1536]{1,0:T(8,128)(2,1)S(1)} %get-tuple-element.66), channel_id=1, source_target_pairs={{0,2},{2,0},{4,6},{6,4},{8,10},{10,8},{12,14},{14,12},{1,3},{3,1},... | collective-permute-start | bytes 663560 | tf_op jit(solution)/shard_map/ppermute | solution.py:267
  19.5 15.0 %collective-permute-start.7 = (bf16[72,3072]{1,0:T(8,128)(2,1)S(1)}, bf16[72,3072]{1,0:T(8,128)(2,1)S(1)}, u32[]{:S(2)}, u32[]{:S(2)}) collective-permute-start(bf16[72,3072]{1,0:T(8,128)(2,1)S(1)} %collective-permute-done.2.other.refs_1_), channel_id=1, source_target_pairs={{0,4},{2,6},{4,0},{6,2},{8,12},{10,14},{12,8},{14,10},{1,5},{3,7},... | collective-permute-start | bytes 1327112 | tf_op jit(solution)/shard_map/ppermute | solution.py:270
  27.6 11.3 %collective-permute-start.5 = (bf16[72,3072]{1,0:T(8,128)(2,1)S(1)}, bf16[72,3072]{1,0:T(8,128)(2,1)S(1)}, u32[]{:S(2)}, u32[]{:S(2)}) collective-permute-start(bf16[72,3072]{1,0:T(8,128)(2,1)S(1)} %get-tuple-element.88.mine.refs_0_), channel_id=1, source_target_pairs={{4,8},{6,10},{8,4},{10,6},{5,9},{7,11},{9,5},{11,7},{20,24},{22,26... | collective-permute-start | bytes 1327112 | tf_op jit(solution)/shard_map/ppermute | solution.py:327
  29.9 10.3 %collective-permute-start.6 = (bf16[72,3072]{1,0:T(8,128)(2,1)S(1)}, bf16[72,3072]{1,0:T(8,128)(2,1)S(1)}, u32[]{:S(2)}, u32[]{:S(2)}) collective-permute-start(bf16[72,3072]{1,0:T(8,128)(2,1)S(1)} %collective-permute-done.mine.refs_4_), channel_id=1, source_target_pairs={{0,2},{2,0},{4,6},{6,4},{8,10},{10,8},{12,14},{14,12},{1,3},{3,1},... | collective-permute-start | bytes 1327112 | tf_op jit(solution)/shard_map/ppermute | solution.py:267
  30.7 15.1 %collective-permute-start.9 = (bf16[72,3072]{1,0:T(8,128)(2,1)S(1)}, bf16[72,3072]{1,0:T(8,128)(2,1)S(1)}, u32[]{:S(2)}, u32[]{:S(2)}) collective-permute-start(bf16[72,3072]{1,0:T(8,128)(2,1)S(1)} %collective-permute-done.mine.refs_4_), channel_id=1, source_target_pairs={{8,12},{10,14},{4,0},{6,2},{9,13},{11,15},{5,1},{7,3},{24,28},{26,... | collective-permute-start | bytes 1327112 | tf_op jit(solution)/shard_map/ppermute | solution.py:330
  35.7 1.4 %collective-permute-start.8 = (bf16[80,768]{1,0:T(8,128)(2,1)S(1)}, bf16[80,768]{1,0:T(8,128)(2,1)S(1)}, u32[]{:S(2)}, u32[]{:S(2)}) collective-permute-start(bf16[80,768]{1,0:T(8,128)(2,1)S(1)} %get-tuple-element.72), channel_id=1, source_target_pairs={{0,1},{1,0},{2,3},{3,2},{4,5},{5,4},{6,7},{7,6},{8,9},{9,8},{10,11... | collective-permute-start | bytes 368648 | tf_op jit(solution)/shard_map/ppermute | solution.py:309
  38.2 7.5 %collective-permute-start.10 = (bf16[72,1536]{1,0:T(8,128)(2,1)S(1)}, bf16[72,1536]{1,0:T(8,128)(2,1)S(1)}, u32[]{:S(2)}, u32[]{:S(2)}) collective-permute-start(bf16[72,1536]{1,0:T(8,128)(2,1)S(1)} %get-tuple-element.73), channel_id=1, source_target_pairs={{0,2},{2,0},{4,6},{6,4},{8,10},{10,8},{12,14},{14,12},{1,3},{3,1},... | collective-permute-start | bytes 663560 | tf_op jit(solution)/shard_map/ppermute | solution.py:267
  40.3 14.9 %collective-permute-start.13 = (bf16[72,3072]{1,0:T(8,128)(2,1)S(1)}, bf16[72,3072]{1,0:T(8,128)(2,1)S(1)}, u32[]{:S(2)}, u32[]{:S(2)}) collective-permute-start(bf16[72,3072]{1,0:T(8,128)(2,1)S(1)} %collective-permute-done.2.other.refs_1_), channel_id=1, source_target_pairs={{4,8},{6,10},{8,4},{10,6},{5,9},{7,11},{9,5},{11,7},{20,24},{22,26... | collective-permute-start | bytes 1327112 | tf_op jit(solution)/shard_map/ppermute | solution.py:327
  42.6 12.6 %collective-permute-start.14 = (bf16[72,3072]{1,0:T(8,128)(2,1)S(1)}, bf16[72,3072]{1,0:T(8,128)(2,1)S(1)}, u32[]{:S(2)}, u32[]{:S(2)}) collective-permute-start(bf16[72,3072]{1,0:T(8,128)(2,1)S(1)} %collective-permute-done.6.other.refs_5_), channel_id=1, source_target_pairs={{8,12},{10,14},{4,0},{6,2},{9,13},{11,15},{5,1},{7,3},{24,28},{26,... | collective-permute-start | bytes 1327112 | tf_op jit(solution)/shard_map/ppermute | solution.py:330
  45.1 1.4 %collective-permute-start.11 = (bf16[80,768]{1,0:T(8,128)(2,1)S(1)}, bf16[80,768]{1,0:T(8,128)(2,1)S(1)}, u32[]{:S(2)}, u32[]{:S(2)}) collective-permute-start(bf16[80,768]{1,0:T(8,128)(2,1)S(1)} %get-tuple-element.79), channel_id=1, source_target_pairs={{0,1},{1,0},{2,3},{3,2},{4,5},{5,4},{6,7},{7,6},{8,9},{9,8},{10,11... | collective-permute-start | bytes 368648 | tf_op jit(solution)/shard_map/ppermute | solution.py:309
  47.6 7.6 %collective-permute-start.12 = (bf16[72,1536]{1,0:T(8,128)(2,1)S(1)}, bf16[72,1536]{1,0:T(8,128)(2,1)S(1)}, u32[]{:S(2)}, u32[]{:S(2)}) collective-permute-start(bf16[72,1536]{1,0:T(8,128)(2,1)S(1)} %get-tuple-element.81), channel_id=1, source_target_pairs={{0,2},{2,0},{4,6},{6,4},{8,10},{10,8},{12,14},{14,12},{1,3},{3,1},... | collective-permute-start | bytes 663560 | tf_op jit(solution)/shard_map/ppermute | solution.py:267
  56.4 2.5 %collective-permute-start.15 = (bf16[80,768]{1,0:T(8,128)(2,1)S(1)}, bf16[80,768]{1,0:T(8,128)(2,1)S(1)}, u32[]{:S(2)}, u32[]{:S(2)}) collective-permute-start(bf16[80,768]{1,0:T(8,128)(2,1)S(1)} %get-tuple-element.85), channel_id=1, source_target_pairs={{0,1},{1,0},{2,3},{3,2},{4,5},{5,4},{6,7},{7,6},{8,9},{9,8},{10,11... | collective-permute-start | bytes 368648 | tf_op jit(solution)/shard_map/ppermute | solution.py:309
  56.5 8.3 %collective-permute-start.17 = (bf16[72,1536]{1,0:T(8,128)(2,1)S(1)}, bf16[72,1536]{1,0:T(8,128)(2,1)S(1)}, u32[]{:S(2)}, u32[]{:S(2)}) collective-permute-start(bf16[72,1536]{1,0:T(8,128)(2,1)S(1)} %add.13), channel_id=1, source_target_pairs={{0,4},{2,6},{4,12},{6,14},{8,0},{10,2},{12,8},{14,10},{1,5},{3,7},... | collective-permute-start | bytes 663560 | tf_op jit(solution)/shard_map/ppermute | solution.py:334
  60.1 7.6 %collective-permute-start.16 = (bf16[72,1536]{1,0:T(8,128)(2,1)S(1)}, bf16[72,1536]{1,0:T(8,128)(2,1)S(1)}, u32[]{:S(2)}, u32[]{:S(2)}) collective-permute-start(bf16[72,1536]{1,0:T(8,128)(2,1)S(1)} %get-tuple-element.87), channel_id=1, source_target_pairs={{0,2},{2,0},{4,6},{6,4},{8,10},{10,8},{12,14},{14,12},{1,3},{3,1},... | collective-permute-start | bytes 663560 | tf_op jit(solution)/shard_map/ppermute | solution.py:267
  61.1 10.8 %collective-permute-start.18 = (bf16[72,1536]{1,0:T(8,128)(2,1)S(1)}, bf16[72,1536]{1,0:T(8,128)(2,1)S(1)}, u32[]{:S(2)}, u32[]{:S(2)}) collective-permute-start(bf16[72,1536]{1,0:T(8,128)(2,1)S(1)} %add.12), channel_id=1, source_target_pairs={{0,4},{2,6},{4,0},{6,2},{8,12},{10,14},{12,8},{14,10},{1,5},{3,7},... | collective-permute-start | bytes 663560 | tf_op jit(solution)/shard_map/ppermute | solution.py:270
  67.7 11.5 %collective-permute-start.19 = (bf16[72,1536]{1,0:T(8,128)(2,1)S(1)}, bf16[72,1536]{1,0:T(8,128)(2,1)S(1)}, u32[]{:S(2)}, u32[]{:S(2)}) collective-permute-start(bf16[72,1536]{1,0:T(8,128)(2,1)S(1)} %last.1), channel_id=1, source_target_pairs={{0,12},{2,14},{4,8},{6,10},{8,4},{10,6},{12,0},{14,2},{1,13},{3,15... | collective-permute-start | bytes 663560 | tf_op jit(solution)/shard_map/ppermute | solution.py:270

commit v6 on v5

--- a/solution.py
+++ b/solution.py
@@ -1,3 +1,5 @@
+import functools
+
 import jax
 import jax.numpy as jnp
 from jax import lax
@@ -178,7 +180,7 @@
     return jnp.concatenate([main[:, :half], last[:, :half], main[:, half:], last[:, half:]], axis=0)
 
 
-def back_kernel(part, arrived, w_gate, w_up, hidden, d_pre, term, sent):
+def back_kernel(part, arrived, w_gate, w_up, hidden, d_pre, term, *sent):
     width = w_gate.shape[1]
     sums = part[...] + arrived[...].astype(F32)
     z_gate, z_up, d_hidden = (sums[:, i * width : (i + 1) * width] for i in range(3))
@@ -194,7 +196,11 @@
     d_pre[:, width:] = d_up
     value = mul(d_gate, w_gate[...], 1, 1) + mul(d_up, w_up[...], 1, 1)
     term[...] = folded(value[0:MAIN], value[2 * MAIN : 2 * MAIN + TAIL])
-    sent[...] = folded(value[MAIN : 2 * MAIN], value[2 * MAIN + 8 : 2 * MAIN + 8 + TAIL]).astype(BF16)
+    other = folded(value[MAIN : 2 * MAIN], value[2 * MAIN + 8 : 2 * MAIN + 8 + TAIL]).astype(BF16)
+    at = 0
+    for piece in sent:
+        piece[...] = other[:, at : at + piece.shape[1]]
+        at += piece.shape[1]
 
 
 def add_kernel(term, arrived, total):
@@ -206,9 +212,10 @@
     return (line == 1) | (line == 2)
 
 
-def last_kernel(term, arrived, passed, total):
-    value = term[...] + arrived[...].astype(F32)
-    total[...] = jnp.where(is_inner(), value + passed[...].astype(F32), value).astype(BF16)
+def last_kernel(start, term, arrived, passed, total):
+    columns = slice(start, start + total.shape[1])
+    value = term[:, columns] + arrived[...].astype(F32)
+    total[...] = jnp.where(is_inner(), value + passed[:, columns].astype(F32), value).astype(BF16)
 
 
 def near_kernel(first, second, passed, total):
@@ -216,8 +223,8 @@
     total[...] = jnp.where(is_inner(), value, value + passed[...].astype(F32))
 
 
-def finish_kernel(placing_t, near, last, grad_in):
-    total = near[...] + last[...].astype(F32)
+def finish_kernel(placing_t, near, left, right, grad_in):
+    total = near[...] + jnp.concatenate([left[...], right[...]], axis=1).astype(F32)
     half = total.shape[1]
     placing = placing_t[:, :CAP]
     grad_in[:, :half] = mul(placing, total[:CAP].astype(BF16)).astype(BF16)
@@ -308,15 +315,11 @@
         )
         return part, lax.ppermute(sent, "tensor", [(0, 1), (1, 0)])
 
-    def back(part, arrived):
+    def back(part, arrived, *pieces):
         return call(
             back_kernel,
-            (
-                struct(GROUP, width, BF16),
-                struct(GROUP, 2 * width, BF16),
-                struct(BLOCK, half, F32),
-                struct(BLOCK, half, BF16),
-            ),
+            (struct(GROUP, width, BF16), struct(GROUP, 2 * width, BF16), struct(BLOCK, half, F32))
+            + tuple(struct(BLOCK, size, BF16) for size in pieces or (half,)),
             part, arrived, gate, up, name="back",
         )
 
@@ -340,29 +343,36 @@
     one_y = along(own_y, 1)
     q0 = add(t0, s0)
     two, one, q0 = lax.optimization_barrier((two, one, q0))
+    two_y = across(two)
+    outer = ends(two)
     inner = middle(after(own, two))
-    outer = ends(two)
-    two_y = across(two)
     h1, d1, t1, s1 = back(*front(one, one_y))
     q1 = add(t1, s1)
     inner, two_y, s1 = lax.optimization_barrier((inner, two_y, s1))
+    outer_y = ends(two_y)
     inner_y = middle(after(own_y, inner))
-    outer_y = ends(two_y)
     three = inner + outer
     three_y = inner_y + outer_y
     part2, swap2 = front(two, two_y)
-    h2, d2, t2, s2 = back(after(part2, three, q1), swap2)
-    q2 = add(t2, s2)
+    h2, d2, t2, s2 = back(after(part2, three), swap2)
+    q2 = add(t2, after(s2, q1))
     got = relay(q2)
-    h3, d3, t3, s3 = back(*front(after(three, q2), three_y))
-    r1 = along(after(q1, s3), 1)
-    q3 = call(last_kernel, struct(BLOCK, half, BF16), t3, across(s3), got, name="last")
-    r3 = along(q3, 3)
+    large = half * 2 // 3
+    h3, d3, t3, *s3 = back(*front(three, three_y), large, half - large)
+    r1 = along(after(q1, *s3), 1)
+    q3 = [
+        call(
+            functools.partial(last_kernel, at), struct(*value.shape, BF16),
+            t3, across(value), got, name="last",
+        )
+        for at, value in zip((0, large), s3)
+    ]
+    r3 = [along(value, 3) for value in q3]
 
     grads = call(
         grads_kernel,
         (struct(features, width, BF16), struct(features, width, BF16), struct(width, features, BF16)),
-        after(own, q3), own_y, one, one_y, two, two_y, three, three_y, h0, h1, h2, h3, d0, d1, d2, d3,
+        after(own, q3[1]), own_y, one, one_y, two, two_y, three, three_y, h0, h1, h2, h3, d0, d1, d2, d3,
         name="grads",
         out_specs=(pl.BlockSpec(memory_space=pltpu.HBM),) * 3,
         scratch_shapes=[
@@ -375,7 +385,7 @@
     grads, r1 = lax.optimization_barrier((grads, r1))
     near = call(near_kernel, struct(BLOCK, half, F32), q0, r1, got, name="near")
     grad_in = call(
-        finish_kernel, struct(tokens.shape[0], features, BF16), placing_t, near, after(r3, near), name="finish"
+        finish_kernel, struct(tokens.shape[0], features, BF16), placing_t, near, *after(r3, near), name="finish"
     )
     return (grad_in,) + tuple(grads)
 

time: 80.6 us -> 78 us (0.968)
  the two profiles are of different devices: /device:TPU:8 before, /device:TPU:0 now
where the time goes in v6:
time: 78 us; the launch traced here: 77.8 us
  waiting for transfers between devices  32.5 us (42%)
  starting transfers between devices  26.2 us (34%)
  Pallas kernels  18.1 us (23%)
  between operations  0.81 us (1%)
    pallas_call x18, Pallas kernels, call(): pl.pallas_call(kernel, out_shape=outs, name=name, compiler_params=pltpu.C...  18.1 us
    ppermute x7, waiting for transfers between devices, across(): return lax.ppermute(value, 'expert', [(i, i ^ 1) for i in range(8)])  15.4 us
    ppermute x6, starting transfers between devices, along(): lax.ppermute(value, 'expert', [(i, i ^ 2 * distance) for i in range(8)])  11 us
    ppermute x6, waiting for transfers between devices, along(): lax.ppermute(value, 'expert', [(i, i ^ 2 * distance) for i in range(8)])  9.19 us
    ppermute x7, starting transfers between devices, across(): return lax.ppermute(value, 'expert', [(i, i ^ 1) for i in range(8)])  8.54 us
    ppermute x2, waiting for transfers between devices, ends(): return lax.ppermute(value, 'expert', [(4, 6), (5, 7), (2, 0), (3, 1)])  4.33 us
    ppermute x4, waiting for transfers between devices, front(): return (part, lax.ppermute(sent, 'tensor', [(0, 1), (1, 0)]))  2.65 us
    ppermute x2, starting transfers between devices, ends(): return lax.ppermute(value, 'expert', [(4, 6), (5, 7), (2, 0), (3, 1)])  2.57 us
  transfers between devices with their start and end apart: 22, of which 12 were waited for; matrix products, arithmetic and copies ran while one was open for 0% of the time, Pallas kernels for 19%

profile of v6, /device:TPU:0, one launch (start us, length us, event | category | flops | bytes accessed | tf_op | source)
XLA Modules:
  0.0 77.8 jit_solution(6344229594427022209)
XLA Ops:
  0.6 1.7 %place.1 = (bf16[72,3072]{1,0:T(8,128)(2,1)S(1)}, bf16[128,128]{1,0:T(8,128)(2,1)S(1)}) custom-call(bf16[128,3072]{1,0:T(8,128)(2,1)} %tokens_at.1, bf16[128,3072]{1,0:T(8,128)(2,1)} %grad_out_at.1, s32[2,128]{1,0:T(2,128)} %bitcast.2, f32[2,128]{1,0:T(2,128)} %bitcast.3), custom_call_target="tpu_custom_call" | custom-call | flops 1000 | bytes 1000 | tf_op jit(solution)/shard_map/place/pallas_call | solution.py:103
  2.3 3.0 %collective-permute-start.2 = (bf16[72,3072]{1,0:T(8,128)(2,1)S(1)}, bf16[72,3072]{1,0:T(8,128)(2,1)S(1)}, u32[]{:S(2)}, u32[]{:S(2)}) collective-permute-start(bf16[72,3072]{1,0:T(8,128)(2,1)S(1)} %get-tuple-element.90.mine.refs_0_), channel_id=1, source_target_pairs={{0,2},{2,0},{4,6},{6,4},{8,10},{10,8},{12,14},{14,12},{1,3},{3,1},... | collective-permute-start | bytes 1327112 | tf_op jit(solution)/shard_map/ppermute | solution.py:274
  5.4 1.6 %collective-permute-start.1 = (bf16[72,3072]{1,0:T(8,128)(2,1)S(1)}, bf16[72,3072]{1,0:T(8,128)(2,1)S(1)}, u32[]{:S(2)}, u32[]{:S(2)}) collective-permute-start(bf16[72,3072]{1,0:T(8,128)(2,1)S(1)} %get-tuple-element.90.mine.refs_0_), channel_id=1, source_target_pairs={{0,4},{2,6},{4,0},{6,2},{8,12},{10,14},{12,8},{14,10},{1,5},{3,7},... | collective-permute-start | bytes 1327112 | tf_op jit(solution)/shard_map/ppermute | solution.py:277
  7.0 2.6 %collective-permute-start = (bf16[72,3072]{1,0:T(8,128)(2,1)S(1)}, bf16[72,3072]{1,0:T(8,128)(2,1)S(1)}, u32[]{:S(2)}, u32[]{:S(2)}) collective-permute-start(bf16[72,3072]{1,0:T(8,128)(2,1)S(1)} %get-tuple-element.90.mine.refs_0_), channel_id=1, source_target_pairs={{0,8},{2,10},{4,12},{6,14},{8,0},{10,2},{12,4},{14,6},{1,9},{3,11}... | collective-permute-start | bytes 1327112 | tf_op jit(solution)/shard_map/ppermute | solution.py:277
  9.6 2.4 %load.1 = (bf16[3072,256]{1,0:T(8,128)(2,1)S(1)}, bf16[3072,256]{1,0:T(8,128)(2,1)S(1)}, bf16[256,3072]{1,0:T(8,128)(2,1)S(1)}) custom-call(bf16[3072,256]{1,0:T(8,128)(2,1)} %refs_0_, bf16[3072,256]{1,0:T(8,128)(2,1)} %refs_1_, bf16[256,3072]{1,0:T(8,128)(2,1)} %refs_2_), custom_call_target="tpu_custom_call" | custom-call | flops 1000 | bytes 1000 | tf_op jit(solution)/shard_map/load/pallas_call | solution.py:103
  11.9 3.6 %collective-permute-done.2.other.refs_1_ = bf16[72,3072]{1,0:T(8,128)(2,1)S(1)} collective-permute-done((bf16[72,3072]{1,0:T(8,128)(2,1)S(1)}, bf16[72,3072]{1,0:T(8,128)(2,1)S(1)}, u32[]{:S(2)}, u32[]{:S(2)}) %collective-permute-start.2) | collective-permute-done | bytes 442400 | tf_op jit(solution)/shard_map/ppermute | solution.py:274
  16.8 1.3 %collective-permute-done.3.arrived = bf16[80,768]{1,0:T(8,128)(2,1)S(1)} collective-permute-done((bf16[80,768]{1,0:T(8,128)(2,1)S(1)}, bf16[80,768]{1,0:T(8,128)(2,1)S(1)}, u32[]{:S(2)}, u32[]{:S(2)}) %collective-permute-start.3) | collective-permute-done | bytes 122912 | tf_op jit(solution)/shard_map/ppermute | solution.py:316
  19.2 1.8 %collective-permute-start.4 = (bf16[72,1536]{1,0:T(8,128)(2,1)S(1)}, bf16[72,1536]{1,0:T(8,128)(2,1)S(1)}, u32[]{:S(2)}, u32[]{:S(2)}) collective-permute-start(bf16[72,1536]{1,0:T(8,128)(2,1)S(1)} %get-tuple-element.68), channel_id=1, source_target_pairs={{0,2},{2,0},{4,6},{6,4},{8,10},{10,8},{12,14},{14,12},{1,3},{3,1},... | collective-permute-start | bytes 663560 | tf_op jit(solution)/shard_map/ppermute | solution.py:274
  21.0 1.6 %collective-permute-start.7 = (bf16[72,3072]{1,0:T(8,128)(2,1)S(1)}, bf16[72,3072]{1,0:T(8,128)(2,1)S(1)}, u32[]{:S(2)}, u32[]{:S(2)}) collective-permute-start(bf16[72,3072]{1,0:T(8,128)(2,1)S(1)} %collective-permute-done.2.other.refs_1_), channel_id=1, source_target_pairs={{0,4},{2,6},{4,0},{6,2},{8,12},{10,14},{12,8},{14,10},{1,5},{3,7},... | collective-permute-start | bytes 1327112 | tf_op jit(solution)/shard_map/ppermute | solution.py:277
  22.6 4.2 %collective-permute-done.4.arrived = bf16[72,1536]{1,0:T(8,128)(2,1)S(1)} collective-permute-done((bf16[72,1536]{1,0:T(8,128)(2,1)S(1)}, bf16[72,1536]{1,0:T(8,128)(2,1)S(1)}, u32[]{:S(2)}, u32[]{:S(2)}) %collective-permute-start.4) | collective-permute-done | bytes 221216 | tf_op jit(solution)/shard_map/ppermute | solution.py:274
  29.3 1.3 %collective-permute-start.9 = (bf16[72,3072]{1,0:T(8,128)(2,1)S(1)}, bf16[72,3072]{1,0:T(8,128)(2,1)S(1)}, u32[]{:S(2)}, u32[]{:S(2)}) collective-permute-start(bf16[72,3072]{1,0:T(8,128)(2,1)S(1)} %collective-permute-done.mine.refs_4_), channel_id=1, source_target_pairs={{8,12},{10,14},{4,0},{6,2},{9,13},{11,15},{5,1},{7,3},{24,28},{26,... | collective-permute-start | bytes 1327112 | tf_op jit(solution)/shard_map/ppermute | solution.py:333
  30.6 6.7 %collective-permute-done.7.other.refs_3_ = bf16[72,3072]{1,0:T(8,128)(2,1)S(1)} collective-permute-done((bf16[72,3072]{1,0:T(8,128)(2,1)S(1)}, bf16[72,3072]{1,0:T(8,128)(2,1)S(1)}, u32[]{:S(2)}, u32[]{:S(2)}) %collective-permute-start.7) | collective-permute-done | bytes 442400 | tf_op jit(solution)/shard_map/ppermute | solution.py:277
  38.6 1.3 %collective-permute-done.8.arrived = bf16[80,768]{1,0:T(8,128)(2,1)S(1)} collective-permute-done((bf16[80,768]{1,0:T(8,128)(2,1)S(1)}, bf16[80,768]{1,0:T(8,128)(2,1)S(1)}, u32[]{:S(2)}, u32[]{:S(2)}) %collective-permute-start.8) | collective-permute-done | bytes 122912 | tf_op jit(solution)/shard_map/ppermute | solution.py:316
  41.7 1.3 %collective-permute-start.11 = (bf16[72,3072]{1,0:T(8,128)(2,1)S(1)}, bf16[72,3072]{1,0:T(8,128)(2,1)S(1)}, u32[]{:S(2)}, u32[]{:S(2)}) collective-permute-start(bf16[72,3072]{1,0:T(8,128)(2,1)S(1)} %collective-permute-done.6.other.refs_5_), channel_id=1, source_target_pairs={{8,12},{10,14},{4,0},{6,2},{9,13},{11,15},{5,1},{7,3},{24,28},{26,... | collective-permute-start | bytes 1327112 | tf_op jit(solution)/shard_map/ppermute | solution.py:333
  44.4 6.1 %collective-permute-done.15.arrived = bf16[72,1536]{1,0:T(8,128)(2,1)S(1)} collective-permute-done((bf16[72,1536]{1,0:T(8,128)(2,1)S(1)}, bf16[72,1536]{1,0:T(8,128)(2,1)S(1)}, u32[]{:S(2)}, u32[]{:S(2)}) %collective-permute-start.15) | collective-permute-done | bytes 221216 | tf_op jit(solution)/shard_map/ppermute | solution.py:274
  52.2 4.3 %collective-permute-done.11 = bf16[72,3072]{1,0:T(8,128)(2,1)S(1)} collective-permute-done((bf16[72,3072]{1,0:T(8,128)(2,1)S(1)}, bf16[72,3072]{1,0:T(8,128)(2,1)S(1)}, u32[]{:S(2)}, u32[]{:S(2)}) %collective-permute-start.11) | collective-permute-done | bytes 442400 | tf_op jit(solution)/shard_map/ppermute | solution.py:333
  58.6 2.4 %collective-permute-start.17 = (bf16[72,1536]{1,0:T(8,128)(2,1)S(1)}, bf16[72,1536]{1,0:T(8,128)(2,1)S(1)}, u32[]{:S(2)}, u32[]{:S(2)}) collective-permute-start(bf16[72,1536]{1,0:T(8,128)(2,1)S(1)} %add.13), channel_id=1, source_target_pairs={{0,4},{2,6},{4,12},{6,14},{8,0},{10,2},{12,8},{14,10},{1,5},{3,7},... | collective-permute-start | bytes 663560 | tf_op jit(solution)/shard_map/ppermute | solution.py:337
  63.0 1.3 %collective-permute-start.18 = (bf16[72,1536]{1,0:T(8,128)(2,1)S(1)}, bf16[72,1536]{1,0:T(8,128)(2,1)S(1)}, u32[]{:S(2)}, u32[]{:S(2)}) collective-permute-start(bf16[72,1536]{1,0:T(8,128)(2,1)S(1)} %add.12), channel_id=1, source_target_pairs={{0,4},{2,6},{4,0},{6,2},{8,12},{10,14},{12,8},{14,10},{1,5},{3,7},... | collective-permute-start | bytes 663560 | tf_op jit(solution)/shard_map/ppermute | solution.py:277
  64.3 1.5 %collective-permute-start.13 = (bf16[72,512]{1,0:T(8,128)(2,1)S(1)}, bf16[72,512]{1,0:T(8,128)(2,1)S(1)}, u32[]{:S(2)}, u32[]{:S(2)}) collective-permute-start(bf16[72,512]{1,0:T(8,128)(2,1)S(1)} %get-tuple-element.82), channel_id=1, source_target_pairs={{0,2},{2,0},{4,6},{6,4},{8,10},{10,8},{12,14},{14,12},{1,3},{3,1},... | collective-permute-start | bytes 221192 | tf_op jit(solution)/shard_map/ppermute | solution.py:274
  67.6 2.6 %collective-permute-start.20 = (bf16[72,1024]{1,0:T(8,128)(2,1)S(1)}, bf16[72,1024]{1,0:T(8,128)(2,1)S(1)}, u32[]{:S(2)}, u32[]{:S(2)}) collective-permute-start(bf16[72,1024]{1,0:T(8,128)(2,1)S(1)} %last.3), channel_id=1, source_target_pairs={{0,12},{2,14},{4,8},{6,10},{8,4},{10,6},{12,0},{14,2},{1,13},{3,15... | collective-permute-start | bytes 442376 | tf_op jit(solution)/shard_map/ppermute | solution.py:277
  70.3 1.4 %collective-permute-start.21 = (bf16[72,512]{1,0:T(8,128)(2,1)S(1)}, bf16[72,512]{1,0:T(8,128)(2,1)S(1)}, u32[]{:S(2)}, u32[]{:S(2)}) collective-permute-start(bf16[72,512]{1,0:T(8,128)(2,1)S(1)} %last.2), channel_id=1, source_target_pairs={{0,12},{2,14},{4,8},{6,10},{8,4},{10,6},{12,0},{14,2},{1,13},{3,15... | collective-permute-start | bytes 221192 | tf_op jit(solution)/shard_map/ppermute | solution.py:277
  71.6 3.5 %grads.1 = (bf16[3072,256]{1,0:T(8,128)(2,1)}, bf16[3072,256]{1,0:T(8,128)(2,1)}, bf16[256,3072]{1,0:T(8,128)(2,1)}) custom-call(bf16[72,3072]{1,0:T(8,128)(2,1)S(1)} %get-tuple-element.90.mine.refs_0_, bf16[72,3072]{1,0:T(8,128)(2,1)S(1)} %collective-permute-done.2.other.refs_1_, bf16[72,3072]{1,0:T(8,128)(2,1)S(1)} %collective-permute-done.1.mine.refs_2_, ...), custom_call_target="tpu_custom_call" | custom-call | flops 1000 | bytes 1000 | tf_op jit(solution)/shard_map/grads/pallas_call | solution.py:103
  75.2 1.3 %collective-permute-done.21.right = bf16[72,512]{1,0:T(8,128)(2,1)S(1)} collective-permute-done((bf16[72,512]{1,0:T(8,128)(2,1)S(1)}, bf16[72,512]{1,0:T(8,128)(2,1)S(1)}, u32[]{:S(2)}, u32[]{:S(2)}) %collective-permute-start.21) | collective-permute-done | bytes 73760 | tf_op jit(solution)/shard_map/ppermute | solution.py:277
  76.5 1.2 %finish.1 = bf16[128,3072]{1,0:T(8,128)(2,1)} custom-call(bf16[128,128]{1,0:T(8,128)(2,1)S(1)} %get-tuple-element.57.placing_t, f32[72,1536]{1,0:T(8,128)S(1)} %near.1, bf16[72,1024]{1,0:T(8,128)(2,1)S(1)} %collective-permute-done.20.left, bf16[72,512]{1,0:T(8,128)(2,1)S(1)} %collective-permute-done.21.right), custom_call_target="tpu_custom_call" | custom-call | flops 1000 | bytes 1000 | tf_op jit(solution)/shard_map/finish/pallas_call | solution.py:103
  (40 shorter events, 16.9 us)
Async XLA Ops:
  2.3 13.2 %collective-permute-start.2 = (bf16[72,3072]{1,0:T(8,128)(2,1)S(1)}, bf16[72,3072]{1,0:T(8,128)(2,1)S(1)}, u32[]{:S(2)}, u32[]{:S(2)}) collective-permute-start(bf16[72,3072]{1,0:T(8,128)(2,1)S(1)} %get-tuple-element.90.mine.refs_0_), channel_id=1, source_target_pairs={{0,2},{2,0},{4,6},{6,4},{8,10},{10,8},{12,14},{14,12},{1,3},{3,1},... | collective-permute-start | bytes 1327112 | tf_op jit(solution)/shard_map/ppermute | solution.py:274
  5.4 22.6 %collective-permute-start.1 = (bf16[72,3072]{1,0:T(8,128)(2,1)S(1)}, bf16[72,3072]{1,0:T(8,128)(2,1)S(1)}, u32[]{:S(2)}, u32[]{:S(2)}) collective-permute-start(bf16[72,3072]{1,0:T(8,128)(2,1)S(1)} %get-tuple-element.90.mine.refs_0_), channel_id=1, source_target_pairs={{0,4},{2,6},{4,0},{6,2},{8,12},{10,14},{12,8},{14,10},{1,5},{3,7},... | collective-permute-start | bytes 1327112 | tf_op jit(solution)/shard_map/ppermute | solution.py:277
  7.0 21.0 %collective-permute-start = (bf16[72,3072]{1,0:T(8,128)(2,1)S(1)}, bf16[72,3072]{1,0:T(8,128)(2,1)S(1)}, u32[]{:S(2)}, u32[]{:S(2)}) collective-permute-start(bf16[72,3072]{1,0:T(8,128)(2,1)S(1)} %get-tuple-element.90.mine.refs_0_), channel_id=1, source_target_pairs={{0,8},{2,10},{4,12},{6,14},{8,0},{10,2},{12,4},{14,6},{1,9},{3,11}... | collective-permute-start | bytes 1327112 | tf_op jit(solution)/shard_map/ppermute | solution.py:277
  16.7 1.4 %collective-permute-start.3 = (bf16[80,768]{1,0:T(8,128)(2,1)S(1)}, bf16[80,768]{1,0:T(8,128)(2,1)S(1)}, u32[]{:S(2)}, u32[]{:S(2)}) collective-permute-start(bf16[80,768]{1,0:T(8,128)(2,1)S(1)} %get-tuple-element.66), channel_id=1, source_target_pairs={{0,1},{1,0},{2,3},{3,2},{4,5},{5,4},{6,7},{7,6},{8,9},{9,8},{10,11... | collective-permute-start | bytes 368648 | tf_op jit(solution)/shard_map/ppermute | solution.py:316
  19.2 7.6 %collective-permute-start.4 = (bf16[72,1536]{1,0:T(8,128)(2,1)S(1)}, bf16[72,1536]{1,0:T(8,128)(2,1)S(1)}, u32[]{:S(2)}, u32[]{:S(2)}) collective-permute-start(bf16[72,1536]{1,0:T(8,128)(2,1)S(1)} %get-tuple-element.68), channel_id=1, source_target_pairs={{0,2},{2,0},{4,6},{6,4},{8,10},{10,8},{12,14},{14,12},{1,3},{3,1},... | collective-permute-start | bytes 663560 | tf_op jit(solution)/shard_map/ppermute | solution.py:274
  21.0 16.3 %collective-permute-start.7 = (bf16[72,3072]{1,0:T(8,128)(2,1)S(1)}, bf16[72,3072]{1,0:T(8,128)(2,1)S(1)}, u32[]{:S(2)}, u32[]{:S(2)}) collective-permute-start(bf16[72,3072]{1,0:T(8,128)(2,1)S(1)} %collective-permute-done.2.other.refs_1_), channel_id=1, source_target_pairs={{0,4},{2,6},{4,0},{6,2},{8,12},{10,14},{12,8},{14,10},{1,5},{3,7},... | collective-permute-start | bytes 1327112 | tf_op jit(solution)/shard_map/ppermute | solution.py:277
  28.0 13.0 %collective-permute-start.5 = (bf16[72,3072]{1,0:T(8,128)(2,1)S(1)}, bf16[72,3072]{1,0:T(8,128)(2,1)S(1)}, u32[]{:S(2)}, u32[]{:S(2)}) collective-permute-start(bf16[72,3072]{1,0:T(8,128)(2,1)S(1)} %get-tuple-element.90.mine.refs_0_), channel_id=1, source_target_pairs={{4,8},{6,10},{8,4},{10,6},{5,9},{7,11},{9,5},{11,7},{20,24},{22,26... | collective-permute-start | bytes 1327112 | tf_op jit(solution)/shard_map/ppermute | solution.py:330
  28.6 12.3 %collective-permute-start.6 = (bf16[72,3072]{1,0:T(8,128)(2,1)S(1)}, bf16[72,3072]{1,0:T(8,128)(2,1)S(1)}, u32[]{:S(2)}, u32[]{:S(2)}) collective-permute-start(bf16[72,3072]{1,0:T(8,128)(2,1)S(1)} %collective-permute-done.mine.refs_4_), channel_id=1, source_target_pairs={{0,2},{2,0},{4,6},{6,4},{8,10},{10,8},{12,14},{14,12},{1,3},{3,1},... | collective-permute-start | bytes 1327112 | tf_op jit(solution)/shard_map/ppermute | solution.py:274
  29.3 21.3 %collective-permute-start.9 = (bf16[72,3072]{1,0:T(8,128)(2,1)S(1)}, bf16[72,3072]{1,0:T(8,128)(2,1)S(1)}, u32[]{:S(2)}, u32[]{:S(2)}) collective-permute-start(bf16[72,3072]{1,0:T(8,128)(2,1)S(1)} %collective-permute-done.mine.refs_4_), channel_id=1, source_target_pairs={{8,12},{10,14},{4,0},{6,2},{9,13},{11,15},{5,1},{7,3},{24,28},{26,... | collective-permute-start | bytes 1327112 | tf_op jit(solution)/shard_map/ppermute | solution.py:333
  38.5 1.4 %collective-permute-start.8 = (bf16[80,768]{1,0:T(8,128)(2,1)S(1)}, bf16[80,768]{1,0:T(8,128)(2,1)S(1)}, u32[]{:S(2)}, u32[]{:S(2)}) collective-permute-start(bf16[80,768]{1,0:T(8,128)(2,1)S(1)} %get-tuple-element.74), channel_id=1, source_target_pairs={{0,1},{1,0},{2,3},{3,2},{4,5},{5,4},{6,7},{7,6},{8,9},{9,8},{10,11... | collective-permute-start | bytes 368648 | tf_op jit(solution)/shard_map/ppermute | solution.py:316
  41.0 11.2 %collective-permute-start.10 = (bf16[72,3072]{1,0:T(8,128)(2,1)S(1)}, bf16[72,3072]{1,0:T(8,128)(2,1)S(1)}, u32[]{:S(2)}, u32[]{:S(2)}) collective-permute-start(bf16[72,3072]{1,0:T(8,128)(2,1)S(1)} %collective-permute-done.2.other.refs_1_), channel_id=1, source_target_pairs={{4,8},{6,10},{8,4},{10,6},{5,9},{7,11},{9,5},{11,7},{20,24},{22,26... | collective-permute-start | bytes 1327112 | tf_op jit(solution)/shard_map/ppermute | solution.py:330
  41.7 14.8 %collective-permute-start.11 = (bf16[72,3072]{1,0:T(8,128)(2,1)S(1)}, bf16[72,3072]{1,0:T(8,128)(2,1)S(1)}, u32[]{:S(2)}, u32[]{:S(2)}) collective-permute-start(bf16[72,3072]{1,0:T(8,128)(2,1)S(1)} %collective-permute-done.6.other.refs_5_), channel_id=1, source_target_pairs={{8,12},{10,14},{4,0},{6,2},{9,13},{11,15},{5,1},{7,3},{24,28},{26,... | collective-permute-start | bytes 1327112 | tf_op jit(solution)/shard_map/ppermute | solution.py:333
  43.0 7.5 %collective-permute-start.15 = (bf16[72,1536]{1,0:T(8,128)(2,1)S(1)}, bf16[72,1536]{1,0:T(8,128)(2,1)S(1)}, u32[]{:S(2)}, u32[]{:S(2)}) collective-permute-start(bf16[72,1536]{1,0:T(8,128)(2,1)S(1)} %get-tuple-element.75), channel_id=1, source_target_pairs={{0,2},{2,0},{4,6},{6,4},{8,10},{10,8},{12,14},{14,12},{1,3},{3,1},... | collective-permute-start | bytes 663560 | tf_op jit(solution)/shard_map/ppermute | solution.py:274
  44.3 6.4 %collective-permute-start.14 = (bf16[80,768]{1,0:T(8,128)(2,1)S(1)}, bf16[80,768]{1,0:T(8,128)(2,1)S(1)}, u32[]{:S(2)}, u32[]{:S(2)}) collective-permute-start(bf16[80,768]{1,0:T(8,128)(2,1)S(1)} %get-tuple-element.85), channel_id=1, source_target_pairs={{0,1},{1,0},{2,3},{3,2},{4,5},{5,4},{6,7},{7,6},{8,9},{9,8},{10,11... | collective-permute-start | bytes 368648 | tf_op jit(solution)/shard_map/ppermute | solution.py:316
  51.8 6.7 %collective-permute-start.16 = (bf16[72,1536]{1,0:T(8,128)(2,1)S(1)}, bf16[72,1536]{1,0:T(8,128)(2,1)S(1)}, u32[]{:S(2)}, u32[]{:S(2)}) collective-permute-start(bf16[72,1536]{1,0:T(8,128)(2,1)S(1)} %get-tuple-element.89), channel_id=1, source_target_pairs={{0,2},{2,0},{4,6},{6,4},{8,10},{10,8},{12,14},{14,12},{1,3},{3,1},... | collective-permute-start | bytes 663560 | tf_op jit(solution)/shard_map/ppermute | solution.py:274
  57.7 3.2 %collective-permute-start.12 = (bf16[80,768]{1,0:T(8,128)(2,1)S(1)}, bf16[80,768]{1,0:T(8,128)(2,1)S(1)}, u32[]{:S(2)}, u32[]{:S(2)}) collective-permute-start(bf16[80,768]{1,0:T(8,128)(2,1)S(1)} %get-tuple-element.80), channel_id=1, source_target_pairs={{0,1},{1,0},{2,3},{3,2},{4,5},{5,4},{6,7},{7,6},{8,9},{9,8},{10,11... | collective-permute-start | bytes 368648 | tf_op jit(solution)/shard_map/ppermute | solution.py:316
  58.6 8.2 %collective-permute-start.17 = (bf16[72,1536]{1,0:T(8,128)(2,1)S(1)}, bf16[72,1536]{1,0:T(8,128)(2,1)S(1)}, u32[]{:S(2)}, u32[]{:S(2)}) collective-permute-start(bf16[72,1536]{1,0:T(8,128)(2,1)S(1)} %add.13), channel_id=1, source_target_pairs={{0,4},{2,6},{4,12},{6,14},{8,0},{10,2},{12,8},{14,10},{1,5},{3,7},... | collective-permute-start | bytes 663560 | tf_op jit(solution)/shard_map/ppermute | solution.py:337
  62.1 5.5 %collective-permute-start.19 = (bf16[72,1024]{1,0:T(8,128)(2,1)S(1)}, bf16[72,1024]{1,0:T(8,128)(2,1)S(1)}, u32[]{:S(2)}, u32[]{:S(2)}) collective-permute-start(bf16[72,1024]{1,0:T(8,128)(2,1)S(1)} %get-tuple-element.102), channel_id=1, source_target_pairs={{0,2},{2,0},{4,6},{6,4},{8,10},{10,8},{12,14},{14,12},{1,3},{3,1},... | collective-permute-start | bytes 442376 | tf_op jit(solution)/shard_map/ppermute | solution.py:274
  63.0 12.1 %collective-permute-start.18 = (bf16[72,1536]{1,0:T(8,128)(2,1)S(1)}, bf16[72,1536]{1,0:T(8,128)(2,1)S(1)}, u32[]{:S(2)}, u32[]{:S(2)}) collective-permute-start(bf16[72,1536]{1,0:T(8,128)(2,1)S(1)} %add.12), channel_id=1, source_target_pairs={{0,4},{2,6},{4,0},{6,2},{8,12},{10,14},{12,8},{14,10},{1,5},{3,7},... | collective-permute-start | bytes 663560 | tf_op jit(solution)/shard_map/ppermute | solution.py:277
  64.3 5.9 %collective-permute-start.13 = (bf16[72,512]{1,0:T(8,128)(2,1)S(1)}, bf16[72,512]{1,0:T(8,128)(2,1)S(1)}, u32[]{:S(2)}, u32[]{:S(2)}) collective-permute-start(bf16[72,512]{1,0:T(8,128)(2,1)S(1)} %get-tuple-element.82), channel_id=1, source_target_pairs={{0,2},{2,0},{4,6},{6,4},{8,10},{10,8},{12,14},{14,12},{1,3},{3,1},... | collective-permute-start | bytes 221192 | tf_op jit(solution)/shard_map/ppermute | solution.py:274
  67.6 8.9 %collective-permute-start.20 = (bf16[72,1024]{1,0:T(8,128)(2,1)S(1)}, bf16[72,1024]{1,0:T(8,128)(2,1)S(1)}, u32[]{:S(2)}, u32[]{:S(2)}) collective-permute-start(bf16[72,1024]{1,0:T(8,128)(2,1)S(1)} %last.3), channel_id=1, source_target_pairs={{0,12},{2,14},{4,8},{6,10},{8,4},{10,6},{12,0},{14,2},{1,13},{3,15... | collective-permute-start | bytes 442376 | tf_op jit(solution)/shard_map/ppermute | solution.py:277
  70.3 6.3 %collective-permute-start.21 = (bf16[72,512]{1,0:T(8,128)(2,1)S(1)}, bf16[72,512]{1,0:T(8,128)(2,1)S(1)}, u32[]{:S(2)}, u32[]{:S(2)}) collective-permute-start(bf16[72,512]{1,0:T(8,128)(2,1)S(1)} %last.2), channel_id=1, source_target_pairs={{0,12},{2,14},{4,8},{6,10},{8,4},{10,6},{12,0},{14,2},{1,13},{3,15... | collective-permute-start | bytes 221192 | tf_op jit(solution)/shard_map/ppermute | solution.py:277

commit v7 on v6

--- a/solution.py
+++ b/solution.py
@@ -203,6 +203,18 @@
         at += piece.shape[1]
 
 
+def pair_kernel(left, right, out):
+    width = left.shape[1]
+    out[:, :width] = left[...]
+    out[:, width:] = right[...]
+
+
+def split_kernel(inner, outer, outer_y, block, block_y):
+    width = block.shape[1]
+    block[...] = inner[:, :width] + outer[...]
+    block_y[...] = inner[:, width:] + outer_y[...]
+
+
 def add_kernel(term, arrived, total):
     total[...] = (term[...] + arrived[...].astype(F32)).astype(BF16)
 
@@ -341,23 +353,24 @@
     one = along(own, 1)
     h0, d0, t0, s0 = back(*front(own, own_y))
     one_y = along(own_y, 1)
+    pair = call(pair_kernel, struct(BLOCK, 2 * features, BF16), own, own_y, name="pair")
     q0 = add(t0, s0)
-    two, one, q0 = lax.optimization_barrier((two, one, q0))
+    two, one, q0, pair = lax.optimization_barrier((two, one, q0, pair))
+    inner = middle(after(pair, two))
+    outer = ends(two)
     two_y = across(two)
-    outer = ends(two)
-    inner = middle(after(own, two))
     h1, d1, t1, s1 = back(*front(one, one_y))
     q1 = add(t1, s1)
-    inner, two_y, s1 = lax.optimization_barrier((inner, two_y, s1))
+    two_y, s1 = lax.optimization_barrier((two_y, s1))
     outer_y = ends(two_y)
-    inner_y = middle(after(own_y, inner))
-    three = inner + outer
-    three_y = inner_y + outer_y
     part2, swap2 = front(two, two_y)
-    h2, d2, t2, s2 = back(after(part2, three), swap2)
-    q2 = add(t2, after(s2, q1))
+    h2, d2, t2, s2 = back(after(part2, outer, q1), swap2)
+    q2 = add(t2, s2)
     got = relay(q2)
     large = half * 2 // 3
+    three, three_y = call(
+        split_kernel, (struct(BLOCK, features, BF16),) * 2, inner, outer, outer_y, name="split"
+    )
     h3, d3, t3, *s3 = back(*front(three, three_y), large, half - large)
     r1 = along(after(q1, *s3), 1)
     q3 = [

time: 78 us -> 77.8 us (level)
    pallas_call x18 -> x20, Pallas kernels: 18.1 us -> 18.3 us  [call(): pl.pallas_call(kernel, out_shape=outs, name=name, compiler_params=pltpu.C...]
  transfers between devices with their start and end apart: 22 -> 21, of which waited for: 12 -> 12; matrix products, arithmetic and copies ran while one was open for 0% -> 0% of each run, Pallas kernels for 19% -> 20%
where the time goes in v7:
time: 77.8 us; the launch traced here: 77.6 us
  waiting for transfers between devices  33 us (42%)
  starting transfers between devices  25.5 us (33%)
  Pallas kernels  18.3 us (24%)
  between operations  0.79 us (1%)
    pallas_call x20, Pallas kernels, call(): pl.pallas_call(kernel, out_shape=outs, name=name, compiler_params=pltpu.C...  18.3 us
    ppermute x7, waiting for transfers between devices, across(): return lax.ppermute(value, 'expert', [(i, i ^ 1) for i in range(8)])  16.1 us
    ppermute x6, starting transfers between devices, along(): lax.ppermute(value, 'expert', [(i, i ^ 2 * distance) for i in range(8)])  11.7 us
    ppermute x6, waiting for transfers between devices, along(): lax.ppermute(value, 'expert', [(i, i ^ 2 * distance) for i in range(8)])  9.65 us
    ppermute x7, starting transfers between devices, across(): return lax.ppermute(value, 'expert', [(i, i ^ 1) for i in range(8)])  8.08 us
    ppermute x2, waiting for transfers between devices, ends(): return lax.ppermute(value, 'expert', [(4, 6), (5, 7), (2, 0), (3, 1)])  3.75 us
    ppermute x4, waiting for transfers between devices, front(): return (part, lax.ppermute(sent, 'tensor', [(0, 1), (1, 0)]))  2.65 us
    ppermute x2, starting transfers between devices, ends(): return lax.ppermute(value, 'expert', [(4, 6), (5, 7), (2, 0), (3, 1)])  2.58 us
  transfers between devices with their start and end apart: 21, of which 12 were waited for; matrix products, arithmetic and copies ran while one was open for 0% of the time, Pallas kernels for 20%

profile of v7, /device:TPU:0, one launch (start us, length us, event | category | flops | bytes accessed | tf_op | source)
XLA Modules:
  0.0 77.6 jit_solution(8169149023187547273)
XLA Ops:
  0.6 1.7 %place.1 = (bf16[72,3072]{1,0:T(8,128)(2,1)S(1)}, bf16[128,128]{1,0:T(8,128)(2,1)S(1)}) custom-call(bf16[128,3072]{1,0:T(8,128)(2,1)} %tokens_at.1, bf16[128,3072]{1,0:T(8,128)(2,1)} %grad_out_at.1, s32[2,128]{1,0:T(2,128)} %bitcast.2, f32[2,128]{1,0:T(2,128)} %bitcast.3), custom_call_target="tpu_custom_call" | custom-call | flops 1000 | bytes 1000 | tf_op jit(solution)/shard_map/place/pallas_call | solution.py:103
  2.3 3.0 %collective-permute-start.2 = (bf16[72,3072]{1,0:T(8,128)(2,1)S(1)}, bf16[72,3072]{1,0:T(8,128)(2,1)S(1)}, u32[]{:S(2)}, u32[]{:S(2)}) collective-permute-start(bf16[72,3072]{1,0:T(8,128)(2,1)S(1)} %get-tuple-element.90.mine.left.refs_0_), channel_id=1, source_target_pairs={{0,2},{2,0},{4,6},{6,4},{8,10},{10,8},{12,14},{14,12},{1,3},{3,1},... | collective-permute-start | bytes 1327112 | tf_op jit(solution)/shard_map/ppermute | solution.py:286
  5.4 1.6 %collective-permute-start.1 = (bf16[72,3072]{1,0:T(8,128)(2,1)S(1)}, bf16[72,3072]{1,0:T(8,128)(2,1)S(1)}, u32[]{:S(2)}, u32[]{:S(2)}) collective-permute-start(bf16[72,3072]{1,0:T(8,128)(2,1)S(1)} %get-tuple-element.90.mine.left.refs_0_), channel_id=1, source_target_pairs={{0,4},{2,6},{4,0},{6,2},{8,12},{10,14},{12,8},{14,10},{1,5},{3,7},... | collective-permute-start | bytes 1327112 | tf_op jit(solution)/shard_map/ppermute | solution.py:289
  7.0 2.6 %collective-permute-start = (bf16[72,3072]{1,0:T(8,128)(2,1)S(1)}, bf16[72,3072]{1,0:T(8,128)(2,1)S(1)}, u32[]{:S(2)}, u32[]{:S(2)}) collective-permute-start(bf16[72,3072]{1,0:T(8,128)(2,1)S(1)} %get-tuple-element.90.mine.left.refs_0_), channel_id=1, source_target_pairs={{0,8},{2,10},{4,12},{6,14},{8,0},{10,2},{12,4},{14,6},{1,9},{3,11}... | collective-permute-start | bytes 1327112 | tf_op jit(solution)/shard_map/ppermute | solution.py:289
  9.6 2.4 %load.1 = (bf16[3072,256]{1,0:T(8,128)(2,1)S(1)}, bf16[3072,256]{1,0:T(8,128)(2,1)S(1)}, bf16[256,3072]{1,0:T(8,128)(2,1)S(1)}) custom-call(bf16[3072,256]{1,0:T(8,128)(2,1)} %refs_0_, bf16[3072,256]{1,0:T(8,128)(2,1)} %refs_1_, bf16[256,3072]{1,0:T(8,128)(2,1)} %refs_2_), custom_call_target="tpu_custom_call" | custom-call | flops 1000 | bytes 1000 | tf_op jit(solution)/shard_map/load/pallas_call | solution.py:103
  11.9 3.6 %collective-permute-done.2.other.right.refs_1_ = bf16[72,3072]{1,0:T(8,128)(2,1)S(1)} collective-permute-done((bf16[72,3072]{1,0:T(8,128)(2,1)S(1)}, bf16[72,3072]{1,0:T(8,128)(2,1)S(1)}, u32[]{:S(2)}, u32[]{:S(2)}) %collective-permute-start.2) | collective-permute-done | bytes 442400 | tf_op jit(solution)/shard_map/ppermute | solution.py:286
  16.8 1.3 %collective-permute-done.3.arrived = bf16[80,768]{1,0:T(8,128)(2,1)S(1)} collective-permute-done((bf16[80,768]{1,0:T(8,128)(2,1)S(1)}, bf16[80,768]{1,0:T(8,128)(2,1)S(1)}, u32[]{:S(2)}, u32[]{:S(2)}) %collective-permute-start.3) | collective-permute-done | bytes 122912 | tf_op jit(solution)/shard_map/ppermute | solution.py:328
  19.2 1.8 %collective-permute-start.4 = (bf16[72,1536]{1,0:T(8,128)(2,1)S(1)}, bf16[72,1536]{1,0:T(8,128)(2,1)S(1)}, u32[]{:S(2)}, u32[]{:S(2)}) collective-permute-start(bf16[72,1536]{1,0:T(8,128)(2,1)S(1)} %get-tuple-element.68), channel_id=1, source_target_pairs={{0,2},{2,0},{4,6},{6,4},{8,10},{10,8},{12,14},{14,12},{1,3},{3,1},... | collective-permute-start | bytes 663560 | tf_op jit(solution)/shard_map/ppermute | solution.py:286
  21.0 1.6 %collective-permute-start.8 = (bf16[72,3072]{1,0:T(8,128)(2,1)S(1)}, bf16[72,3072]{1,0:T(8,128)(2,1)S(1)}, u32[]{:S(2)}, u32[]{:S(2)}) collective-permute-start(bf16[72,3072]{1,0:T(8,128)(2,1)S(1)} %collective-permute-done.2.other.right.refs_1_), channel_id=1, source_target_pairs={{0,4},{2,6},{4,0},{6,2},{8,12},{10,14},{12,8},{14,10},{1,5},{3,7},... | collective-permute-start | bytes 1327112 | tf_op jit(solution)/shard_map/ppermute | solution.py:289
  22.6 4.1 %collective-permute-done.4.arrived = bf16[72,1536]{1,0:T(8,128)(2,1)S(1)} collective-permute-done((bf16[72,1536]{1,0:T(8,128)(2,1)S(1)}, bf16[72,1536]{1,0:T(8,128)(2,1)S(1)}, u32[]{:S(2)}, u32[]{:S(2)}) %collective-permute-start.4) | collective-permute-done | bytes 221216 | tf_op jit(solution)/shard_map/ppermute | solution.py:286
  29.3 1.3 %collective-permute-start.6 = (bf16[72,3072]{1,0:T(8,128)(2,1)S(1)}, bf16[72,3072]{1,0:T(8,128)(2,1)S(1)}, u32[]{:S(2)}, u32[]{:S(2)}) collective-permute-start(bf16[72,3072]{1,0:T(8,128)(2,1)S(1)} %collective-permute-done.mine.refs_4_), channel_id=1, source_target_pairs={{8,12},{10,14},{4,0},{6,2},{9,13},{11,15},{5,1},{7,3},{24,28},{26,... | collective-permute-start | bytes 1327112 | tf_op jit(solution)/shard_map/ppermute | solution.py:345
  30.6 6.7 %collective-permute-done.8.other.refs_3_ = bf16[72,3072]{1,0:T(8,128)(2,1)S(1)} collective-permute-done((bf16[72,3072]{1,0:T(8,128)(2,1)S(1)}, bf16[72,3072]{1,0:T(8,128)(2,1)S(1)}, u32[]{:S(2)}, u32[]{:S(2)}) %collective-permute-start.8) | collective-permute-done | bytes 442400 | tf_op jit(solution)/shard_map/ppermute | solution.py:289
  38.5 1.3 %collective-permute-done.9.arrived = bf16[80,768]{1,0:T(8,128)(2,1)S(1)} collective-permute-done((bf16[80,768]{1,0:T(8,128)(2,1)S(1)}, bf16[80,768]{1,0:T(8,128)(2,1)S(1)}, u32[]{:S(2)}, u32[]{:S(2)}) %collective-permute-start.9) | collective-permute-done | bytes 122912 | tf_op jit(solution)/shard_map/ppermute | solution.py:328
  41.0 1.3 %collective-permute-start.10 = (bf16[72,3072]{1,0:T(8,128)(2,1)S(1)}, bf16[72,3072]{1,0:T(8,128)(2,1)S(1)}, u32[]{:S(2)}, u32[]{:S(2)}) collective-permute-start(bf16[72,3072]{1,0:T(8,128)(2,1)S(1)} %collective-permute-done.7.other.refs_5_), channel_id=1, source_target_pairs={{8,12},{10,14},{4,0},{6,2},{9,13},{11,15},{5,1},{7,3},{24,28},{26,... | collective-permute-start | bytes 1327112 | tf_op jit(solution)/shard_map/ppermute | solution.py:345
  43.7 6.1 %collective-permute-done.13.arrived = bf16[72,1536]{1,0:T(8,128)(2,1)S(1)} collective-permute-done((bf16[72,1536]{1,0:T(8,128)(2,1)S(1)}, bf16[72,1536]{1,0:T(8,128)(2,1)S(1)}, u32[]{:S(2)}, u32[]{:S(2)}) %collective-permute-start.13) | collective-permute-done | bytes 221216 | tf_op jit(solution)/shard_map/ppermute | solution.py:286
  51.3 3.8 %collective-permute-done.10.outer_y = bf16[72,3072]{1,0:T(8,128)(2,1)S(1)} collective-permute-done((bf16[72,3072]{1,0:T(8,128)(2,1)S(1)}, bf16[72,3072]{1,0:T(8,128)(2,1)S(1)}, u32[]{:S(2)}, u32[]{:S(2)}) %collective-permute-start.10) | collective-permute-done | bytes 442400 | tf_op jit(solution)/shard_map/ppermute | solution.py:345
  56.4 1.3 %collective-permute-done.15.arrived = bf16[72,1536]{1,0:T(8,128)(2,1)S(1)} collective-permute-done((bf16[72,1536]{1,0:T(8,128)(2,1)S(1)}, bf16[72,1536]{1,0:T(8,128)(2,1)S(1)}, u32[]{:S(2)}, u32[]{:S(2)}) %collective-permute-start.15) | collective-permute-done | bytes 221216 | tf_op jit(solution)/shard_map/ppermute | solution.py:286
  57.8 2.1 %collective-permute-start.16 = (bf16[72,1536]{1,0:T(8,128)(2,1)S(1)}, bf16[72,1536]{1,0:T(8,128)(2,1)S(1)}, u32[]{:S(2)}, u32[]{:S(2)}) collective-permute-start(bf16[72,1536]{1,0:T(8,128)(2,1)S(1)} %add.5), channel_id=1, source_target_pairs={{0,4},{2,6},{4,12},{6,14},{8,0},{10,2},{12,8},{14,10},{1,5},{3,7},... | collective-permute-start | bytes 663560 | tf_op jit(solution)/shard_map/ppermute | solution.py:349
  61.5 2.0 %collective-permute-start.17 = (bf16[72,1536]{1,0:T(8,128)(2,1)S(1)}, bf16[72,1536]{1,0:T(8,128)(2,1)S(1)}, u32[]{:S(2)}, u32[]{:S(2)}) collective-permute-start(bf16[72,1536]{1,0:T(8,128)(2,1)S(1)} %add.4), channel_id=1, source_target_pairs={{0,4},{2,6},{4,0},{6,2},{8,12},{10,14},{12,8},{14,10},{1,5},{3,7},... | collective-permute-start | bytes 663560 | tf_op jit(solution)/shard_map/ppermute | solution.py:289
  63.5 1.5 %collective-permute-start.12 = (bf16[72,512]{1,0:T(8,128)(2,1)S(1)}, bf16[72,512]{1,0:T(8,128)(2,1)S(1)}, u32[]{:S(2)}, u32[]{:S(2)}) collective-permute-start(bf16[72,512]{1,0:T(8,128)(2,1)S(1)} %get-tuple-element.83), channel_id=1, source_target_pairs={{0,2},{2,0},{4,6},{6,4},{8,10},{10,8},{12,14},{14,12},{1,3},{3,1},... | collective-permute-start | bytes 221192 | tf_op jit(solution)/shard_map/ppermute | solution.py:286
  66.9 2.9 %collective-permute-start.19 = (bf16[72,1024]{1,0:T(8,128)(2,1)S(1)}, bf16[72,1024]{1,0:T(8,128)(2,1)S(1)}, u32[]{:S(2)}, u32[]{:S(2)}) collective-permute-start(bf16[72,1024]{1,0:T(8,128)(2,1)S(1)} %last.3), channel_id=1, source_target_pairs={{0,12},{2,14},{4,8},{6,10},{8,4},{10,6},{12,0},{14,2},{1,13},{3,15... | collective-permute-start | bytes 442376 | tf_op jit(solution)/shard_map/ppermute | solution.py:289
  70.9 3.5 %grads.1 = (bf16[3072,256]{1,0:T(8,128)(2,1)}, bf16[3072,256]{1,0:T(8,128)(2,1)}, bf16[256,3072]{1,0:T(8,128)(2,1)}) custom-call(bf16[72,3072]{1,0:T(8,128)(2,1)S(1)} %get-tuple-element.90.mine.left.refs_0_, bf16[72,3072]{1,0:T(8,128)(2,1)S(1)} %collective-permute-done.2.other.right.refs_1_, bf16[72,3072]{1,0:T(8,128)(2,1)S(1)} %collective-permute-done.1.mine.refs_2_, ...), custom_call_target="tpu_custom_call" | custom-call | flops 1000 | bytes 1000 | tf_op jit(solution)/shard_map/grads/pallas_call | solution.py:103
  74.5 1.8 %collective-permute-done.20.right = bf16[72,512]{1,0:T(8,128)(2,1)S(1)} collective-permute-done((bf16[72,512]{1,0:T(8,128)(2,1)S(1)}, bf16[72,512]{1,0:T(8,128)(2,1)S(1)}, u32[]{:S(2)}, u32[]{:S(2)}) %collective-permute-start.20) | collective-permute-done | bytes 73760 | tf_op jit(solution)/shard_map/ppermute | solution.py:289
  76.3 1.2 %finish.1 = bf16[128,3072]{1,0:T(8,128)(2,1)} custom-call(bf16[128,128]{1,0:T(8,128)(2,1)S(1)} %get-tuple-element.57.placing_t, f32[72,1536]{1,0:T(8,128)S(1)} %near.1, bf16[72,1024]{1,0:T(8,128)(2,1)S(1)} %collective-permute-done.19.left, bf16[72,512]{1,0:T(8,128)(2,1)S(1)} %collective-permute-done.20.right), custom_call_target="tpu_custom_call" | custom-call | flops 1000 | bytes 1000 | tf_op jit(solution)/shard_map/finish/pallas_call | solution.py:103
  (38 shorter events, 16.2 us)
Async XLA Ops:
  2.3 13.2 %collective-permute-start.2 = (bf16[72,3072]{1,0:T(8,128)(2,1)S(1)}, bf16[72,3072]{1,0:T(8,128)(2,1)S(1)}, u32[]{:S(2)}, u32[]{:S(2)}) collective-permute-start(bf16[72,3072]{1,0:T(8,128)(2,1)S(1)} %get-tuple-element.90.mine.left.refs_0_), channel_id=1, source_target_pairs={{0,2},{2,0},{4,6},{6,4},{8,10},{10,8},{12,14},{14,12},{1,3},{3,1},... | collective-permute-start | bytes 1327112 | tf_op jit(solution)/shard_map/ppermute | solution.py:286
  5.4 22.6 %collective-permute-start.1 = (bf16[72,3072]{1,0:T(8,128)(2,1)S(1)}, bf16[72,3072]{1,0:T(8,128)(2,1)S(1)}, u32[]{:S(2)}, u32[]{:S(2)}) collective-permute-start(bf16[72,3072]{1,0:T(8,128)(2,1)S(1)} %get-tuple-element.90.mine.left.refs_0_), channel_id=1, source_target_pairs={{0,4},{2,6},{4,0},{6,2},{8,12},{10,14},{12,8},{14,10},{1,5},{3,7},... | collective-permute-start | bytes 1327112 | tf_op jit(solution)/shard_map/ppermute | solution.py:289
  7.0 21.0 %collective-permute-start = (bf16[72,3072]{1,0:T(8,128)(2,1)S(1)}, bf16[72,3072]{1,0:T(8,128)(2,1)S(1)}, u32[]{:S(2)}, u32[]{:S(2)}) collective-permute-start(bf16[72,3072]{1,0:T(8,128)(2,1)S(1)} %get-tuple-element.90.mine.left.refs_0_), channel_id=1, source_target_pairs={{0,8},{2,10},{4,12},{6,14},{8,0},{10,2},{12,4},{14,6},{1,9},{3,11}... | collective-permute-start | bytes 1327112 | tf_op jit(solution)/shard_map/ppermute | solution.py:289
  16.7 1.4 %collective-permute-start.3 = (bf16[80,768]{1,0:T(8,128)(2,1)S(1)}, bf16[80,768]{1,0:T(8,128)(2,1)S(1)}, u32[]{:S(2)}, u32[]{:S(2)}) collective-permute-start(bf16[80,768]{1,0:T(8,128)(2,1)S(1)} %get-tuple-element.66), channel_id=1, source_target_pairs={{0,1},{1,0},{2,3},{3,2},{4,5},{5,4},{6,7},{7,6},{8,9},{9,8},{10,11... | collective-permute-start | bytes 368648 | tf_op jit(solution)/shard_map/ppermute | solution.py:328
  19.2 7.5 %collective-permute-start.4 = (bf16[72,1536]{1,0:T(8,128)(2,1)S(1)}, bf16[72,1536]{1,0:T(8,128)(2,1)S(1)}, u32[]{:S(2)}, u32[]{:S(2)}) collective-permute-start(bf16[72,1536]{1,0:T(8,128)(2,1)S(1)} %get-tuple-element.68), channel_id=1, source_target_pairs={{0,2},{2,0},{4,6},{6,4},{8,10},{10,8},{12,14},{14,12},{1,3},{3,1},... | collective-permute-start | bytes 663560 | tf_op jit(solution)/shard_map/ppermute | solution.py:286
  21.0 16.3 %collective-permute-start.8 = (bf16[72,3072]{1,0:T(8,128)(2,1)S(1)}, bf16[72,3072]{1,0:T(8,128)(2,1)S(1)}, u32[]{:S(2)}, u32[]{:S(2)}) collective-permute-start(bf16[72,3072]{1,0:T(8,128)(2,1)S(1)} %collective-permute-done.2.other.right.refs_1_), channel_id=1, source_target_pairs={{0,4},{2,6},{4,0},{6,2},{8,12},{10,14},{12,8},{14,10},{1,5},{3,7},... | collective-permute-start | bytes 1327112 | tf_op jit(solution)/shard_map/ppermute | solution.py:289
  28.0 13.0 %collective-permute-start.7 = (bf16[72,3072]{1,0:T(8,128)(2,1)S(1)}, bf16[72,3072]{1,0:T(8,128)(2,1)S(1)}, u32[]{:S(2)}, u32[]{:S(2)}) collective-permute-start(bf16[72,3072]{1,0:T(8,128)(2,1)S(1)} %collective-permute-done.mine.refs_4_), channel_id=1, source_target_pairs={{0,2},{2,0},{4,6},{6,4},{8,10},{10,8},{12,14},{14,12},{1,3},{3,1},... | collective-permute-start | bytes 1327112 | tf_op jit(solution)/shard_map/ppermute | solution.py:286
  28.6 26.5 %collective-permute-start.5 = (bf16[72,6144]{1,0:T(8,128)(2,1)S(1)}, bf16[72,6144]{1,0:T(8,128)(2,1)S(1)}, u32[]{:S(2)}, u32[]{:S(2)}) collective-permute-start(bf16[72,6144]{1,0:T(8,128)(2,1)S(1)} %pair.1), channel_id=1, source_target_pairs={{4,8},{6,10},{8,4},{10,6},{5,9},{7,11},{9,5},{11,7},{20,24},{22,26... | collective-permute-start | bytes 2654216 | tf_op jit(solution)/shard_map/ppermute | solution.py:342
  29.3 20.5 %collective-permute-start.6 = (bf16[72,3072]{1,0:T(8,128)(2,1)S(1)}, bf16[72,3072]{1,0:T(8,128)(2,1)S(1)}, u32[]{:S(2)}, u32[]{:S(2)}) collective-permute-start(bf16[72,3072]{1,0:T(8,128)(2,1)S(1)} %collective-permute-done.mine.refs_4_), channel_id=1, source_target_pairs={{8,12},{10,14},{4,0},{6,2},{9,13},{11,15},{5,1},{7,3},{24,28},{26,... | collective-permute-start | bytes 1327112 | tf_op jit(solution)/shard_map/ppermute | solution.py:345
  38.5 1.4 %collective-permute-start.9 = (bf16[80,768]{1,0:T(8,128)(2,1)S(1)}, bf16[80,768]{1,0:T(8,128)(2,1)S(1)}, u32[]{:S(2)}, u32[]{:S(2)}) collective-permute-start(bf16[80,768]{1,0:T(8,128)(2,1)S(1)} %get-tuple-element.75), channel_id=1, source_target_pairs={{0,1},{1,0},{2,3},{3,2},{4,5},{5,4},{6,7},{7,6},{8,9},{9,8},{10,11... | collective-permute-start | bytes 368648 | tf_op jit(solution)/shard_map/ppermute | solution.py:328
  41.0 14.1 %collective-permute-start.10 = (bf16[72,3072]{1,0:T(8,128)(2,1)S(1)}, bf16[72,3072]{1,0:T(8,128)(2,1)S(1)}, u32[]{:S(2)}, u32[]{:S(2)}) collective-permute-start(bf16[72,3072]{1,0:T(8,128)(2,1)S(1)} %collective-permute-done.7.other.refs_5_), channel_id=1, source_target_pairs={{8,12},{10,14},{4,0},{6,2},{9,13},{11,15},{5,1},{7,3},{24,28},{26,... | collective-permute-start | bytes 1327112 | tf_op jit(solution)/shard_map/ppermute | solution.py:345
  42.3 7.5 %collective-permute-start.13 = (bf16[72,1536]{1,0:T(8,128)(2,1)S(1)}, bf16[72,1536]{1,0:T(8,128)(2,1)S(1)}, u32[]{:S(2)}, u32[]{:S(2)}) collective-permute-start(bf16[72,1536]{1,0:T(8,128)(2,1)S(1)} %get-tuple-element.76), channel_id=1, source_target_pairs={{0,2},{2,0},{4,6},{6,4},{8,10},{10,8},{12,14},{14,12},{1,3},{3,1},... | collective-permute-start | bytes 663560 | tf_op jit(solution)/shard_map/ppermute | solution.py:286
  43.6 6.3 %collective-permute-start.14 = (bf16[80,768]{1,0:T(8,128)(2,1)S(1)}, bf16[80,768]{1,0:T(8,128)(2,1)S(1)}, u32[]{:S(2)}, u32[]{:S(2)}) collective-permute-start(bf16[80,768]{1,0:T(8,128)(2,1)S(1)} %get-tuple-element.87), channel_id=1, source_target_pairs={{0,1},{1,0},{2,3},{3,2},{4,5},{5,4},{6,7},{7,6},{8,9},{9,8},{10,11... | collective-permute-start | bytes 368648 | tf_op jit(solution)/shard_map/ppermute | solution.py:328
  51.0 6.7 %collective-permute-start.15 = (bf16[72,1536]{1,0:T(8,128)(2,1)S(1)}, bf16[72,1536]{1,0:T(8,128)(2,1)S(1)}, u32[]{:S(2)}, u32[]{:S(2)}) collective-permute-start(bf16[72,1536]{1,0:T(8,128)(2,1)S(1)} %get-tuple-element.89), channel_id=1, source_target_pairs={{0,2},{2,0},{4,6},{6,4},{8,10},{10,8},{12,14},{14,12},{1,3},{3,1},... | collective-permute-start | bytes 663560 | tf_op jit(solution)/shard_map/ppermute | solution.py:286
  56.3 3.5 %collective-permute-start.11 = (bf16[80,768]{1,0:T(8,128)(2,1)S(1)}, bf16[80,768]{1,0:T(8,128)(2,1)S(1)}, u32[]{:S(2)}, u32[]{:S(2)}) collective-permute-start(bf16[80,768]{1,0:T(8,128)(2,1)S(1)} %get-tuple-element.81), channel_id=1, source_target_pairs={{0,1},{1,0},{2,3},{3,2},{4,5},{5,4},{6,7},{7,6},{8,9},{9,8},{10,11... | collective-permute-start | bytes 368648 | tf_op jit(solution)/shard_map/ppermute | solution.py:328
  57.8 8.1 %collective-permute-start.16 = (bf16[72,1536]{1,0:T(8,128)(2,1)S(1)}, bf16[72,1536]{1,0:T(8,128)(2,1)S(1)}, u32[]{:S(2)}, u32[]{:S(2)}) collective-permute-start(bf16[72,1536]{1,0:T(8,128)(2,1)S(1)} %add.5), channel_id=1, source_target_pairs={{0,4},{2,6},{4,12},{6,14},{8,0},{10,2},{12,8},{14,10},{1,5},{3,7},... | collective-permute-start | bytes 663560 | tf_op jit(solution)/shard_map/ppermute | solution.py:349
  61.0 5.9 %collective-permute-start.18 = (bf16[72,1024]{1,0:T(8,128)(2,1)S(1)}, bf16[72,1024]{1,0:T(8,128)(2,1)S(1)}, u32[]{:S(2)}, u32[]{:S(2)}) collective-permute-start(bf16[72,1024]{1,0:T(8,128)(2,1)S(1)} %get-tuple-element.102), channel_id=1, source_target_pairs={{0,2},{2,0},{4,6},{6,4},{8,10},{10,8},{12,14},{14,12},{1,3},{3,1},... | collective-permute-start | bytes 442376 | tf_op jit(solution)/shard_map/ppermute | solution.py:286
  61.5 13.0 %collective-permute-start.17 = (bf16[72,1536]{1,0:T(8,128)(2,1)S(1)}, bf16[72,1536]{1,0:T(8,128)(2,1)S(1)}, u32[]{:S(2)}, u32[]{:S(2)}) collective-permute-start(bf16[72,1536]{1,0:T(8,128)(2,1)S(1)} %add.4), channel_id=1, source_target_pairs={{0,4},{2,6},{4,0},{6,2},{8,12},{10,14},{12,8},{14,10},{1,5},{3,7},... | collective-permute-start | bytes 663560 | tf_op jit(solution)/shard_map/ppermute | solution.py:289
  63.5 6.3 %collective-permute-start.12 = (bf16[72,512]{1,0:T(8,128)(2,1)S(1)}, bf16[72,512]{1,0:T(8,128)(2,1)S(1)}, u32[]{:S(2)}, u32[]{:S(2)}) collective-permute-start(bf16[72,512]{1,0:T(8,128)(2,1)S(1)} %get-tuple-element.83), channel_id=1, source_target_pairs={{0,2},{2,0},{4,6},{6,4},{8,10},{10,8},{12,14},{14,12},{1,3},{3,1},... | collective-permute-start | bytes 221192 | tf_op jit(solution)/shard_map/ppermute | solution.py:286
  66.9 9.4 %collective-permute-start.19 = (bf16[72,1024]{1,0:T(8,128)(2,1)S(1)}, bf16[72,1024]{1,0:T(8,128)(2,1)S(1)}, u32[]{:S(2)}, u32[]{:S(2)}) collective-permute-start(bf16[72,1024]{1,0:T(8,128)(2,1)S(1)} %last.3), channel_id=1, source_target_pairs={{0,12},{2,14},{4,8},{6,10},{8,4},{10,6},{12,0},{14,2},{1,13},{3,15... | collective-permute-start | bytes 442376 | tf_op jit(solution)/shard_map/ppermute | solution.py:289
  69.8 6.5 %collective-permute-start.20 = (bf16[72,512]{1,0:T(8,128)(2,1)S(1)}, bf16[72,512]{1,0:T(8,128)(2,1)S(1)}, u32[]{:S(2)}, u32[]{:S(2)}) collective-permute-start(bf16[72,512]{1,0:T(8,128)(2,1)S(1)} %last.2), channel_id=1, source_target_pairs={{0,12},{2,14},{4,8},{6,10},{8,4},{10,6},{12,0},{14,2},{1,13},{3,15... | collective-permute-start | bytes 221192 | tf_op jit(solution)/shard_map/ppermute | solution.py:289

commit v8 on v7

--- a/solution.py
+++ b/solution.py
@@ -235,12 +235,21 @@
     total[...] = jnp.where(is_inner(), value, value + passed[...].astype(F32))
 
 
-def finish_kernel(placing_t, near, left, right, grad_in):
+def finish_kernel(placing_t, near, left, right, grad_in, tile, done):
     total = near[...] + jnp.concatenate([left[...], right[...]], axis=1).astype(F32)
     half = total.shape[1]
+    size = half // 2
     placing = placing_t[:, :CAP]
-    grad_in[:, :half] = mul(placing, total[:CAP].astype(BF16)).astype(BF16)
-    grad_in[:, half:] = mul(placing, total[CAP:].astype(BF16)).astype(BF16)
+    copies = []
+    for step in range(4):
+        rows = slice(0, CAP) if step < 2 else slice(CAP, BLOCK)
+        at = (step % 2) * size
+        columns = slice(step * size, (step + 1) * size)
+        tile[:, columns] = mul(placing, total[rows, at : at + size].astype(BF16)).astype(BF16)
+        copies.append(pltpu.make_async_copy(tile.at[:, columns], grad_in.at[:, columns], done.at[step]))
+        copies[-1].start()
+    for copy in copies:
+        copy.wait()
 
 
 def grads_kernel(*refs):
@@ -398,7 +407,9 @@
     grads, r1 = lax.optimization_barrier((grads, r1))
     near = call(near_kernel, struct(BLOCK, half, F32), q0, r1, got, name="near")
     grad_in = call(
-        finish_kernel, struct(tokens.shape[0], features, BF16), placing_t, near, *after(r3, near), name="finish"
+        finish_kernel, struct(tokens.shape[0], features, BF16), placing_t, near, *after(r3, near), name="finish",
+        out_specs=in_hbm,
+        scratch_shapes=[pltpu.VMEM(tokens.shape, BF16), pltpu.SemaphoreType.DMA((4,))],
     )
     return (grad_in,) + tuple(grads)
 

time: 77.8 us -> 77.6 us (level)
  no operation moved by 1% of the time
where the time goes in v8:
time: 77.6 us; the launch traced here: 77.4 us
  waiting for transfers between devices  33 us (43%)
  starting transfers between devices  25.5 us (33%)
  Pallas kernels  18.1 us (23%)
  between operations  0.79 us (1%)
    pallas_call x20, Pallas kernels, call(): pl.pallas_call(kernel, out_shape=outs, name=name, compiler_params=pltpu.C...  18.1 us
    ppermute x7, waiting for transfers between devices, across(): return lax.ppermute(value, 'expert', [(i, i ^ 1) for i in range(8)])  16.1 us
    ppermute x6, starting transfers between devices, along(): lax.ppermute(value, 'expert', [(i, i ^ 2 * distance) for i in range(8)])  11.7 us
    ppermute x6, waiting for transfers between devices, along(): lax.ppermute(value, 'expert', [(i, i ^ 2 * distance) for i in range(8)])  9.65 us
    ppermute x7, starting transfers between devices, across(): return lax.ppermute(value, 'expert', [(i, i ^ 1) for i in range(8)])  8.08 us
    ppermute x2, waiting for transfers between devices, ends(): return lax.ppermute(value, 'expert', [(4, 6), (5, 7), (2, 0), (3, 1)])  3.75 us
    ppermute x4, waiting for transfers between devices, front(): return (part, lax.ppermute(sent, 'tensor', [(0, 1), (1, 0)]))  2.65 us
    ppermute x2, starting transfers between devices, ends(): return lax.ppermute(value, 'expert', [(4, 6), (5, 7), (2, 0), (3, 1)])  2.58 us
  transfers between devices with their start and end apart: 21, of which 12 were waited for; matrix products, arithmetic and copies ran while one was open for 0% of the time, Pallas kernels for 20%

profile of v8, /device:TPU:0, one launch (start us, length us, event | category | flops | bytes accessed | tf_op | source)
XLA Modules:
  0.0 77.4 jit_solution(9684957373750313129)
XLA Ops:
  0.6 1.7 %place.1 = (bf16[72,3072]{1,0:T(8,128)(2,1)S(1)}, bf16[128,128]{1,0:T(8,128)(2,1)S(1)}) custom-call(bf16[128,3072]{1,0:T(8,128)(2,1)} %tokens_at.1, bf16[128,3072]{1,0:T(8,128)(2,1)} %grad_out_at.1, s32[2,128]{1,0:T(2,128)} %bitcast.2, f32[2,128]{1,0:T(2,128)} %bitcast.3), custom_call_target="tpu_custom_call" | custom-call | flops 1000 | bytes 1000 | tf_op jit(solution)/shard_map/place/pallas_call | solution.py:103
  2.3 3.0 %collective-permute-start.2 = (bf16[72,3072]{1,0:T(8,128)(2,1)S(1)}, bf16[72,3072]{1,0:T(8,128)(2,1)S(1)}, u32[]{:S(2)}, u32[]{:S(2)}) collective-permute-start(bf16[72,3072]{1,0:T(8,128)(2,1)S(1)} %get-tuple-element.90.mine.left.refs_0_), channel_id=1, source_target_pairs={{0,2},{2,0},{4,6},{6,4},{8,10},{10,8},{12,14},{14,12},{1,3},{3,1},... | collective-permute-start | bytes 1327112 | tf_op jit(solution)/shard_map/ppermute | solution.py:295
  5.4 1.6 %collective-permute-start.1 = (bf16[72,3072]{1,0:T(8,128)(2,1)S(1)}, bf16[72,3072]{1,0:T(8,128)(2,1)S(1)}, u32[]{:S(2)}, u32[]{:S(2)}) collective-permute-start(bf16[72,3072]{1,0:T(8,128)(2,1)S(1)} %get-tuple-element.90.mine.left.refs_0_), channel_id=1, source_target_pairs={{0,4},{2,6},{4,0},{6,2},{8,12},{10,14},{12,8},{14,10},{1,5},{3,7},... | collective-permute-start | bytes 1327112 | tf_op jit(solution)/shard_map/ppermute | solution.py:298
  7.0 2.6 %collective-permute-start = (bf16[72,3072]{1,0:T(8,128)(2,1)S(1)}, bf16[72,3072]{1,0:T(8,128)(2,1)S(1)}, u32[]{:S(2)}, u32[]{:S(2)}) collective-permute-start(bf16[72,3072]{1,0:T(8,128)(2,1)S(1)} %get-tuple-element.90.mine.left.refs_0_), channel_id=1, source_target_pairs={{0,8},{2,10},{4,12},{6,14},{8,0},{10,2},{12,4},{14,6},{1,9},{3,11}... | collective-permute-start | bytes 1327112 | tf_op jit(solution)/shard_map/ppermute | solution.py:298
  9.6 2.4 %load.1 = (bf16[3072,256]{1,0:T(8,128)(2,1)S(1)}, bf16[3072,256]{1,0:T(8,128)(2,1)S(1)}, bf16[256,3072]{1,0:T(8,128)(2,1)S(1)}) custom-call(bf16[3072,256]{1,0:T(8,128)(2,1)} %refs_0_, bf16[3072,256]{1,0:T(8,128)(2,1)} %refs_1_, bf16[256,3072]{1,0:T(8,128)(2,1)} %refs_2_), custom_call_target="tpu_custom_call" | custom-call | flops 1000 | bytes 1000 | tf_op jit(solution)/shard_map/load/pallas_call | solution.py:103
  11.9 3.6 %collective-permute-done.2.other.right.refs_1_ = bf16[72,3072]{1,0:T(8,128)(2,1)S(1)} collective-permute-done((bf16[72,3072]{1,0:T(8,128)(2,1)S(1)}, bf16[72,3072]{1,0:T(8,128)(2,1)S(1)}, u32[]{:S(2)}, u32[]{:S(2)}) %collective-permute-start.2) | collective-permute-done | bytes 442400 | tf_op jit(solution)/shard_map/ppermute | solution.py:295
  16.8 1.3 %collective-permute-done.3.arrived = bf16[80,768]{1,0:T(8,128)(2,1)S(1)} collective-permute-done((bf16[80,768]{1,0:T(8,128)(2,1)S(1)}, bf16[80,768]{1,0:T(8,128)(2,1)S(1)}, u32[]{:S(2)}, u32[]{:S(2)}) %collective-permute-start.3) | collective-permute-done | bytes 122912 | tf_op jit(solution)/shard_map/ppermute | solution.py:337
  19.2 1.8 %collective-permute-start.4 = (bf16[72,1536]{1,0:T(8,128)(2,1)S(1)}, bf16[72,1536]{1,0:T(8,128)(2,1)S(1)}, u32[]{:S(2)}, u32[]{:S(2)}) collective-permute-start(bf16[72,1536]{1,0:T(8,128)(2,1)S(1)} %get-tuple-element.68), channel_id=1, source_target_pairs={{0,2},{2,0},{4,6},{6,4},{8,10},{10,8},{12,14},{14,12},{1,3},{3,1},... | collective-permute-start | bytes 663560 | tf_op jit(solution)/shard_map/ppermute | solution.py:295
  21.0 1.6 %collective-permute-start.8 = (bf16[72,3072]{1,0:T(8,128)(2,1)S(1)}, bf16[72,3072]{1,0:T(8,128)(2,1)S(1)}, u32[]{:S(2)}, u32[]{:S(2)}) collective-permute-start(bf16[72,3072]{1,0:T(8,128)(2,1)S(1)} %collective-permute-done.2.other.right.refs_1_), channel_id=1, source_target_pairs={{0,4},{2,6},{4,0},{6,2},{8,12},{10,14},{12,8},{14,10},{1,5},{3,7},... | collective-permute-start | bytes 1327112 | tf_op jit(solution)/shard_map/ppermute | solution.py:298
  22.6 4.1 %collective-permute-done.4.arrived = bf16[72,1536]{1,0:T(8,128)(2,1)S(1)} collective-permute-done((bf16[72,1536]{1,0:T(8,128)(2,1)S(1)}, bf16[72,1536]{1,0:T(8,128)(2,1)S(1)}, u32[]{:S(2)}, u32[]{:S(2)}) %collective-permute-start.4) | collective-permute-done | bytes 221216 | tf_op jit(solution)/shard_map/ppermute | solution.py:295
  26.8 1.2 %collective-permute-done.1.mine.refs_2_ = bf16[72,3072]{1,0:T(8,128)(2,1)S(1)} collective-permute-done((bf16[72,3072]{1,0:T(8,128)(2,1)S(1)}, bf16[72,3072]{1,0:T(8,128)(2,1)S(1)}, u32[]{:S(2)}, u32[]{:S(2)}) %collective-permute-start.1) | collective-permute-done | bytes 442400 | tf_op jit(solution)/shard_map/ppermute | solution.py:298
  29.3 1.3 %collective-permute-start.6 = (bf16[72,3072]{1,0:T(8,128)(2,1)S(1)}, bf16[72,3072]{1,0:T(8,128)(2,1)S(1)}, u32[]{:S(2)}, u32[]{:S(2)}) collective-permute-start(bf16[72,3072]{1,0:T(8,128)(2,1)S(1)} %collective-permute-done.mine.refs_4_), channel_id=1, source_target_pairs={{8,12},{10,14},{4,0},{6,2},{9,13},{11,15},{5,1},{7,3},{24,28},{26,... | collective-permute-start | bytes 1327112 | tf_op jit(solution)/shard_map/ppermute | solution.py:354
  30.6 6.7 %collective-permute-done.8.other.refs_3_ = bf16[72,3072]{1,0:T(8,128)(2,1)S(1)} collective-permute-done((bf16[72,3072]{1,0:T(8,128)(2,1)S(1)}, bf16[72,3072]{1,0:T(8,128)(2,1)S(1)}, u32[]{:S(2)}, u32[]{:S(2)}) %collective-permute-start.8) | collective-permute-done | bytes 442400 | tf_op jit(solution)/shard_map/ppermute | solution.py:298
  38.5 1.3 %collective-permute-done.9.arrived = bf16[80,768]{1,0:T(8,128)(2,1)S(1)} collective-permute-done((bf16[80,768]{1,0:T(8,128)(2,1)S(1)}, bf16[80,768]{1,0:T(8,128)(2,1)S(1)}, u32[]{:S(2)}, u32[]{:S(2)}) %collective-permute-start.9) | collective-permute-done | bytes 122912 | tf_op jit(solution)/shard_map/ppermute | solution.py:337
  41.0 1.3 %collective-permute-start.10 = (bf16[72,3072]{1,0:T(8,128)(2,1)S(1)}, bf16[72,3072]{1,0:T(8,128)(2,1)S(1)}, u32[]{:S(2)}, u32[]{:S(2)}) collective-permute-start(bf16[72,3072]{1,0:T(8,128)(2,1)S(1)} %collective-permute-done.7.other.refs_5_), channel_id=1, source_target_pairs={{8,12},{10,14},{4,0},{6,2},{9,13},{11,15},{5,1},{7,3},{24,28},{26,... | collective-permute-start | bytes 1327112 | tf_op jit(solution)/shard_map/ppermute | solution.py:354
  43.7 6.1 %collective-permute-done.13.arrived = bf16[72,1536]{1,0:T(8,128)(2,1)S(1)} collective-permute-done((bf16[72,1536]{1,0:T(8,128)(2,1)S(1)}, bf16[72,1536]{1,0:T(8,128)(2,1)S(1)}, u32[]{:S(2)}, u32[]{:S(2)}) %collective-permute-start.13) | collective-permute-done | bytes 221216 | tf_op jit(solution)/shard_map/ppermute | solution.py:295
  51.3 3.8 %collective-permute-done.10.outer_y = bf16[72,3072]{1,0:T(8,128)(2,1)S(1)} collective-permute-done((bf16[72,3072]{1,0:T(8,128)(2,1)S(1)}, bf16[72,3072]{1,0:T(8,128)(2,1)S(1)}, u32[]{:S(2)}, u32[]{:S(2)}) %collective-permute-start.10) | collective-permute-done | bytes 442400 | tf_op jit(solution)/shard_map/ppermute | solution.py:354
  56.4 1.3 %collective-permute-done.15.arrived = bf16[72,1536]{1,0:T(8,128)(2,1)S(1)} collective-permute-done((bf16[72,1536]{1,0:T(8,128)(2,1)S(1)}, bf16[72,1536]{1,0:T(8,128)(2,1)S(1)}, u32[]{:S(2)}, u32[]{:S(2)}) %collective-permute-start.15) | collective-permute-done | bytes 221216 | tf_op jit(solution)/shard_map/ppermute | solution.py:295
  57.8 2.1 %collective-permute-start.16 = (bf16[72,1536]{1,0:T(8,128)(2,1)S(1)}, bf16[72,1536]{1,0:T(8,128)(2,1)S(1)}, u32[]{:S(2)}, u32[]{:S(2)}) collective-permute-start(bf16[72,1536]{1,0:T(8,128)(2,1)S(1)} %add.5), channel_id=1, source_target_pairs={{0,4},{2,6},{4,12},{6,14},{8,0},{10,2},{12,8},{14,10},{1,5},{3,7},... | collective-permute-start | bytes 663560 | tf_op jit(solution)/shard_map/ppermute | solution.py:358
  61.5 2.0 %collective-permute-start.17 = (bf16[72,1536]{1,0:T(8,128)(2,1)S(1)}, bf16[72,1536]{1,0:T(8,128)(2,1)S(1)}, u32[]{:S(2)}, u32[]{:S(2)}) collective-permute-start(bf16[72,1536]{1,0:T(8,128)(2,1)S(1)} %add.4), channel_id=1, source_target_pairs={{0,4},{2,6},{4,0},{6,2},{8,12},{10,14},{12,8},{14,10},{1,5},{3,7},... | collective-permute-start | bytes 663560 | tf_op jit(solution)/shard_map/ppermute | solution.py:298
  63.5 1.5 %collective-permute-start.12 = (bf16[72,512]{1,0:T(8,128)(2,1)S(1)}, bf16[72,512]{1,0:T(8,128)(2,1)S(1)}, u32[]{:S(2)}, u32[]{:S(2)}) collective-permute-start(bf16[72,512]{1,0:T(8,128)(2,1)S(1)} %get-tuple-element.83), channel_id=1, source_target_pairs={{0,2},{2,0},{4,6},{6,4},{8,10},{10,8},{12,14},{14,12},{1,3},{3,1},... | collective-permute-start | bytes 221192 | tf_op jit(solution)/shard_map/ppermute | solution.py:295
  66.9 2.9 %collective-permute-start.19 = (bf16[72,1024]{1,0:T(8,128)(2,1)S(1)}, bf16[72,1024]{1,0:T(8,128)(2,1)S(1)}, u32[]{:S(2)}, u32[]{:S(2)}) collective-permute-start(bf16[72,1024]{1,0:T(8,128)(2,1)S(1)} %last.3), channel_id=1, source_target_pairs={{0,12},{2,14},{4,8},{6,10},{8,4},{10,6},{12,0},{14,2},{1,13},{3,15... | collective-permute-start | bytes 442376 | tf_op jit(solution)/shard_map/ppermute | solution.py:298
  70.9 3.5 %grads.1 = (bf16[3072,256]{1,0:T(8,128)(2,1)}, bf16[3072,256]{1,0:T(8,128)(2,1)}, bf16[256,3072]{1,0:T(8,128)(2,1)}) custom-call(bf16[72,3072]{1,0:T(8,128)(2,1)S(1)} %get-tuple-element.90.mine.left.refs_0_, bf16[72,3072]{1,0:T(8,128)(2,1)S(1)} %collective-permute-done.2.other.right.refs_1_, bf16[72,3072]{1,0:T(8,128)(2,1)S(1)} %collective-permute-done.1.mine.refs_2_, ...), custom_call_target="tpu_custom_call" | custom-call | flops 1000 | bytes 1000 | tf_op jit(solution)/shard_map/grads/pallas_call | solution.py:103
  74.5 1.8 %collective-permute-done.20.right = bf16[72,512]{1,0:T(8,128)(2,1)S(1)} collective-permute-done((bf16[72,512]{1,0:T(8,128)(2,1)S(1)}, bf16[72,512]{1,0:T(8,128)(2,1)S(1)}, u32[]{:S(2)}, u32[]{:S(2)}) %collective-permute-start.20) | collective-permute-done | bytes 73760 | tf_op jit(solution)/shard_map/ppermute | solution.py:298
  (38 shorter events, 16.2 us)
Async XLA Ops:
  2.3 13.2 %collective-permute-start.2 = (bf16[72,3072]{1,0:T(8,128)(2,1)S(1)}, bf16[72,3072]{1,0:T(8,128)(2,1)S(1)}, u32[]{:S(2)}, u32[]{:S(2)}) collective-permute-start(bf16[72,3072]{1,0:T(8,128)(2,1)S(1)} %get-tuple-element.90.mine.left.refs_0_), channel_id=1, source_target_pairs={{0,2},{2,0},{4,6},{6,4},{8,10},{10,8},{12,14},{14,12},{1,3},{3,1},... | collective-permute-start | bytes 1327112 | tf_op jit(solution)/shard_map/ppermute | solution.py:295
  5.4 22.6 %collective-permute-start.1 = (bf16[72,3072]{1,0:T(8,128)(2,1)S(1)}, bf16[72,3072]{1,0:T(8,128)(2,1)S(1)}, u32[]{:S(2)}, u32[]{:S(2)}) collective-permute-start(bf16[72,3072]{1,0:T(8,128)(2,1)S(1)} %get-tuple-element.90.mine.left.refs_0_), channel_id=1, source_target_pairs={{0,4},{2,6},{4,0},{6,2},{8,12},{10,14},{12,8},{14,10},{1,5},{3,7},... | collective-permute-start | bytes 1327112 | tf_op jit(solution)/shard_map/ppermute | solution.py:298
  7.0 21.0 %collective-permute-start = (bf16[72,3072]{1,0:T(8,128)(2,1)S(1)}, bf16[72,3072]{1,0:T(8,128)(2,1)S(1)}, u32[]{:S(2)}, u32[]{:S(2)}) collective-permute-start(bf16[72,3072]{1,0:T(8,128)(2,1)S(1)} %get-tuple-element.90.mine.left.refs_0_), channel_id=1, source_target_pairs={{0,8},{2,10},{4,12},{6,14},{8,0},{10,2},{12,4},{14,6},{1,9},{3,11}... | collective-permute-start | bytes 1327112 | tf_op jit(solution)/shard_map/ppermute | solution.py:298
  16.7 1.4 %collective-permute-start.3 = (bf16[80,768]{1,0:T(8,128)(2,1)S(1)}, bf16[80,768]{1,0:T(8,128)(2,1)S(1)}, u32[]{:S(2)}, u32[]{:S(2)}) collective-permute-start(bf16[80,768]{1,0:T(8,128)(2,1)S(1)} %get-tuple-element.66), channel_id=1, source_target_pairs={{0,1},{1,0},{2,3},{3,2},{4,5},{5,4},{6,7},{7,6},{8,9},{9,8},{10,11... | collective-permute-start | bytes 368648 | tf_op jit(solution)/shard_map/ppermute | solution.py:337
  19.2 7.5 %collective-permute-start.4 = (bf16[72,1536]{1,0:T(8,128)(2,1)S(1)}, bf16[72,1536]{1,0:T(8,128)(2,1)S(1)}, u32[]{:S(2)}, u32[]{:S(2)}) collective-permute-start(bf16[72,1536]{1,0:T(8,128)(2,1)S(1)} %get-tuple-element.68), channel_id=1, source_target_pairs={{0,2},{2,0},{4,6},{6,4},{8,10},{10,8},{12,14},{14,12},{1,3},{3,1},... | collective-permute-start | bytes 663560 | tf_op jit(solution)/shard_map/ppermute | solution.py:295
  21.0 16.3 %collective-permute-start.8 = (bf16[72,3072]{1,0:T(8,128)(2,1)S(1)}, bf16[72,3072]{1,0:T(8,128)(2,1)S(1)}, u32[]{:S(2)}, u32[]{:S(2)}) collective-permute-start(bf16[72,3072]{1,0:T(8,128)(2,1)S(1)} %collective-permute-done.2.other.right.refs_1_), channel_id=1, source_target_pairs={{0,4},{2,6},{4,0},{6,2},{8,12},{10,14},{12,8},{14,10},{1,5},{3,7},... | collective-permute-start | bytes 1327112 | tf_op jit(solution)/shard_map/ppermute | solution.py:298
  28.0 13.0 %collective-permute-start.7 = (bf16[72,3072]{1,0:T(8,128)(2,1)S(1)}, bf16[72,3072]{1,0:T(8,128)(2,1)S(1)}, u32[]{:S(2)}, u32[]{:S(2)}) collective-permute-start(bf16[72,3072]{1,0:T(8,128)(2,1)S(1)} %collective-permute-done.mine.refs_4_), channel_id=1, source_target_pairs={{0,2},{2,0},{4,6},{6,4},{8,10},{10,8},{12,14},{14,12},{1,3},{3,1},... | collective-permute-start | bytes 1327112 | tf_op jit(solution)/shard_map/ppermute | solution.py:295
  28.6 26.5 %collective-permute-start.5 = (bf16[72,6144]{1,0:T(8,128)(2,1)S(1)}, bf16[72,6144]{1,0:T(8,128)(2,1)S(1)}, u32[]{:S(2)}, u32[]{:S(2)}) collective-permute-start(bf16[72,6144]{1,0:T(8,128)(2,1)S(1)} %pair.1), channel_id=1, source_target_pairs={{4,8},{6,10},{8,4},{10,6},{5,9},{7,11},{9,5},{11,7},{20,24},{22,26... | collective-permute-start | bytes 2654216 | tf_op jit(solution)/shard_map/ppermute | solution.py:351
  29.3 20.5 %collective-permute-start.6 = (bf16[72,3072]{1,0:T(8,128)(2,1)S(1)}, bf16[72,3072]{1,0:T(8,128)(2,1)S(1)}, u32[]{:S(2)}, u32[]{:S(2)}) collective-permute-start(bf16[72,3072]{1,0:T(8,128)(2,1)S(1)} %collective-permute-done.mine.refs_4_), channel_id=1, source_target_pairs={{8,12},{10,14},{4,0},{6,2},{9,13},{11,15},{5,1},{7,3},{24,28},{26,... | collective-permute-start | bytes 1327112 | tf_op jit(solution)/shard_map/ppermute | solution.py:354
  38.5 1.4 %collective-permute-start.9 = (bf16[80,768]{1,0:T(8,128)(2,1)S(1)}, bf16[80,768]{1,0:T(8,128)(2,1)S(1)}, u32[]{:S(2)}, u32[]{:S(2)}) collective-permute-start(bf16[80,768]{1,0:T(8,128)(2,1)S(1)} %get-tuple-element.75), channel_id=1, source_target_pairs={{0,1},{1,0},{2,3},{3,2},{4,5},{5,4},{6,7},{7,6},{8,9},{9,8},{10,11... | collective-permute-start | bytes 368648 | tf_op jit(solution)/shard_map/ppermute | solution.py:337
  41.0 14.1 %collective-permute-start.10 = (bf16[72,3072]{1,0:T(8,128)(2,1)S(1)}, bf16[72,3072]{1,0:T(8,128)(2,1)S(1)}, u32[]{:S(2)}, u32[]{:S(2)}) collective-permute-start(bf16[72,3072]{1,0:T(8,128)(2,1)S(1)} %collective-permute-done.7.other.refs_5_), channel_id=1, source_target_pairs={{8,12},{10,14},{4,0},{6,2},{9,13},{11,15},{5,1},{7,3},{24,28},{26,... | collective-permute-start | bytes 1327112 | tf_op jit(solution)/shard_map/ppermute | solution.py:354
  42.3 7.5 %collective-permute-start.13 = (bf16[72,1536]{1,0:T(8,128)(2,1)S(1)}, bf16[72,1536]{1,0:T(8,128)(2,1)S(1)}, u32[]{:S(2)}, u32[]{:S(2)}) collective-permute-start(bf16[72,1536]{1,0:T(8,128)(2,1)S(1)} %get-tuple-element.76), channel_id=1, source_target_pairs={{0,2},{2,0},{4,6},{6,4},{8,10},{10,8},{12,14},{14,12},{1,3},{3,1},... | collective-permute-start | bytes 663560 | tf_op jit(solution)/shard_map/ppermute | solution.py:295
  43.6 6.3 %collective-permute-start.14 = (bf16[80,768]{1,0:T(8,128)(2,1)S(1)}, bf16[80,768]{1,0:T(8,128)(2,1)S(1)}, u32[]{:S(2)}, u32[]{:S(2)}) collective-permute-start(bf16[80,768]{1,0:T(8,128)(2,1)S(1)} %get-tuple-element.87), channel_id=1, source_target_pairs={{0,1},{1,0},{2,3},{3,2},{4,5},{5,4},{6,7},{7,6},{8,9},{9,8},{10,11... | collective-permute-start | bytes 368648 | tf_op jit(solution)/shard_map/ppermute | solution.py:337
  51.0 6.7 %collective-permute-start.15 = (bf16[72,1536]{1,0:T(8,128)(2,1)S(1)}, bf16[72,1536]{1,0:T(8,128)(2,1)S(1)}, u32[]{:S(2)}, u32[]{:S(2)}) collective-permute-start(bf16[72,1536]{1,0:T(8,128)(2,1)S(1)} %get-tuple-element.89), channel_id=1, source_target_pairs={{0,2},{2,0},{4,6},{6,4},{8,10},{10,8},{12,14},{14,12},{1,3},{3,1},... | collective-permute-start | bytes 663560 | tf_op jit(solution)/shard_map/ppermute | solution.py:295
  56.3 3.5 %collective-permute-start.11 = (bf16[80,768]{1,0:T(8,128)(2,1)S(1)}, bf16[80,768]{1,0:T(8,128)(2,1)S(1)}, u32[]{:S(2)}, u32[]{:S(2)}) collective-permute-start(bf16[80,768]{1,0:T(8,128)(2,1)S(1)} %get-tuple-element.81), channel_id=1, source_target_pairs={{0,1},{1,0},{2,3},{3,2},{4,5},{5,4},{6,7},{7,6},{8,9},{9,8},{10,11... | collective-permute-start | bytes 368648 | tf_op jit(solution)/shard_map/ppermute | solution.py:337
  57.8 8.1 %collective-permute-start.16 = (bf16[72,1536]{1,0:T(8,128)(2,1)S(1)}, bf16[72,1536]{1,0:T(8,128)(2,1)S(1)}, u32[]{:S(2)}, u32[]{:S(2)}) collective-permute-start(bf16[72,1536]{1,0:T(8,128)(2,1)S(1)} %add.5), channel_id=1, source_target_pairs={{0,4},{2,6},{4,12},{6,14},{8,0},{10,2},{12,8},{14,10},{1,5},{3,7},... | collective-permute-start | bytes 663560 | tf_op jit(solution)/shard_map/ppermute | solution.py:358
  61.0 5.9 %collective-permute-start.18 = (bf16[72,1024]{1,0:T(8,128)(2,1)S(1)}, bf16[72,1024]{1,0:T(8,128)(2,1)S(1)}, u32[]{:S(2)}, u32[]{:S(2)}) collective-permute-start(bf16[72,1024]{1,0:T(8,128)(2,1)S(1)} %get-tuple-element.102), channel_id=1, source_target_pairs={{0,2},{2,0},{4,6},{6,4},{8,10},{10,8},{12,14},{14,12},{1,3},{3,1},... | collective-permute-start | bytes 442376 | tf_op jit(solution)/shard_map/ppermute | solution.py:295
  61.5 13.0 %collective-permute-start.17 = (bf16[72,1536]{1,0:T(8,128)(2,1)S(1)}, bf16[72,1536]{1,0:T(8,128)(2,1)S(1)}, u32[]{:S(2)}, u32[]{:S(2)}) collective-permute-start(bf16[72,1536]{1,0:T(8,128)(2,1)S(1)} %add.4), channel_id=1, source_target_pairs={{0,4},{2,6},{4,0},{6,2},{8,12},{10,14},{12,8},{14,10},{1,5},{3,7},... | collective-permute-start | bytes 663560 | tf_op jit(solution)/shard_map/ppermute | solution.py:298
  63.5 6.3 %collective-permute-start.12 = (bf16[72,512]{1,0:T(8,128)(2,1)S(1)}, bf16[72,512]{1,0:T(8,128)(2,1)S(1)}, u32[]{:S(2)}, u32[]{:S(2)}) collective-permute-start(bf16[72,512]{1,0:T(8,128)(2,1)S(1)} %get-tuple-element.83), channel_id=1, source_target_pairs={{0,2},{2,0},{4,6},{6,4},{8,10},{10,8},{12,14},{14,12},{1,3},{3,1},... | collective-permute-start | bytes 221192 | tf_op jit(solution)/shard_map/ppermute | solution.py:295
  66.9 9.4 %collective-permute-start.19 = (bf16[72,1024]{1,0:T(8,128)(2,1)S(1)}, bf16[72,1024]{1,0:T(8,128)(2,1)S(1)}, u32[]{:S(2)}, u32[]{:S(2)}) collective-permute-start(bf16[72,1024]{1,0:T(8,128)(2,1)S(1)} %last.3), channel_id=1, source_target_pairs={{0,12},{2,14},{4,8},{6,10},{8,4},{10,6},{12,0},{14,2},{1,13},{3,15... | collective-permute-start | bytes 442376 | tf_op jit(solution)/shard_map/ppermute | solution.py:298
  69.8 6.5 %collective-permute-start.20 = (bf16[72,512]{1,0:T(8,128)(2,1)S(1)}, bf16[72,512]{1,0:T(8,128)(2,1)S(1)}, u32[]{:S(2)}, u32[]{:S(2)}) collective-permute-start(bf16[72,512]{1,0:T(8,128)(2,1)S(1)} %last.2), channel_id=1, source_target_pairs={{0,12},{2,14},{4,8},{6,10},{8,4},{10,6},{12,0},{14,2},{1,13},{3,15... | collective-permute-start | bytes 221192 | tf_op jit(solution)/shard_map/ppermute | solution.py:298

commit v9 on v8

--- a/solution.py
+++ b/solution.py
@@ -119,7 +119,12 @@
 def place_kernel(
     tokens_at, grad_out_at, ids_at, probs_at, block, placing_t, tokens, grad_out, ids, probs, done
 ):
-    pairs = ((ids_at, ids), (probs_at, probs), (tokens_at, tokens), (grad_out_at, grad_out))
+    half = tokens.shape[1] // 2
+    parts = (slice(0, half), slice(half, 2 * half))
+    pairs = [(ids_at, ids), (probs_at, probs)]
+    for columns in parts:
+        pairs += [(tokens_at.at[:, columns], tokens.at[:, columns])]
+        pairs += [(grad_out_at.at[:, columns], grad_out.at[:, columns])]
     copies = [pltpu.make_async_copy(a, b, done.at[i]) for i, (a, b) in enumerate(pairs)]
     for copy in copies:
         copy.start()
@@ -141,13 +146,14 @@
     placing_t[...] = jnp.where((slot == wanted) & (routed > 0.0), 1.0, 0.0).astype(BF16)
     scale = jnp.sum(placing * weight_row, axis=1, keepdims=True)
     placing = placing.astype(BF16)
-    copies[2].wait()
-    x = mul(placing, tokens[...])
-    copies[3].wait()
-    dy = mul(placing, grad_out[...]) * scale
-    last = jnp.concatenate([x[MAIN:CAP], dy[MAIN:CAP]], axis=0)
-    for at, value in ((0, x[0:MAIN]), (MAIN, dy[0:MAIN]), (2 * MAIN, last)):
-        block[at : at + value.shape[0], :] = value.astype(BF16)
+    for step, columns in enumerate(parts):
+        copies[2 * step + 2].wait()
+        x = mul(placing, tokens[:, columns])
+        copies[2 * step + 3].wait()
+        dy = mul(placing, grad_out[:, columns]) * scale
+        last = jnp.concatenate([x[MAIN:CAP], dy[MAIN:CAP]], axis=0)
+        for at, value in ((0, x[0:MAIN]), (MAIN, dy[0:MAIN]), (2 * MAIN, last)):
+            block[at : at + value.shape[0], columns] = value.astype(BF16)
 
 
 def tails(blocks, turned, columns):
@@ -316,7 +322,7 @@
             pltpu.VMEM(tokens.shape, BF16),
             pltpu.VMEM(expert_ids.shape[::-1], jnp.int32),
             pltpu.VMEM(gate_probs.shape[::-1], F32),
-            pltpu.SemaphoreType.DMA((4,)),
+            pltpu.SemaphoreType.DMA((6,)),
         ],
     )
     w_gate, w_up, w_down, _ = lax.optimization_barrier((w_gate, w_up, w_down, own))

time: 77.6 us -> 77.8 us (level)
  no operation moved by 1% of the time
where the time goes in v9:
time: 77.8 us; the launch traced here: 77.6 us
  waiting for transfers between devices  33 us (42%)
  starting transfers between devices  25.5 us (33%)
  Pallas kernels  18.3 us (24%)
  between operations  0.8 us (1%)
    pallas_call x20, Pallas kernels, call(): pl.pallas_call(kernel, out_shape=outs, name=name, compiler_params=pltpu.C...  18.3 us
    ppermute x7, waiting for transfers between devices, across(): return lax.ppermute(value, 'expert', [(i, i ^ 1) for i in range(8)])  16.1 us
    ppermute x6, starting transfers between devices, along(): lax.ppermute(value, 'expert', [(i, i ^ 2 * distance) for i in range(8)])  11.8 us
    ppermute x6, waiting for transfers between devices, along(): lax.ppermute(value, 'expert', [(i, i ^ 2 * distance) for i in range(8)])  9.65 us
    ppermute x7, starting transfers between devices, across(): return lax.ppermute(value, 'expert', [(i, i ^ 1) for i in range(8)])  8.09 us
    ppermute x2, waiting for transfers between devices, ends(): return lax.ppermute(value, 'expert', [(4, 6), (5, 7), (2, 0), (3, 1)])  3.75 us
    ppermute x4, waiting for transfers between devices, front(): return (part, lax.ppermute(sent, 'tensor', [(0, 1), (1, 0)]))  2.65 us
    ppermute x2, starting transfers between devices, ends(): return lax.ppermute(value, 'expert', [(4, 6), (5, 7), (2, 0), (3, 1)])  2.58 us
  transfers between devices with their start and end apart: 21, of which 12 were waited for; matrix products, arithmetic and copies ran while one was open for 0% of the time, Pallas kernels for 20%

profile of v9, /device:TPU:0, one launch (start us, length us, event | category | flops | bytes accessed | tf_op | source)
XLA Modules:
  0.0 77.6 jit_solution(6217682897614093236)
XLA Ops:
  0.6 1.9 %place.1 = (bf16[72,3072]{1,0:T(8,128)(2,1)S(1)}, bf16[128,128]{1,0:T(8,128)(2,1)S(1)}) custom-call(bf16[128,3072]{1,0:T(8,128)(2,1)} %tokens_at.1, bf16[128,3072]{1,0:T(8,128)(2,1)} %grad_out_at.1, s32[2,128]{1,0:T(2,128)} %bitcast.2, f32[2,128]{1,0:T(2,128)} %bitcast.3), custom_call_target="tpu_custom_call" | custom-call | flops 1000 | bytes 1000 | tf_op jit(solution)/shard_map/place/pallas_call | solution.py:103
  2.5 3.0 %collective-permute-start.2 = (bf16[72,3072]{1,0:T(8,128)(2,1)S(1)}, bf16[72,3072]{1,0:T(8,128)(2,1)S(1)}, u32[]{:S(2)}, u32[]{:S(2)}) collective-permute-start(bf16[72,3072]{1,0:T(8,128)(2,1)S(1)} %get-tuple-element.90.mine.left.refs_0_), channel_id=1, source_target_pairs={{0,2},{2,0},{4,6},{6,4},{8,10},{10,8},{12,14},{14,12},{1,3},{3,1},... | collective-permute-start | bytes 1327112 | tf_op jit(solution)/shard_map/ppermute | solution.py:301
  5.5 1.6 %collective-permute-start.1 = (bf16[72,3072]{1,0:T(8,128)(2,1)S(1)}, bf16[72,3072]{1,0:T(8,128)(2,1)S(1)}, u32[]{:S(2)}, u32[]{:S(2)}) collective-permute-start(bf16[72,3072]{1,0:T(8,128)(2,1)S(1)} %get-tuple-element.90.mine.left.refs_0_), channel_id=1, source_target_pairs={{0,4},{2,6},{4,0},{6,2},{8,12},{10,14},{12,8},{14,10},{1,5},{3,7},... | collective-permute-start | bytes 1327112 | tf_op jit(solution)/shard_map/ppermute | solution.py:304
  7.1 2.6 %collective-permute-start = (bf16[72,3072]{1,0:T(8,128)(2,1)S(1)}, bf16[72,3072]{1,0:T(8,128)(2,1)S(1)}, u32[]{:S(2)}, u32[]{:S(2)}) collective-permute-start(bf16[72,3072]{1,0:T(8,128)(2,1)S(1)} %get-tuple-element.90.mine.left.refs_0_), channel_id=1, source_target_pairs={{0,8},{2,10},{4,12},{6,14},{8,0},{10,2},{12,4},{14,6},{1,9},{3,11}... | collective-permute-start | bytes 1327112 | tf_op jit(solution)/shard_map/ppermute | solution.py:304
  9.7 2.4 %load.1 = (bf16[3072,256]{1,0:T(8,128)(2,1)S(1)}, bf16[3072,256]{1,0:T(8,128)(2,1)S(1)}, bf16[256,3072]{1,0:T(8,128)(2,1)S(1)}) custom-call(bf16[3072,256]{1,0:T(8,128)(2,1)} %refs_0_, bf16[3072,256]{1,0:T(8,128)(2,1)} %refs_1_, bf16[256,3072]{1,0:T(8,128)(2,1)} %refs_2_), custom_call_target="tpu_custom_call" | custom-call | flops 1000 | bytes 1000 | tf_op jit(solution)/shard_map/load/pallas_call | solution.py:103
  12.1 3.6 %collective-permute-done.2.other.right.refs_1_ = bf16[72,3072]{1,0:T(8,128)(2,1)S(1)} collective-permute-done((bf16[72,3072]{1,0:T(8,128)(2,1)S(1)}, bf16[72,3072]{1,0:T(8,128)(2,1)S(1)}, u32[]{:S(2)}, u32[]{:S(2)}) %collective-permute-start.2) | collective-permute-done | bytes 442400 | tf_op jit(solution)/shard_map/ppermute | solution.py:301
  16.9 1.3 %collective-permute-done.3.arrived = bf16[80,768]{1,0:T(8,128)(2,1)S(1)} collective-permute-done((bf16[80,768]{1,0:T(8,128)(2,1)S(1)}, bf16[80,768]{1,0:T(8,128)(2,1)S(1)}, u32[]{:S(2)}, u32[]{:S(2)}) %collective-permute-start.3) | collective-permute-done | bytes 122912 | tf_op jit(solution)/shard_map/ppermute | solution.py:343
  19.3 1.8 %collective-permute-start.4 = (bf16[72,1536]{1,0:T(8,128)(2,1)S(1)}, bf16[72,1536]{1,0:T(8,128)(2,1)S(1)}, u32[]{:S(2)}, u32[]{:S(2)}) collective-permute-start(bf16[72,1536]{1,0:T(8,128)(2,1)S(1)} %get-tuple-element.68), channel_id=1, source_target_pairs={{0,2},{2,0},{4,6},{6,4},{8,10},{10,8},{12,14},{14,12},{1,3},{3,1},... | collective-permute-start | bytes 663560 | tf_op jit(solution)/shard_map/ppermute | solution.py:301
  21.1 1.6 %collective-permute-start.8 = (bf16[72,3072]{1,0:T(8,128)(2,1)S(1)}, bf16[72,3072]{1,0:T(8,128)(2,1)S(1)}, u32[]{:S(2)}, u32[]{:S(2)}) collective-permute-start(bf16[72,3072]{1,0:T(8,128)(2,1)S(1)} %collective-permute-done.2.other.right.refs_1_), channel_id=1, source_target_pairs={{0,4},{2,6},{4,0},{6,2},{8,12},{10,14},{12,8},{14,10},{1,5},{3,7},... | collective-permute-start | bytes 1327112 | tf_op jit(solution)/shard_map/ppermute | solution.py:304
  22.8 4.1 %collective-permute-done.4.arrived = bf16[72,1536]{1,0:T(8,128)(2,1)S(1)} collective-permute-done((bf16[72,1536]{1,0:T(8,128)(2,1)S(1)}, bf16[72,1536]{1,0:T(8,128)(2,1)S(1)}, u32[]{:S(2)}, u32[]{:S(2)}) %collective-permute-start.4) | collective-permute-done | bytes 221216 | tf_op jit(solution)/shard_map/ppermute | solution.py:301
  26.9 1.2 %collective-permute-done.1.mine.refs_2_ = bf16[72,3072]{1,0:T(8,128)(2,1)S(1)} collective-permute-done((bf16[72,3072]{1,0:T(8,128)(2,1)S(1)}, bf16[72,3072]{1,0:T(8,128)(2,1)S(1)}, u32[]{:S(2)}, u32[]{:S(2)}) %collective-permute-start.1) | collective-permute-done | bytes 442400 | tf_op jit(solution)/shard_map/ppermute | solution.py:304
  29.5 1.3 %collective-permute-start.6 = (bf16[72,3072]{1,0:T(8,128)(2,1)S(1)}, bf16[72,3072]{1,0:T(8,128)(2,1)S(1)}, u32[]{:S(2)}, u32[]{:S(2)}) collective-permute-start(bf16[72,3072]{1,0:T(8,128)(2,1)S(1)} %collective-permute-done.mine.refs_4_), channel_id=1, source_target_pairs={{8,12},{10,14},{4,0},{6,2},{9,13},{11,15},{5,1},{7,3},{24,28},{26,... | collective-permute-start | bytes 1327112 | tf_op jit(solution)/shard_map/ppermute | solution.py:360
  30.8 6.7 %collective-permute-done.8.other.refs_3_ = bf16[72,3072]{1,0:T(8,128)(2,1)S(1)} collective-permute-done((bf16[72,3072]{1,0:T(8,128)(2,1)S(1)}, bf16[72,3072]{1,0:T(8,128)(2,1)S(1)}, u32[]{:S(2)}, u32[]{:S(2)}) %collective-permute-start.8) | collective-permute-done | bytes 442400 | tf_op jit(solution)/shard_map/ppermute | solution.py:304
  38.7 1.3 %collective-permute-done.9.arrived = bf16[80,768]{1,0:T(8,128)(2,1)S(1)} collective-permute-done((bf16[80,768]{1,0:T(8,128)(2,1)S(1)}, bf16[80,768]{1,0:T(8,128)(2,1)S(1)}, u32[]{:S(2)}, u32[]{:S(2)}) %collective-permute-start.9) | collective-permute-done | bytes 122912 | tf_op jit(solution)/shard_map/ppermute | solution.py:343
  41.1 1.3 %collective-permute-start.10 = (bf16[72,3072]{1,0:T(8,128)(2,1)S(1)}, bf16[72,3072]{1,0:T(8,128)(2,1)S(1)}, u32[]{:S(2)}, u32[]{:S(2)}) collective-permute-start(bf16[72,3072]{1,0:T(8,128)(2,1)S(1)} %collective-permute-done.7.other.refs_5_), channel_id=1, source_target_pairs={{8,12},{10,14},{4,0},{6,2},{9,13},{11,15},{5,1},{7,3},{24,28},{26,... | collective-permute-start | bytes 1327112 | tf_op jit(solution)/shard_map/ppermute | solution.py:360
  43.9 6.1 %collective-permute-done.13.arrived = bf16[72,1536]{1,0:T(8,128)(2,1)S(1)} collective-permute-done((bf16[72,1536]{1,0:T(8,128)(2,1)S(1)}, bf16[72,1536]{1,0:T(8,128)(2,1)S(1)}, u32[]{:S(2)}, u32[]{:S(2)}) %collective-permute-start.13) | collective-permute-done | bytes 221216 | tf_op jit(solution)/shard_map/ppermute | solution.py:301
  51.5 3.8 %collective-permute-done.10.outer_y = bf16[72,3072]{1,0:T(8,128)(2,1)S(1)} collective-permute-done((bf16[72,3072]{1,0:T(8,128)(2,1)S(1)}, bf16[72,3072]{1,0:T(8,128)(2,1)S(1)}, u32[]{:S(2)}, u32[]{:S(2)}) %collective-permute-start.10) | collective-permute-done | bytes 442400 | tf_op jit(solution)/shard_map/ppermute | solution.py:360
  56.6 1.3 %collective-permute-done.15.arrived = bf16[72,1536]{1,0:T(8,128)(2,1)S(1)} collective-permute-done((bf16[72,1536]{1,0:T(8,128)(2,1)S(1)}, bf16[72,1536]{1,0:T(8,128)(2,1)S(1)}, u32[]{:S(2)}, u32[]{:S(2)}) %collective-permute-start.15) | collective-permute-done | bytes 221216 | tf_op jit(solution)/shard_map/ppermute | solution.py:301
  57.9 2.1 %collective-permute-start.16 = (bf16[72,1536]{1,0:T(8,128)(2,1)S(1)}, bf16[72,1536]{1,0:T(8,128)(2,1)S(1)}, u32[]{:S(2)}, u32[]{:S(2)}) collective-permute-start(bf16[72,1536]{1,0:T(8,128)(2,1)S(1)} %add.5), channel_id=1, source_target_pairs={{0,4},{2,6},{4,12},{6,14},{8,0},{10,2},{12,8},{14,10},{1,5},{3,7},... | collective-permute-start | bytes 663560 | tf_op jit(solution)/shard_map/ppermute | solution.py:364
  61.6 2.1 %collective-permute-start.17 = (bf16[72,1536]{1,0:T(8,128)(2,1)S(1)}, bf16[72,1536]{1,0:T(8,128)(2,1)S(1)}, u32[]{:S(2)}, u32[]{:S(2)}) collective-permute-start(bf16[72,1536]{1,0:T(8,128)(2,1)S(1)} %add.4), channel_id=1, source_target_pairs={{0,4},{2,6},{4,0},{6,2},{8,12},{10,14},{12,8},{14,10},{1,5},{3,7},... | collective-permute-start | bytes 663560 | tf_op jit(solution)/shard_map/ppermute | solution.py:304
  63.6 1.5 %collective-permute-start.12 = (bf16[72,512]{1,0:T(8,128)(2,1)S(1)}, bf16[72,512]{1,0:T(8,128)(2,1)S(1)}, u32[]{:S(2)}, u32[]{:S(2)}) collective-permute-start(bf16[72,512]{1,0:T(8,128)(2,1)S(1)} %get-tuple-element.83), channel_id=1, source_target_pairs={{0,2},{2,0},{4,6},{6,4},{8,10},{10,8},{12,14},{14,12},{1,3},{3,1},... | collective-permute-start | bytes 221192 | tf_op jit(solution)/shard_map/ppermute | solution.py:301
  67.1 2.9 %collective-permute-start.19 = (bf16[72,1024]{1,0:T(8,128)(2,1)S(1)}, bf16[72,1024]{1,0:T(8,128)(2,1)S(1)}, u32[]{:S(2)}, u32[]{:S(2)}) collective-permute-start(bf16[72,1024]{1,0:T(8,128)(2,1)S(1)} %last.3), channel_id=1, source_target_pairs={{0,12},{2,14},{4,8},{6,10},{8,4},{10,6},{12,0},{14,2},{1,13},{3,15... | collective-permute-start | bytes 442376 | tf_op jit(solution)/shard_map/ppermute | solution.py:304
  71.0 3.5 %grads.1 = (bf16[3072,256]{1,0:T(8,128)(2,1)}, bf16[3072,256]{1,0:T(8,128)(2,1)}, bf16[256,3072]{1,0:T(8,128)(2,1)}) custom-call(bf16[72,3072]{1,0:T(8,128)(2,1)S(1)} %get-tuple-element.90.mine.left.refs_0_, bf16[72,3072]{1,0:T(8,128)(2,1)S(1)} %collective-permute-done.2.other.right.refs_1_, bf16[72,3072]{1,0:T(8,128)(2,1)S(1)} %collective-permute-done.1.mine.refs_2_, ...), custom_call_target="tpu_custom_call" | custom-call | flops 1000 | bytes 1000 | tf_op jit(solution)/shard_map/grads/pallas_call | solution.py:103
  74.7 1.8 %collective-permute-done.20.right = bf16[72,512]{1,0:T(8,128)(2,1)S(1)} collective-permute-done((bf16[72,512]{1,0:T(8,128)(2,1)S(1)}, bf16[72,512]{1,0:T(8,128)(2,1)S(1)}, u32[]{:S(2)}, u32[]{:S(2)}) %collective-permute-start.20) | collective-permute-done | bytes 73760 | tf_op jit(solution)/shard_map/ppermute | solution.py:304
  (38 shorter events, 16.2 us)
Async XLA Ops:
  2.5 13.2 %collective-permute-start.2 = (bf16[72,3072]{1,0:T(8,128)(2,1)S(1)}, bf16[72,3072]{1,0:T(8,128)(2,1)S(1)}, u32[]{:S(2)}, u32[]{:S(2)}) collective-permute-start(bf16[72,3072]{1,0:T(8,128)(2,1)S(1)} %get-tuple-element.90.mine.left.refs_0_), channel_id=1, source_target_pairs={{0,2},{2,0},{4,6},{6,4},{8,10},{10,8},{12,14},{14,12},{1,3},{3,1},... | collective-permute-start | bytes 1327112 | tf_op jit(solution)/shard_map/ppermute | solution.py:301
  5.5 22.6 %collective-permute-start.1 = (bf16[72,3072]{1,0:T(8,128)(2,1)S(1)}, bf16[72,3072]{1,0:T(8,128)(2,1)S(1)}, u32[]{:S(2)}, u32[]{:S(2)}) collective-permute-start(bf16[72,3072]{1,0:T(8,128)(2,1)S(1)} %get-tuple-element.90.mine.left.refs_0_), channel_id=1, source_target_pairs={{0,4},{2,6},{4,0},{6,2},{8,12},{10,14},{12,8},{14,10},{1,5},{3,7},... | collective-permute-start | bytes 1327112 | tf_op jit(solution)/shard_map/ppermute | solution.py:304
  7.1 21.0 %collective-permute-start = (bf16[72,3072]{1,0:T(8,128)(2,1)S(1)}, bf16[72,3072]{1,0:T(8,128)(2,1)S(1)}, u32[]{:S(2)}, u32[]{:S(2)}) collective-permute-start(bf16[72,3072]{1,0:T(8,128)(2,1)S(1)} %get-tuple-element.90.mine.left.refs_0_), channel_id=1, source_target_pairs={{0,8},{2,10},{4,12},{6,14},{8,0},{10,2},{12,4},{14,6},{1,9},{3,11}... | collective-permute-start | bytes 1327112 | tf_op jit(solution)/shard_map/ppermute | solution.py:304
  16.8 1.4 %collective-permute-start.3 = (bf16[80,768]{1,0:T(8,128)(2,1)S(1)}, bf16[80,768]{1,0:T(8,128)(2,1)S(1)}, u32[]{:S(2)}, u32[]{:S(2)}) collective-permute-start(bf16[80,768]{1,0:T(8,128)(2,1)S(1)} %get-tuple-element.66), channel_id=1, source_target_pairs={{0,1},{1,0},{2,3},{3,2},{4,5},{5,4},{6,7},{7,6},{8,9},{9,8},{10,11... | collective-permute-start | bytes 368648 | tf_op jit(solution)/shard_map/ppermute | solution.py:343
  19.3 7.6 %collective-permute-start.4 = (bf16[72,1536]{1,0:T(8,128)(2,1)S(1)}, bf16[72,1536]{1,0:T(8,128)(2,1)S(1)}, u32[]{:S(2)}, u32[]{:S(2)}) collective-permute-start(bf16[72,1536]{1,0:T(8,128)(2,1)S(1)} %get-tuple-element.68), channel_id=1, source_target_pairs={{0,2},{2,0},{4,6},{6,4},{8,10},{10,8},{12,14},{14,12},{1,3},{3,1},... | collective-permute-start | bytes 663560 | tf_op jit(solution)/shard_map/ppermute | solution.py:301
  21.1 16.3 %collective-permute-start.8 = (bf16[72,3072]{1,0:T(8,128)(2,1)S(1)}, bf16[72,3072]{1,0:T(8,128)(2,1)S(1)}, u32[]{:S(2)}, u32[]{:S(2)}) collective-permute-start(bf16[72,3072]{1,0:T(8,128)(2,1)S(1)} %collective-permute-done.2.other.right.refs_1_), channel_id=1, source_target_pairs={{0,4},{2,6},{4,0},{6,2},{8,12},{10,14},{12,8},{14,10},{1,5},{3,7},... | collective-permute-start | bytes 1327112 | tf_op jit(solution)/shard_map/ppermute | solution.py:304
  28.1 13.0 %collective-permute-start.7 = (bf16[72,3072]{1,0:T(8,128)(2,1)S(1)}, bf16[72,3072]{1,0:T(8,128)(2,1)S(1)}, u32[]{:S(2)}, u32[]{:S(2)}) collective-permute-start(bf16[72,3072]{1,0:T(8,128)(2,1)S(1)} %collective-permute-done.mine.refs_4_), channel_id=1, source_target_pairs={{0,2},{2,0},{4,6},{6,4},{8,10},{10,8},{12,14},{14,12},{1,3},{3,1},... | collective-permute-start | bytes 1327112 | tf_op jit(solution)/shard_map/ppermute | solution.py:301
  28.8 26.5 %collective-permute-start.5 = (bf16[72,6144]{1,0:T(8,128)(2,1)S(1)}, bf16[72,6144]{1,0:T(8,128)(2,1)S(1)}, u32[]{:S(2)}, u32[]{:S(2)}) collective-permute-start(bf16[72,6144]{1,0:T(8,128)(2,1)S(1)} %pair.1), channel_id=1, source_target_pairs={{4,8},{6,10},{8,4},{10,6},{5,9},{7,11},{9,5},{11,7},{20,24},{22,26... | collective-permute-start | bytes 2654216 | tf_op jit(solution)/shard_map/ppermute | solution.py:357
  29.5 20.5 %collective-permute-start.6 = (bf16[72,3072]{1,0:T(8,128)(2,1)S(1)}, bf16[72,3072]{1,0:T(8,128)(2,1)S(1)}, u32[]{:S(2)}, u32[]{:S(2)}) collective-permute-start(bf16[72,3072]{1,0:T(8,128)(2,1)S(1)} %collective-permute-done.mine.refs_4_), channel_id=1, source_target_pairs={{8,12},{10,14},{4,0},{6,2},{9,13},{11,15},{5,1},{7,3},{24,28},{26,... | collective-permute-start | bytes 1327112 | tf_op jit(solution)/shard_map/ppermute | solution.py:360
  38.6 1.4 %collective-permute-start.9 = (bf16[80,768]{1,0:T(8,128)(2,1)S(1)}, bf16[80,768]{1,0:T(8,128)(2,1)S(1)}, u32[]{:S(2)}, u32[]{:S(2)}) collective-permute-start(bf16[80,768]{1,0:T(8,128)(2,1)S(1)} %get-tuple-element.75), channel_id=1, source_target_pairs={{0,1},{1,0},{2,3},{3,2},{4,5},{5,4},{6,7},{7,6},{8,9},{9,8},{10,11... | collective-permute-start | bytes 368648 | tf_op jit(solution)/shard_map/ppermute | solution.py:343
  41.1 14.1 %collective-permute-start.10 = (bf16[72,3072]{1,0:T(8,128)(2,1)S(1)}, bf16[72,3072]{1,0:T(8,128)(2,1)S(1)}, u32[]{:S(2)}, u32[]{:S(2)}) collective-permute-start(bf16[72,3072]{1,0:T(8,128)(2,1)S(1)} %collective-permute-done.7.other.refs_5_), channel_id=1, source_target_pairs={{8,12},{10,14},{4,0},{6,2},{9,13},{11,15},{5,1},{7,3},{24,28},{26,... | collective-permute-start | bytes 1327112 | tf_op jit(solution)/shard_map/ppermute | solution.py:360
  42.4 7.5 %collective-permute-start.13 = (bf16[72,1536]{1,0:T(8,128)(2,1)S(1)}, bf16[72,1536]{1,0:T(8,128)(2,1)S(1)}, u32[]{:S(2)}, u32[]{:S(2)}) collective-permute-start(bf16[72,1536]{1,0:T(8,128)(2,1)S(1)} %get-tuple-element.76), channel_id=1, source_target_pairs={{0,2},{2,0},{4,6},{6,4},{8,10},{10,8},{12,14},{14,12},{1,3},{3,1},... | collective-permute-start | bytes 663560 | tf_op jit(solution)/shard_map/ppermute | solution.py:301
  43.8 6.2 %collective-permute-start.14 = (bf16[80,768]{1,0:T(8,128)(2,1)S(1)}, bf16[80,768]{1,0:T(8,128)(2,1)S(1)}, u32[]{:S(2)}, u32[]{:S(2)}) collective-permute-start(bf16[80,768]{1,0:T(8,128)(2,1)S(1)} %get-tuple-element.87), channel_id=1, source_target_pairs={{0,1},{1,0},{2,3},{3,2},{4,5},{5,4},{6,7},{7,6},{8,9},{9,8},{10,11... | collective-permute-start | bytes 368648 | tf_op jit(solution)/shard_map/ppermute | solution.py:343
  51.1 6.7 %collective-permute-start.15 = (bf16[72,1536]{1,0:T(8,128)(2,1)S(1)}, bf16[72,1536]{1,0:T(8,128)(2,1)S(1)}, u32[]{:S(2)}, u32[]{:S(2)}) collective-permute-start(bf16[72,1536]{1,0:T(8,128)(2,1)S(1)} %get-tuple-element.89), channel_id=1, source_target_pairs={{0,2},{2,0},{4,6},{6,4},{8,10},{10,8},{12,14},{14,12},{1,3},{3,1},... | collective-permute-start | bytes 663560 | tf_op jit(solution)/shard_map/ppermute | solution.py:301
  56.5 3.5 %collective-permute-start.11 = (bf16[80,768]{1,0:T(8,128)(2,1)S(1)}, bf16[80,768]{1,0:T(8,128)(2,1)S(1)}, u32[]{:S(2)}, u32[]{:S(2)}) collective-permute-start(bf16[80,768]{1,0:T(8,128)(2,1)S(1)} %get-tuple-element.81), channel_id=1, source_target_pairs={{0,1},{1,0},{2,3},{3,2},{4,5},{5,4},{6,7},{7,6},{8,9},{9,8},{10,11... | collective-permute-start | bytes 368648 | tf_op jit(solution)/shard_map/ppermute | solution.py:343
  57.9 8.1 %collective-permute-start.16 = (bf16[72,1536]{1,0:T(8,128)(2,1)S(1)}, bf16[72,1536]{1,0:T(8,128)(2,1)S(1)}, u32[]{:S(2)}, u32[]{:S(2)}) collective-permute-start(bf16[72,1536]{1,0:T(8,128)(2,1)S(1)} %add.5), channel_id=1, source_target_pairs={{0,4},{2,6},{4,12},{6,14},{8,0},{10,2},{12,8},{14,10},{1,5},{3,7},... | collective-permute-start | bytes 663560 | tf_op jit(solution)/shard_map/ppermute | solution.py:364
  61.1 5.9 %collective-permute-start.18 = (bf16[72,1024]{1,0:T(8,128)(2,1)S(1)}, bf16[72,1024]{1,0:T(8,128)(2,1)S(1)}, u32[]{:S(2)}, u32[]{:S(2)}) collective-permute-start(bf16[72,1024]{1,0:T(8,128)(2,1)S(1)} %get-tuple-element.102), channel_id=1, source_target_pairs={{0,2},{2,0},{4,6},{6,4},{8,10},{10,8},{12,14},{14,12},{1,3},{3,1},... | collective-permute-start | bytes 442376 | tf_op jit(solution)/shard_map/ppermute | solution.py:301
  61.6 13.0 %collective-permute-start.17 = (bf16[72,1536]{1,0:T(8,128)(2,1)S(1)}, bf16[72,1536]{1,0:T(8,128)(2,1)S(1)}, u32[]{:S(2)}, u32[]{:S(2)}) collective-permute-start(bf16[72,1536]{1,0:T(8,128)(2,1)S(1)} %add.4), channel_id=1, source_target_pairs={{0,4},{2,6},{4,0},{6,2},{8,12},{10,14},{12,8},{14,10},{1,5},{3,7},... | collective-permute-start | bytes 663560 | tf_op jit(solution)/shard_map/ppermute | solution.py:304
  63.6 6.3 %collective-permute-start.12 = (bf16[72,512]{1,0:T(8,128)(2,1)S(1)}, bf16[72,512]{1,0:T(8,128)(2,1)S(1)}, u32[]{:S(2)}, u32[]{:S(2)}) collective-permute-start(bf16[72,512]{1,0:T(8,128)(2,1)S(1)} %get-tuple-element.83), channel_id=1, source_target_pairs={{0,2},{2,0},{4,6},{6,4},{8,10},{10,8},{12,14},{14,12},{1,3},{3,1},... | collective-permute-start | bytes 221192 | tf_op jit(solution)/shard_map/ppermute | solution.py:301
  67.1 9.4 %collective-permute-start.19 = (bf16[72,1024]{1,0:T(8,128)(2,1)S(1)}, bf16[72,1024]{1,0:T(8,128)(2,1)S(1)}, u32[]{:S(2)}, u32[]{:S(2)}) collective-permute-start(bf16[72,1024]{1,0:T(8,128)(2,1)S(1)} %last.3), channel_id=1, source_target_pairs={{0,12},{2,14},{4,8},{6,10},{8,4},{10,6},{12,0},{14,2},{1,13},{3,15... | collective-permute-start | bytes 442376 | tf_op jit(solution)/shard_map/ppermute | solution.py:304
  70.0 6.5 %collective-permute-start.20 = (bf16[72,512]{1,0:T(8,128)(2,1)S(1)}, bf16[72,512]{1,0:T(8,128)(2,1)S(1)}, u32[]{:S(2)}, u32[]{:S(2)}) collective-permute-start(bf16[72,512]{1,0:T(8,128)(2,1)S(1)} %last.2), channel_id=1, source_target_pairs={{0,12},{2,14},{4,8},{6,10},{8,4},{10,6},{12,0},{14,2},{1,13},{3,15... | collective-permute-start | bytes 221192 | tf_op jit(solution)/shard_map/ppermute | solution.py:304
